TPU v7x, 32 devices: a whole 2x2x4 slice. The times are simulated.
32 devices in a mesh: grp: 4 (over y, core), sub: 8 (over z, x).
Axes of the slice: x: 2, y: 2, z: 4, core: 2. Of those that a mesh axis runs over, the one named last changes fastest.
Arguments:
- activations: bfloat16 [16384, 2048], P(('grp', 'sub')), may hold values from -110 to 110
- norm_gain: float32 [2048], replicated, may hold values from 0.5 to 1.5
- key_weight: bfloat16 [2048, 768], P('sub'), may hold values from -0.125 to 0.125
- key_grads: bfloat16 [16384, 768], P(('grp', 'sub')), may hold values from -3 to 3
Outputs:
- input_grads: bfloat16 [16384, 2048], P(('grp', 'sub'))
- weight_grads: float32 [2048, 768], P('sub', 'grp')
- gain_grads: float32 [2048], P('sub')
All inputs are finite; a program needn't handle non-finite values.
Results may differ from a plain program's by a relative error of at most 0.0029.
Values may be sent and summed in bfloat16 or wider, within the bound.
No kernel may reach another device: no remote copies, remote signals or barrier semaphores. Data moves between devices by JAX's collectives and lax.ppermute only.
A program may use at most 64 MiB of HBM per device.

v0:
```python
import jax
import jax.numpy as jnp
from jax import lax
from jax.sharding import PartitionSpec as P


def local(activations, norm_gain, key_weight, key_grads):
    inputs = activations.astype(jnp.float32)
    mean_square = jnp.mean(inputs * inputs, axis=1, keepdims=True)
    inverse_rms = lax.rsqrt(mean_square + 1e-05)
    normed = inputs * inverse_rms
    scaled = (normed * norm_gain).astype(jnp.bfloat16)
    grad_scaled = lax.dot_general(
        key_grads,
        lax.all_gather(key_weight, "sub", axis=0, tiled=True),
        (((1,), (1,)), ((), ())),
        preferred_element_type=jnp.float32,
    )
    gained = norm_gain * grad_scaled
    input_grads = (
        inverse_rms * (gained - normed * jnp.mean(gained * normed, axis=1, keepdims=True))
    ).astype(jnp.bfloat16)
    groups = lax.axis_size("grp")
    feature_rows = key_weight.shape[0]
    key_width = key_grads.shape[1]
    key_rows = key_width // groups
    model_width = scaled.shape[1]
    term = lax.dot_general(
        key_grads, scaled, (((0,), (0,)), ((), ())), preferred_element_type=jnp.float32
    )
    received = lax.all_to_all(term, "grp", split_axis=0, concat_axis=1, tiled=True)
    shared = jnp.sum(received.reshape(key_rows, groups, model_width), axis=1)
    owned = lax.psum_scatter(shared, "sub", scatter_dimension=1, tiled=True).T
    weight_grads = owned / groups
    local_gain = jnp.sum(grad_scaled * normed, axis=0)
    summed = lax.psum(local_gain, ("grp", "sub"))
    gain_sum = lax.dynamic_slice_in_dim(summed, lax.axis_index("sub") * feature_rows, feature_rows)
    gain_grads = gain_sum / groups
    return (input_grads, weight_grads, gain_grads)


def solution(mesh):
    return jax.shard_map(
        local,
        mesh=mesh,
        in_specs=(P(("grp", "sub"), None), P(), P("sub", None), P(("grp", "sub"), None)),
        out_specs=(P(("grp", "sub"), None), P("sub", "grp"), P("sub")),
        check_vma=False,
    )
```

profile of v0, /device:TPU:0, one launch (start us, length us, event | category | flops | bytes accessed | tf_op | source)
XLA Modules:
  0.0 168.9 jit_solution(18210436257152759157)
XLA Ops:
  7.2 0.0 copy-start
  7.2 0.0 all-gather.2.cloned.1.call-start
  7.2 0.7 all-gather.2.cloned.1.call-update
  7.9 0.0 reduce-scatter.2.cloned.1.call-start
  8.0 2.1 %fusion.10 = f32[512]{0:T(512)S(1)} fusion(bf16[512,2048]{1,0:T(8,128)(2,1)} %param.4), kind=kLoop, calls=%fused_computation.12 | loop fusion | flops 3145216 | bytes 2099200 | tf_op jit(solution)/shard_map/reduce_sum | solution.py:9
  10.0 0.0 copy-done
  10.1 3.6 %fusion.11 = f32[2048,768]{0,1:T(8,128)S(1)} fusion(bf16[512,768]{1,0:T(8,128)(2,1)S(1)} %copy-done, bf16[512,2048]{1,0:T(8,128)(2,1)} %param.4, f32[2048]{0:T(1024)} %param.5, f32[512]{0:T(512)S(1)} %add_rsqrt_fusion), kind=kOutput, calls=%fused_computation.13 | convolution fusion | flops 1614807040 | bytes 9185280 | tf_op jit(solution)/shard_map/dot_general | solution.py:28
  13.7 74.9 %all_to_all.13 = f32[4,192,2048]{2,1,0:T(8,128)} all-to-all(f32[4,192,2048]{2,1,0:T(8,128)S(1)} %bitcast.8), channel_id=1, replica_groups=mesh['grp'=4,'sub'=8] {'grp'}, dimensions={0} | all-to-all | bytes 12582912 | tf_op jit(solution)/shard_map/all_to_all | solution.py:31
  88.6 0.0 copy-start.1
  88.6 0.0 copy-start.2
  88.6 4.8 %reduce_sum.38 = f32[192,2048]{1,0:T(8,128)} reduce(f32[4,192,2048]{2,1,0:T(8,128)} %all_to_all.13, f32[]{:T(128)} %constant.8.clone.1), dimensions={0}, to_apply=%region_2.0 | reduce | flops 1179648 | bytes 7864324 | tf_op jit(solution)/shard_map/reduce_sum | solution.py:32
  93.4 0.0 reduce-scatter.2.cloned.1.call-update
  93.4 0.0 all-gather.2.cloned.1.call-done
  93.4 0.0 copy-done.1
  93.5 0.0 copy-done.2
  93.5 5.9 %fusion.9 = (f32[2048]{0:T(1024)S(1)}, f32[512]{0:T(512)S(1)}, f32[512,2048]{1,0:T(8,128)}) fusion(bf16[512,2048]{1,0:T(8,128)(2,1)S(1)} %copy-done.1, f32[512]{0:T(512)S(1)} %add_rsqrt_fusion, f32[2048]{0:T(1024)S(1)} %copy-done.2, bf16[512,768]{1,0:T(8,128)(2,1)S(1)} %copy-done, bf16[2048,768]{1,0:T(8,128)(2,1)} %all-gather.2.cloned.1.call-done), kind=kOutput, calls=%fused_computation.11 | convolution fusion | flops 1617950208 | bytes 10244096 | tf_op jit(solution)/shard_map/dot_general | solution.py:13
  99.4 40.9 %psum.7 = f32[2048]{0:T(1024)S(1)} all-reduce(f32[2048]{0:T(1024)S(1)} %get-tuple-element.3), channel_id=1, replica_groups=mesh['grp'=4,'sub'=8] {'grp','sub'}, use_global_device_ids=true, to_apply=%region_5.0 | all-reduce | flops 2048 | bytes 16384 | tf_op jit(solution)/shard_map/psum | solution.py:36
  140.3 0.6 dynamic-slice_multiply_fusion
  140.9 4.6 %fusion.7 = bf16[512,2048]{1,0:T(8,128)(2,1)} fusion(bf16[512,2048]{1,0:T(8,128)(2,1)S(1)} %copy-done.1, f32[512,2048]{1,0:T(8,128)} %get-tuple-element.5, f32[512]{0:T(512)S(1)} %broadcast_multiply_fusion, f32[2048]{0:T(1024)S(1)} %copy-done.2, f32[512]{0:T(512)S(1)} %add_rsqrt_fusion), kind=kLoop, calls=%fused_computation.9 | loop fusion | flops 7340032 | bytes 8400896 | tf_op jit(solution)/shard_map/convert_element_type | solution.py:22
  145.5 15.0 %reduce-scatter.2.cloned.1.call-done = f32[192,256]{1,0:T(8,128)} async-done(((f32[192,2048]{1,0:T(8,128)}), f32[192,256]{1,0:T(8,128)}) %reduce-scatter.2.cloned.1.call-update) | async-done | bytes 196624 | tf_op jit(solution)/shard_map/reduce_scatter | solution.py:33
  160.5 1.6 multiply_bitcast_fusion
  (2 shorter events, 0.0 us)
Async XLA Ops:
  7.2 2.9 %copy-start = (bf16[512,768]{1,0:T(8,128)(2,1)S(1)}, bf16[512,768]{1,0:T(8,128)(2,1)}, u32[]{:S(2)}) copy-start(bf16[512,768]{1,0:T(8,128)(2,1)} %param.7) | copy-start | bytes 2359300
  7.2 86.3 %all-gather.2.cloned.1.call-start = ((), (), s32[]{:S(2)}) async-start(), calls=%async_computation.2 | async-start | bytes 3538944 | tf_op jit(solution)/shard_map/all_gather | solution.py:15
  7.9 152.6 %reduce-scatter.2.cloned.1.call-start = ((), (), s32[]{:S(2)}) async-start(), calls=%async_computation.3 | async-start | bytes 1769472 | tf_op jit(solution)/shard_map/reduce_scatter | solution.py:33
  88.6 4.9 %copy-start.1 = (bf16[512,2048]{1,0:T(8,128)(2,1)S(1)}, bf16[512,2048]{1,0:T(8,128)(2,1)}, u32[]{:S(2)}) copy-start(bf16[512,2048]{1,0:T(8,128)(2,1)} %param.4) | copy-start | bytes 6291460
  88.6 4.9 %copy-start.2 = (f32[2048]{0:T(1024)S(1)}, f32[2048]{0:T(1024)}, u32[]{:S(2)}) copy-start(f32[2048]{0:T(1024)} %param.5) | copy-start | bytes 24580
Sparse Core Ops, SparseCore 0:
  10.2 63.1 all-gather.1
  93.5 66.9 reduce-scatter.1
where the time goes:
time: 169 us
  blocking collectives  116 us (69%)
  waiting for transfers between devices  15.7 us (9%)
  between operations  14.1 us (8%)
  other arithmetic  13.7 us (8%)
  matrix products  9.54 us (6%)
    all_to_all x1, blocking collectives, local(): lax.all_to_all(term, 'grp', split_axis=0, concat_axis=1, tiled=True)  74.9 us
    psum x1, blocking collectives, local(): summed = lax.psum(local_gain, ('grp', 'sub'))  40.9 us
    reduce_scatter x1, waiting for transfers between devices, local(): owned = lax.psum_scatter(shared, 'sub', scatter_dimension=1, tiled=True).T  15 us
    dot_general x1, matrix products, local(): lax.dot_general(key_grads, lax.all_gather(key_weight, 'sub', axis=0, tile...  5.93 us
    reduce_sum x1, other arithmetic, local(): shared = jnp.sum(received.reshape(key_rows, groups, model_width), axis=1)  4.82 us
    convert_element_type x1, other arithmetic, local(): input_grads = (inverse_rms * (gained - normed * jnp.mean(gained * normed,...  4.56 us
    dot_general x1, matrix products, local(): lax.dot_general(key_grads, scaled, (((0,), (0,)), ((), ())), preferred_el...  3.61 us
  transfers between devices with their start and end apart: 2, of which 1 were waited for; matrix products, arithmetic and copies ran while one was open for 13% of the time, Pallas kernels for 0%

commit v1 on v0

v1 whole, which is shorter than its diff:
```python
import functools

import jax
import jax.numpy as jnp
from jax import lax
from jax.experimental import pallas as pl
from jax.experimental.pallas import tpu as pltpu
from jax.sharding import PartitionSpec as P

AXES = ("grp", "sub")
EPS = 1e-05
F32 = jnp.float32
BF16 = jnp.bfloat16
VMEM_LIMIT = 48 * 1024 * 1024


def params():
    return pltpu.CompilerParams(vmem_limit_bytes=VMEM_LIMIT)


class Plan:
    def __init__(self, groups, subs):
        self.groups, self.subs = groups, subs
        self.width = groups // 2
        self.depth = subs // self.width

    def index(self, core, y, x, z):
        return (y * 2 + core) * self.subs + z * self.width + x

    def pairs(self, move):
        found = []
        for core in range(2):
            for y in range(self.width):
                for x in range(self.width):
                    for z in range(self.depth):
                        found.append((self.index(core, y, x, z), self.index(*move(core, y, x, z))))
        return found

    def send(self, array, move):
        return lax.ppermute(array, AXES, self.pairs(move))


def place(plan):
    grp, sub = lax.axis_index("grp"), lax.axis_index("sub")
    return grp % 2, grp // 2, sub % plan.width, sub // plan.width


def scale_rows(inputs, norm_gain):
    inverse_rms = lax.rsqrt(jnp.mean(inputs * inputs, axis=1, keepdims=True) + EPS)
    return inputs * inverse_rms, inverse_rms


def term_kernel(
    plan, where, acts_ref, peer_acts_ref, gain_ref, grads_ref, peer_grads_ref,
    sent_ref, kept_ref, total,
):
    core, y, x = where[0], where[1], where[2]
    first = jnp.where(core == 0, y, x)
    width, depth = plan.width, plan.depth
    rows = grads_ref.shape[1] // plan.groups
    cols = acts_ref.shape[1] // plan.subs
    gain = gain_ref[...]

    def chosen(ref):
        both = [
            jnp.concatenate(
                [ref[:, (2 * part + half) * rows : (2 * part + half + 1) * rows] for part in range(width)],
                axis=1,
            )
            for half in range(2)
        ]
        return jnp.where(core == 0, both[0].astype(F32), both[1].astype(F32)).astype(BF16)

    for step, (acts, grads) in enumerate(((acts_ref, grads_ref), (peer_acts_ref, peer_grads_ref))):
        normed, _ = scale_rows(acts[...].astype(F32), gain)
        scaled = (normed * gain).astype(BF16)
        term = lax.dot_general(
            chosen(grads), scaled, (((0,), (0,)), ((), ())), preferred_element_type=F32
        )
        if step == 0:
            total[...] = term
        else:
            total[...] += term

    for to_y in range(width):
        for to_x in range(width):
            to_first = jnp.where(core == 0, to_y, to_x)
            to_second = jnp.where(core == 0, to_x, to_y)
            for to_z in range(depth):
                column = (to_z * width + to_x) * cols
                block = total[to_y * rows : (to_y + 1) * rows, column : column + cols]
                slot = to_second * depth + to_z

                @pl.when(to_first == first)
                def _():
                    kept_ref[pl.ds(slot, 1)] = block[None]

                @pl.when(to_first != first)
                def _():
                    sent_ref[pl.ds(slot, 1)] = block.astype(BF16)[None]


def half_kernel(plan, where, kept_ref, got_ref, sent_ref, held_ref):
    core, y, x = where[0], where[1], where[2]
    second = jnp.where(core == 0, x, y)
    depth = plan.depth
    for to_z in range(depth):
        mine = pl.ds(second * depth + to_z, 1)
        other = pl.ds((1 - second) * depth + to_z, 1)
        held_ref[to_z] = (kept_ref[mine] + got_ref[mine].astype(F32))[0]
        sent_ref[to_z] = (kept_ref[other] + got_ref[other].astype(F32))[0].astype(BF16)


def plane_kernel(plan, where, kept_ref, got_ref, held_ref, *sent_refs):
    z = where[3]
    for step in range(plan.depth):
        plane = pl.ds(z ^ step, 1)
        block = (kept_ref[plane] + got_ref[plane].astype(F32))[0]
        if step == 0:
            held_ref[...] = block
        else:
            sent_refs[step - 1][...] = block.astype(BF16)


def last_kernel(plan, held_ref, *refs):
    total = held_ref[...]
    for ref in refs[:-1]:
        total = total + ref[...].astype(F32)
    refs[-1][...] = total.T / plan.groups


def grad_kernel(plan, where, acts_ref, gain_ref, grads_ref, *refs):
    pieces, (out_ref, sums_ref, weight, sems) = refs[:8], refs[8:]
    core, y, x, z = where[0], where[1], where[2], where[3]
    rows = pieces[0].shape[1]
    step = pl.program_id(0)

    @pl.when(step == 0)
    def _():
        copies = []
        for number, piece in enumerate(pieces):
            other_core, other_y, other_x = number // 4, number // 2 % 2, number % 2
            for offset in range(plan.depth):
                sub = (z ^ offset) * plan.width + (x ^ other_x)
                grp = (y ^ other_y) * 2 + (core ^ other_core)
                start = pl.multiple_of((sub * plan.groups + grp) * rows, rows)
                copies.append(
                    pltpu.make_async_copy(
                        piece.at[offset], weight.at[pl.ds(start, rows)], sems.at[number, offset]
                    )
                )
        for copy in copies:
            copy.start()
        for copy in copies:
            copy.wait()
        sums_ref[...] = jnp.zeros_like(sums_ref)

    gain = gain_ref[...]
    normed, inverse_rms = scale_rows(acts_ref[...].astype(F32), gain)
    grad_scaled = lax.dot_general(
        grads_ref[...], weight[...], (((1,), (1,)), ((), ())), preferred_element_type=F32
    )
    sums_ref[...] += jnp.sum(grad_scaled * normed, axis=0, keepdims=True)
    gained = gain * grad_scaled
    mean = jnp.mean(gained * normed, axis=1, keepdims=True)
    out_ref[...] = (inverse_rms * (gained - normed * mean)).astype(BF16)


SMEM = pl.BlockSpec(memory_space=pltpu.SMEM)
VMEM = pl.BlockSpec(memory_space=pltpu.VMEM)


def by_permutes(plan, activations, norm_gain, key_weight, key_grads):
    tokens, model = activations.shape
    key_width = key_grads.shape[1]
    rows, cols = key_width // plan.groups, model // plan.subs
    width, depth = plan.width, plan.depth
    gain = norm_gain.reshape(1, model)
    core, y, x, z = place(plan)
    where = jnp.stack([core, y, x, z]).astype(jnp.int32)
    shape = jax.ShapeDtypeStruct

    def to_core(core, y, x, z):
        return 1 - core, y, x, z

    def to_x(core, y, x, z):
        return core, y, x ^ 1, z

    def to_y(core, y, x, z):
        return core, y ^ 1, x, z

    def to_z(step):
        return lambda core, y, x, z: (core, y, x, z ^ step)

    def y_then(core, y, x, z):
        return (core, y ^ 1, x, z) if core == 0 else (core, y, x ^ 1, z)

    def x_then(core, y, x, z):
        return (core, y, x ^ 1, z) if core == 0 else (core, y ^ 1, x, z)

    peer_acts = plan.send(activations, to_core)
    peer_grads = plan.send(key_grads, to_core)

    piece_rows = cols // plan.groups
    piece = lax.dynamic_slice_in_dim(key_weight, (y * 2 + core) * piece_rows, piece_rows)
    own = jnp.stack([piece] + [plan.send(piece, to_z(step)) for step in range(1, depth)])
    over_x = plan.send(own, to_x)
    over_y = plan.send(own, to_y)
    over_both = plan.send(jnp.where(core == 0, over_x, over_y), y_then)
    side = [own, over_x, over_y, over_both]
    pieces = side + [plan.send(array, to_core) for array in side]

    term = pl.pallas_call(
        functools.partial(term_kernel, plan),
        out_shape=(
            shape((width * depth, rows, cols), BF16),
            shape((width * depth, rows, cols), F32),
        ),
        in_specs=[SMEM] + [VMEM] * 5,
        out_specs=(VMEM, VMEM),
        scratch_shapes=[pltpu.VMEM((width * rows, model), F32)],
        compiler_params=params(),
        name="term",
    )
    sent, kept = term(where, activations, peer_acts, gain, key_grads, peer_grads)
    got = plan.send(sent, y_then)
    sent, kept = pl.pallas_call(
        functools.partial(half_kernel, plan),
        out_shape=(shape((depth, rows, cols), BF16), shape((depth, rows, cols), F32)),
        in_specs=[SMEM, VMEM, VMEM],
        out_specs=(VMEM, VMEM),
        compiler_params=params(),
        name="half",
    )(where, kept, got)
    got = plan.send(sent, x_then)
    held, *sents = pl.pallas_call(
        functools.partial(plane_kernel, plan),
        out_shape=[shape((rows, cols), F32)] + [shape((rows, cols), BF16)] * (depth - 1),
        in_specs=[SMEM, VMEM, VMEM],
        out_specs=[VMEM] * depth,
        compiler_params=params(),
        name="plane",
    )(where, kept, got)
    gots = [plan.send(array, to_z(step + 1)) for step, array in enumerate(sents)]
    weight_grads = pl.pallas_call(
        functools.partial(last_kernel, plan),
        out_shape=shape((cols, rows), F32),
        in_specs=[VMEM] * depth,
        out_specs=VMEM,
        compiler_params=params(),
        name="last",
    )(held, *gots)

    tile = min(tokens, 128)
    input_grads, sums = pl.pallas_call(
        functools.partial(grad_kernel, plan),
        grid=(tokens // tile,),
        out_shape=(shape((tokens, model), BF16), shape((1, model), F32)),
        in_specs=[
            SMEM,
            pl.BlockSpec((tile, model), lambda i: (i, 0)),
            pl.BlockSpec((1, model), lambda i: (0, 0)),
            pl.BlockSpec((tile, key_width), lambda i: (i, 0)),
        ]
        + [pl.BlockSpec(memory_space=pl.ANY)] * 8,
        out_specs=(
            pl.BlockSpec((tile, model), lambda i: (i, 0)),
            pl.BlockSpec((1, model), lambda i: (0, 0)),
        ),
        scratch_shapes=[
            pltpu.VMEM((model, key_width), BF16),
            pltpu.SemaphoreType.DMA((8, depth)),
        ],
        compiler_params=params(),
        name="grad",
    )(where, activations, gain, key_grads, *pieces)

    sums = sums.reshape(depth, width, cols)
    sums = sums + plan.send(sums, to_core)
    sums = sums + plan.send(sums, to_y)
    mine = lax.dynamic_index_in_dim(sums, x, 1, keepdims=False)
    other = lax.dynamic_index_in_dim(sums, 1 - x, 1, keepdims=False)
    sums = mine + plan.send(other, to_x)
    total = lax.dynamic_index_in_dim(sums, z, 0, keepdims=False)
    for step in range(1, depth):
        part = lax.dynamic_index_in_dim(sums, z ^ step, 0, keepdims=False)
        total = total + plan.send(part, to_z(step))
    return input_grads, weight_grads, total / plan.groups


def by_collectives(activations, norm_gain, key_weight, key_grads):
    inputs = activations.astype(F32)
    inverse_rms = lax.rsqrt(jnp.mean(inputs * inputs, axis=1, keepdims=True) + EPS)
    normed = inputs * inverse_rms
    scaled = (normed * norm_gain).astype(BF16)
    grad_scaled = lax.dot_general(
        key_grads,
        lax.all_gather(key_weight, "sub", axis=0, tiled=True),
        (((1,), (1,)), ((), ())),
        preferred_element_type=F32,
    )
    gained = norm_gain * grad_scaled
    input_grads = (
        inverse_rms * (gained - normed * jnp.mean(gained * normed, axis=1, keepdims=True))
    ).astype(BF16)
    groups = lax.axis_size("grp")
    cols = key_weight.shape[0]
    rows = key_grads.shape[1] // groups
    term = lax.dot_general(
        key_grads, scaled, (((0,), (0,)), ((), ())), preferred_element_type=F32
    )
    received = lax.all_to_all(term, "grp", split_axis=0, concat_axis=1, tiled=True)
    shared = jnp.sum(received.reshape(rows, groups, scaled.shape[1]), axis=1)
    owned = lax.psum_scatter(shared, "sub", scatter_dimension=1, tiled=True).T
    summed = lax.psum(jnp.sum(grad_scaled * normed, axis=0), AXES)
    gain_sum = lax.dynamic_slice_in_dim(summed, lax.axis_index("sub") * cols, cols)
    return input_grads, owned / groups, gain_sum / groups


def local(groups, subs, activations, norm_gain, key_weight, key_grads):
    cols = key_weight.shape[0]
    rows = key_grads.shape[1] // groups
    if groups == 4 and subs % 2 == 0 and subs & (subs - 1) == 0 and cols % 128 == 0 and rows % 16 == 0:
        plan = Plan(groups, subs)
        return by_permutes(plan, activations, norm_gain, key_weight, key_grads)
    return by_collectives(activations, norm_gain, key_weight, key_grads)


def solution(mesh):
    return jax.shard_map(
        functools.partial(local, mesh.shape["grp"], mesh.shape["sub"]),
        mesh=mesh,
        in_specs=(P(AXES, None), P(), P("sub", None), P(AXES, None)),
        out_specs=(P(AXES, None), P("sub", "grp"), P("sub")),
        check_vma=False,
    )
```

time: 169 us -> 83.8 us (0.50)
  blocking collectives: 116 us -> 0 us
  starting transfers between devices: 0.08 us -> 25 us
  Pallas kernels: 0 us -> 19.3 us
  waiting for transfers between devices: 15.7 us -> 31.7 us
  between operations: 14.1 us -> 0.78 us
  other arithmetic: 13.7 us -> 2.38 us
  matrix products: 9.54 us -> 0 us
  local copies, waits for them, and re-layouts: 0.02 us -> 4.39 us
    all_to_all x1 -> x0, blocking collectives: 74.9 us -> none  [local(): lax.all_to_all(term, 'grp', split_axis=0, concat_axis=1, tiled=True)]
    psum x1 -> x0, blocking collectives: 40.9 us -> none  [local(): summed = lax.psum(local_gain, ('grp', 'sub'))]
    ppermute x0 -> x23, waiting for transfers between devices: none -> 31.7 us  [send(): return lax.ppermute(array, AXES, self.pairs(move))]
    ppermute x0 -> x23, starting transfers between devices: none -> 25 us  [send(): return lax.ppermute(array, AXES, self.pairs(move))]
    pallas_call x0 -> x5, Pallas kernels: none -> 19.3 us  [the longest x1 11.6 us: by_permutes(): pl.pallas_call(functools.partial(grad_kernel, plan), grid=(tokens // tile...]
    reduce_scatter x1 -> x0, waiting for transfers between devices: 15 us -> none  [local(): owned = lax.psum_scatter(shared, 'sub', scatter_dimension=1, tiled=True).T]
    dot_general x2 -> x0, matrix products: 9.54 us -> none  [the longest x1 5.93 us: local(): lax.dot_general(key_grads, lax.all_gather(key_weight, 'sub', axis=0, tile...]
    reduce_sum x2 -> x0, other arithmetic: 6.89 us -> none  [the longest x1 4.82 us: local(): shared = jnp.sum(received.reshape(key_rows, groups, model_width), axis=1)]
  transfers between devices with their start and end apart: 2 -> 23, of which waited for: 1 -> 13; matrix products, arithmetic and copies ran while one was open for 13% -> 4% of each run, Pallas kernels for 0% -> 21%
where the time goes in v1:
time: 83.8 us; the launch traced here: 83.5 us
  waiting for transfers between devices  31.7 us (38%)
  starting transfers between devices  25 us (30%)
  Pallas kernels  19.3 us (23%)
  local copies, waits for them, and re-layouts  4.39 us (5%)
  other arithmetic  2.38 us (3%)
    ppermute x23, waiting for transfers between devices, send(): return lax.ppermute(array, AXES, self.pairs(move))  31.7 us
    ppermute x23, starting transfers between devices, send(): return lax.ppermute(array, AXES, self.pairs(move))  25 us
    pallas_call x1, Pallas kernels, by_permutes(): pl.pallas_call(functools.partial(grad_kernel, plan), grid=(tokens // tile...  11.6 us
    pallas_call x1, Pallas kernels, by_permutes(): term(where, activations, peer_acts, gain, key_grads, peer_grads)  5.66 us
    unnamed x14, local copies, waits for them, and re-layouts  3.79 us
  transfers between devices with their start and end apart: 23, of which 13 were waited for; matrix products, arithmetic and copies ran while one was open for 4% of the time, Pallas kernels for 21%

profile of v1, /device:TPU:0, one launch (start us, length us, event | category | flops | bytes accessed | tf_op | source)
XLA Modules:
  0.0 83.5 jit_solution(6894226355294089111)
XLA Ops:
  0.6 0.0 copy-start
  0.7 0.5 collective-permute-start.10
  1.2 0.4 copy-done
  1.6 4.1 %collective-permute-start.1 = (bf16[64,768]{1,0:T(8,128)(2,1)S(1)}, bf16[64,768]{1,0:T(8,128)(2,1)S(1)}, u32[]{:S(2)}, u32[]{:S(2)}) collective-permute-start(bf16[64,768]{1,0:T(8,128)(2,1)S(1)} %constant_dynamic-slice_fusion.6), channel_id=1, source_target_pairs={{0,4},{2,6},{4,0},{6,2},{1,5},{3,7},{5,1},{7,3},{16,20},{18,22},{2... | collective-permute-start | bytes 294920 | tf_op jit(solution)/shard_map/ppermute | solution.py:40
  5.7 1.6 %collective-permute-start = (bf16[64,768]{1,0:T(8,128)(2,1)S(1)}, bf16[64,768]{1,0:T(8,128)(2,1)S(1)}, u32[]{:S(2)}, u32[]{:S(2)}) collective-permute-start(bf16[64,768]{1,0:T(8,128)(2,1)S(1)} %constant_dynamic-slice_fusion.6), channel_id=1, source_target_pairs={{0,2},{2,0},{4,6},{6,4},{1,3},{3,1},{5,7},{7,5},{16,18},{18,16},{2... | collective-permute-start | bytes 294920 | tf_op jit(solution)/shard_map/ppermute | solution.py:40
  7.3 4.4 %collective-permute-done.1 = bf16[64,768]{1,0:T(8,128)(2,1)S(1)} collective-permute-done((bf16[64,768]{1,0:T(8,128)(2,1)S(1)}, bf16[64,768]{1,0:T(8,128)(2,1)S(1)}, u32[]{:S(2)}, u32[]{:S(2)}) %collective-permute-start.1) | collective-permute-done | bytes 98336 | tf_op jit(solution)/shard_map/ppermute | solution.py:40
  11.7 2.2 %collective-permute-done.2 = bf16[64,768]{1,0:T(8,128)(2,1)S(1)} collective-permute-done((bf16[64,768]{1,0:T(8,128)(2,1)S(1)}, bf16[64,768]{1,0:T(8,128)(2,1)S(1)}, u32[]{:S(2)}, u32[]{:S(2)}) %collective-permute-start.2) | collective-permute-done | bytes 98336 | tf_op jit(solution)/shard_map/ppermute | solution.py:40
  13.9 0.1 pad_maximum_fusion.refs_0_
  14.0 1.5 %collective-permute-start.4 = (bf16[4,64,768]{2,1,0:T(8,128)(2,1)S(1)}, bf16[4,64,768]{2,1,0:T(8,128)(2,1)S(1)}, u32[]{:S(2)}, u32[]{:S(2)}) collective-permute-start(bf16[4,64,768]{2,1,0:T(8,128)(2,1)S(1)} %pad_maximum_fusion.refs_0_), channel_id=1, source_target_pairs={{0,16},{2,18},{4,20},{6,22},{1,17},{3,19},{5,21},{7,23},{16,0},{18... | collective-permute-start | bytes 1179656 | tf_op jit(solution)/shard_map/ppermute | solution.py:40
  15.5 1.5 %collective-permute-start.3 = (bf16[4,64,768]{2,1,0:T(8,128)(2,1)S(1)}, bf16[4,64,768]{2,1,0:T(8,128)(2,1)}, u32[]{:S(2)}, u32[]{:S(2)}) collective-permute-start(bf16[4,64,768]{2,1,0:T(8,128)(2,1)S(1)} %pad_maximum_fusion.refs_0_), channel_id=1, source_target_pairs={{0,1},{2,3},{4,5},{6,7},{1,0},{3,2},{5,4},{7,6},{16,17},{18,19},{2... | collective-permute-start | bytes 1179656 | tf_op jit(solution)/shard_map/ppermute | solution.py:40
  17.0 7.1 %collective-permute-done.4.refs_2_ = bf16[4,64,768]{2,1,0:T(8,128)(2,1)S(1)} collective-permute-done((bf16[4,64,768]{2,1,0:T(8,128)(2,1)S(1)}, bf16[4,64,768]{2,1,0:T(8,128)(2,1)S(1)}, u32[]{:S(2)}, u32[]{:S(2)}) %collective-permute-start.4) | collective-permute-done | bytes 393248 | tf_op jit(solution)/shard_map/ppermute | solution.py:40
  24.1 1.3 %collective-permute-done.3.refs_1_ = bf16[4,64,768]{2,1,0:T(8,128)(2,1)} collective-permute-done((bf16[4,64,768]{2,1,0:T(8,128)(2,1)S(1)}, bf16[4,64,768]{2,1,0:T(8,128)(2,1)}, u32[]{:S(2)}, u32[]{:S(2)}) %collective-permute-start.3) | collective-permute-done | bytes 393248 | tf_op jit(solution)/shard_map/ppermute | solution.py:40
  25.4 1.0 %broadcast_select_fusion = bf16[4,64,768]{2,1,0:T(8,128)(2,1)S(1)} fusion(bf16[4,64,768]{2,1,0:T(8,128)(2,1)} %collective-permute-done.3.refs_1_, bf16[4,64,768]{2,1,0:T(8,128)(2,1)S(1)} %collective-permute-done.4.refs_2_, pred[]{:T(512)S(6)} %eq.6), kind=kLoop, calls=%fused_computation.1 | loop fusion | flops 196608 | bytes 1179649 | tf_op jit(solution)/shard_map/jit(_where)/select_n | solution.py:209
  26.4 0.7 collective-permute-start.5
  27.1 0.1 pad_add_fusion.where
  27.2 0.0 copy-start.2
  27.2 1.1 %copy-done.2 = bf16[512,768]{1,0:T(8,128)(2,1)S(1)} copy-done((bf16[512,768]{1,0:T(8,128)(2,1)S(1)}, bf16[512,768]{1,0:T(8,128)(2,1)}, u32[]{:S(2)}) %copy-start.2) | copy-done | bytes 786456
  28.3 5.7 %term.1 = (bf16[8,192,256]{2,1,0:T(8,128)(2,1)}, f32[8,192,256]{2,1,0:T(8,128)S(1)}) custom-call(s32[4]{0:T(128)S(1)} %pad_add_fusion.where, bf16[512,2048]{1,0:T(8,128)(2,1)S(1)} %copy-done.1, bf16[512,2048]{1,0:T(8,128)(2,1)} %collective-permute-done.10.peer_acts_ref, f32[1,2048]{1,0:T(1,128)S(1)} %bitcast.19, bf16[512,768]{1,0:T(8,128)(2,1)S(1)} %copy-done.2, ...), custom_call_target="tpu_custom_call" | custom-call | tf_op jit(solution)/shard_map/term/pallas_call | solution.py:225
  34.0 1.4 %collective-permute-start.12 = (bf16[8,192,256]{2,1,0:T(8,128)(2,1)}, bf16[8,192,256]{2,1,0:T(8,128)(2,1)}, u32[]{:S(2)}, u32[]{:S(2)}) collective-permute-start(bf16[8,192,256]{2,1,0:T(8,128)(2,1)} %get-tuple-element.15), channel_id=1, source_target_pairs={{0,16},{2,18},{4,20},{6,22},{1,17},{3,19},{5,21},{7,23},{16,0},{18... | collective-permute-start | bytes 2359304 | tf_op jit(solution)/shard_map/ppermute | solution.py:40
  35.4 0.5 collective-permute-start.8
  35.9 0.5 collective-permute-start.9
  36.4 0.7 collective-permute-done.6.refs_4_
  37.1 1.1 %collective-permute-done.8.refs_6_ = bf16[4,64,768]{2,1,0:T(8,128)(2,1)S(1)} collective-permute-done((bf16[4,64,768]{2,1,0:T(8,128)(2,1)S(1)}, bf16[4,64,768]{2,1,0:T(8,128)(2,1)S(1)}, u32[]{:S(2)}, u32[]{:S(2)}) %collective-permute-start.8) | collective-permute-done | bytes 393248 | tf_op jit(solution)/shard_map/ppermute | solution.py:40
  38.3 0.2 collective-permute-done.7.refs_5_
  38.5 0.4 collective-permute-done.9.refs_7_
  38.8 11.6 %grad.1 = (bf16[512,2048]{1,0:T(8,128)(2,1)}, f32[1,2048]{1,0:T(1,128)S(1)}) custom-call(s32[4]{0:T(128)S(1)} %pad_add_fusion.where, bf16[512,2048]{1,0:T(8,128)(2,1)S(1)} %copy-done.1, f32[1,2048]{1,0:T(1,128)S(1)} %bitcast.20, bf16[512,768]{1,0:T(8,128)(2,1)S(1)} %copy-done.2, bf16[4,64,768]{2,1,0:T(8,128)(2,1)S(1)} %pad_maximum_fusion.refs_0_, ...), custom_call_target="tpu_custom_call" | custom-call | tf_op jit(solution)/shard_map/grad/pallas_call | solution.py:255
  50.4 0.5 broadcast.8
  51.0 0.6 reduce.3
  51.6 0.2 collective-permute-start.17
  51.8 1.0 %collective-permute-done.17 = f32[4,2,256]{2,1,0:T(2,128)S(1)} collective-permute-done((f32[4,2,256]{2,1,0:T(2,128)S(1)}, f32[4,2,256]{2,1,0:T(2,128)S(1)}, u32[]{:S(2)}, u32[]{:S(2)}) %collective-permute-start.17) | collective-permute-done | bytes 8224 | tf_op jit(solution)/shard_map/ppermute | solution.py:40
  52.9 0.6 collective-permute-start.18
  53.4 3.1 %collective-permute-done.18 = f32[4,2,256]{2,1,0:T(2,128)S(1)} collective-permute-done((f32[4,2,256]{2,1,0:T(2,128)S(1)}, f32[4,2,256]{2,1,0:T(2,128)S(1)}, u32[]{:S(2)}, u32[]{:S(2)}) %collective-permute-start.18) | collective-permute-done | bytes 8224 | tf_op jit(solution)/shard_map/ppermute | solution.py:40
  56.5 1.4 %copy-done.4 = f32[8,192,256]{2,1,0:T(8,128)S(1)} copy-done((f32[8,192,256]{2,1,0:T(8,128)S(1)}, f32[8,192,256]{2,1,0:T(8,128)}, u32[]{:S(2)}) %copy-start.4) | copy-done | bytes 1572888
  57.9 1.3 %half.1 = (bf16[4,192,256]{2,1,0:T(8,128)(2,1)S(1)}, f32[4,192,256]{2,1,0:T(8,128)S(1)}) custom-call(s32[4]{0:T(128)S(1)} %pad_add_fusion.where, f32[8,192,256]{2,1,0:T(8,128)S(1)} %copy-done.4, bf16[8,192,256]{2,1,0:T(8,128)(2,1)} %collective-permute-done.12.got_ref), custom_call_target="tpu_custom_call" | custom-call | tf_op jit(solution)/shard_map/half/pallas_call | solution.py:227
  59.2 1.5 %collective-permute-start.13 = (bf16[4,192,256]{2,1,0:T(8,128)(2,1)S(1)}, bf16[4,192,256]{2,1,0:T(8,128)(2,1)S(1)}, u32[]{:S(2)}, u32[]{:S(2)}) collective-permute-start(bf16[4,192,256]{2,1,0:T(8,128)(2,1)S(1)} %get-tuple-element.17), channel_id=1, source_target_pairs={{0,1},{2,3},{4,5},{6,7},{1,0},{3,2},{5,4},{7,6},{16,17},{18,19},{2... | collective-permute-start | bytes 1179656 | tf_op jit(solution)/shard_map/ppermute | solution.py:40
  60.8 0.6 collective-permute-start.19
  61.4 5.7 %collective-permute-done.19 = f32[4,256]{1,0:T(4,128)S(1)} collective-permute-done((f32[4,256]{1,0:T(4,128)S(1)}, f32[4,256]{1,0:T(4,128)S(1)}, u32[]{:S(2)}, u32[]{:S(2)}) %collective-permute-start.19) | collective-permute-done | bytes 4128 | tf_op jit(solution)/shard_map/ppermute | solution.py:40
  67.1 2.8 %collective-permute-start.22 = (f32[256]{0:T(256)S(1)}, f32[256]{0:T(256)S(1)}, u32[]{:S(2)}, u32[]{:S(2)}) collective-permute-start(f32[256]{0:T(256)S(1)} %bitcast.28), channel_id=1, source_target_pairs={{0,6},{2,4},{4,2},{6,0},{1,7},{3,5},{5,3},{7,1},{16,22},{18,20},{2... | collective-permute-start | bytes 3080 | tf_op jit(solution)/shard_map/ppermute | solution.py:40
  69.9 2.5 %collective-permute-start.20 = (f32[256]{0:T(256)S(1)}, f32[256]{0:T(256)S(1)}, u32[]{:S(2)}, u32[]{:S(2)}) collective-permute-start(f32[256]{0:T(256)S(1)} %bitcast.27), channel_id=1, source_target_pairs={{0,2},{2,0},{4,6},{6,4},{1,3},{3,1},{5,7},{7,5},{16,18},{18,16},{2... | collective-permute-start | bytes 3080 | tf_op jit(solution)/shard_map/ppermute | solution.py:40
  72.4 0.6 plane.1
  73.0 1.6 %collective-permute-start.14 = (bf16[192,256]{1,0:T(8,128)(2,1)S(1)}, bf16[192,256]{1,0:T(8,128)(2,1)S(1)}, u32[]{:S(2)}, u32[]{:S(2)}) collective-permute-start(bf16[192,256]{1,0:T(8,128)(2,1)S(1)} %get-tuple-element.19), channel_id=1, source_target_pairs={{0,2},{2,0},{4,6},{6,4},{1,3},{3,1},{5,7},{7,5},{16,18},{18,16},{2... | collective-permute-start | bytes 294920 | tf_op jit(solution)/shard_map/ppermute | solution.py:40
  74.6 1.5 %collective-permute-start.15 = (bf16[192,256]{1,0:T(8,128)(2,1)S(1)}, bf16[192,256]{1,0:T(8,128)(2,1)S(1)}, u32[]{:S(2)}, u32[]{:S(2)}) collective-permute-start(bf16[192,256]{1,0:T(8,128)(2,1)S(1)} %get-tuple-element.20), channel_id=1, source_target_pairs={{0,4},{2,6},{4,0},{6,2},{1,5},{3,7},{5,1},{7,3},{16,20},{18,22},{2... | collective-permute-start | bytes 294920 | tf_op jit(solution)/shard_map/ppermute | solution.py:40
  76.1 1.4 %collective-permute-start.16 = (bf16[192,256]{1,0:T(8,128)(2,1)S(1)}, bf16[192,256]{1,0:T(8,128)(2,1)S(1)}, u32[]{:S(2)}, u32[]{:S(2)}) collective-permute-start(bf16[192,256]{1,0:T(8,128)(2,1)S(1)} %get-tuple-element.21), channel_id=1, source_target_pairs={{0,6},{2,4},{4,2},{6,0},{1,7},{3,5},{5,3},{7,1},{16,22},{18,20},{2... | collective-permute-start | bytes 294920 | tf_op jit(solution)/shard_map/ppermute | solution.py:40
  77.5 0.6 add_multiply_fusion
  78.0 2.1 %collective-permute-done.15.refs_1_ = bf16[192,256]{1,0:T(8,128)(2,1)S(1)} collective-permute-done((bf16[192,256]{1,0:T(8,128)(2,1)S(1)}, bf16[192,256]{1,0:T(8,128)(2,1)S(1)}, u32[]{:S(2)}, u32[]{:S(2)}) %collective-permute-start.15) | collective-permute-done | bytes 98336 | tf_op jit(solution)/shard_map/ppermute | solution.py:40
  80.1 2.4 %collective-permute-done.16.refs_2_ = bf16[192,256]{1,0:T(8,128)(2,1)S(1)} collective-permute-done((bf16[192,256]{1,0:T(8,128)(2,1)S(1)}, bf16[192,256]{1,0:T(8,128)(2,1)S(1)}, u32[]{:S(2)}, u32[]{:S(2)}) %collective-permute-start.16) | collective-permute-done | bytes 98336 | tf_op jit(solution)/shard_map/ppermute | solution.py:40
  82.6 0.1 last.1
  82.7 0.8 copy.7
  (31 shorter events, 0.1 us)
Async XLA Ops:
  0.6 1.0 %copy-start = (bf16[256,768]{1,0:T(8,128)(2,1)S(1)}, bf16[256,768]{1,0:T(8,128)(2,1)}, u32[]{:S(2)}) copy-start(bf16[256,768]{1,0:T(8,128)(2,1)} %param.6) | copy-start | bytes 1179652
  0.6 26.5 %copy-start.1 = (bf16[512,2048]{1,0:T(8,128)(2,1)S(1)}, bf16[512,2048]{1,0:T(8,128)(2,1)}, u32[]{:S(2)}) copy-start(bf16[512,2048]{1,0:T(8,128)(2,1)} %acts_ref.3) | copy-start | bytes 6291460
  0.7 26.5 %copy-start.5 = (f32[2048]{0:T(1024)S(1)}, f32[2048]{0:T(1024)}, u32[]{:S(2)}) copy-start(f32[2048]{0:T(1024)} %param.5) | copy-start | bytes 24580
  0.7 26.5 %collective-permute-start.10 = (bf16[512,2048]{1,0:T(8,128)(2,1)}, bf16[512,2048]{1,0:T(8,128)(2,1)}, u32[]{:S(2)}, u32[]{:S(2)}) collective-permute-start(bf16[512,2048]{1,0:T(8,128)(2,1)} %acts_ref.3), channel_id=1, source_target_pairs={{0,8},{2,10},{4,12},{6,14},{1,9},{3,11},{5,13},{7,15},{16,24},{18,... | collective-permute-start | bytes 6291464 | tf_op jit(solution)/shard_map/ppermute | solution.py:40
  1.6 10.0 %collective-permute-start.1 = (bf16[64,768]{1,0:T(8,128)(2,1)S(1)}, bf16[64,768]{1,0:T(8,128)(2,1)S(1)}, u32[]{:S(2)}, u32[]{:S(2)}) collective-permute-start(bf16[64,768]{1,0:T(8,128)(2,1)S(1)} %constant_dynamic-slice_fusion.6), channel_id=1, source_target_pairs={{0,4},{2,6},{4,0},{6,2},{1,5},{3,7},{5,1},{7,3},{16,20},{18,22},{2... | collective-permute-start | bytes 294920 | tf_op jit(solution)/shard_map/ppermute | solution.py:40
  5.7 6.0 %collective-permute-start = (bf16[64,768]{1,0:T(8,128)(2,1)S(1)}, bf16[64,768]{1,0:T(8,128)(2,1)S(1)}, u32[]{:S(2)}, u32[]{:S(2)}) collective-permute-start(bf16[64,768]{1,0:T(8,128)(2,1)S(1)} %constant_dynamic-slice_fusion.6), channel_id=1, source_target_pairs={{0,2},{2,0},{4,6},{6,4},{1,3},{3,1},{5,7},{7,5},{16,18},{18,16},{2... | collective-permute-start | bytes 294920 | tf_op jit(solution)/shard_map/ppermute | solution.py:40
  7.3 6.6 %collective-permute-start.2 = (bf16[64,768]{1,0:T(8,128)(2,1)S(1)}, bf16[64,768]{1,0:T(8,128)(2,1)S(1)}, u32[]{:S(2)}, u32[]{:S(2)}) collective-permute-start(bf16[64,768]{1,0:T(8,128)(2,1)S(1)} %constant_dynamic-slice_fusion.6), channel_id=1, source_target_pairs={{0,6},{2,4},{4,2},{6,0},{1,7},{3,5},{5,3},{7,1},{16,22},{18,20},{2... | collective-permute-start | bytes 294920 | tf_op jit(solution)/shard_map/ppermute | solution.py:40
  7.3 19.8 %collective-permute-start.11 = (bf16[512,768]{1,0:T(8,128)(2,1)}, bf16[512,768]{1,0:T(8,128)(2,1)}, u32[]{:S(2)}, u32[]{:S(2)}) collective-permute-start(bf16[512,768]{1,0:T(8,128)(2,1)} %grads_ref.3), channel_id=1, source_target_pairs={{0,8},{2,10},{4,12},{6,14},{1,9},{3,11},{5,13},{7,15},{16,24},{18,... | collective-permute-start | bytes 2359304 | tf_op jit(solution)/shard_map/ppermute | solution.py:40
  14.0 10.1 %collective-permute-start.4 = (bf16[4,64,768]{2,1,0:T(8,128)(2,1)S(1)}, bf16[4,64,768]{2,1,0:T(8,128)(2,1)S(1)}, u32[]{:S(2)}, u32[]{:S(2)}) collective-permute-start(bf16[4,64,768]{2,1,0:T(8,128)(2,1)S(1)} %pad_maximum_fusion.refs_0_), channel_id=1, source_target_pairs={{0,16},{2,18},{4,20},{6,22},{1,17},{3,19},{5,21},{7,23},{16,0},{18... | collective-permute-start | bytes 1179656 | tf_op jit(solution)/shard_map/ppermute | solution.py:40
  15.5 9.9 %collective-permute-start.3 = (bf16[4,64,768]{2,1,0:T(8,128)(2,1)S(1)}, bf16[4,64,768]{2,1,0:T(8,128)(2,1)}, u32[]{:S(2)}, u32[]{:S(2)}) collective-permute-start(bf16[4,64,768]{2,1,0:T(8,128)(2,1)S(1)} %pad_maximum_fusion.refs_0_), channel_id=1, source_target_pairs={{0,1},{2,3},{4,5},{6,7},{1,0},{3,2},{5,4},{7,6},{16,17},{18,19},{2... | collective-permute-start | bytes 1179656 | tf_op jit(solution)/shard_map/ppermute | solution.py:40
  26.4 9.5 %collective-permute-start.5 = (bf16[4,64,768]{2,1,0:T(8,128)(2,1)S(1)}, bf16[4,64,768]{2,1,0:T(8,128)(2,1)S(1)}, u32[]{:S(2)}, u32[]{:S(2)}) collective-permute-start(bf16[4,64,768]{2,1,0:T(8,128)(2,1)S(1)} %broadcast_select_fusion), channel_id=1, source_target_pairs={{0,16},{2,18},{4,20},{6,22},{1,17},{3,19},{5,21},{7,23},{16,0},{18... | collective-permute-start | bytes 1179656 | tf_op jit(solution)/shard_map/ppermute | solution.py:40
  27.2 1.1 %copy-start.2 = (bf16[512,768]{1,0:T(8,128)(2,1)S(1)}, bf16[512,768]{1,0:T(8,128)(2,1)}, u32[]{:S(2)}) copy-start(bf16[512,768]{1,0:T(8,128)(2,1)} %grads_ref.3) | copy-start | bytes 2359300
  34.0 16.4 %copy-start.3 = (f32[8,192,256]{2,1,0:T(8,128)}, f32[8,192,256]{2,1,0:T(8,128)S(1)}, u32[]{:S(2)}) copy-start(f32[8,192,256]{2,1,0:T(8,128)S(1)} %get-tuple-element.14.kept_ref) | copy-start | bytes 4718596
  34.0 22.5 %collective-permute-start.12 = (bf16[8,192,256]{2,1,0:T(8,128)(2,1)}, bf16[8,192,256]{2,1,0:T(8,128)(2,1)}, u32[]{:S(2)}, u32[]{:S(2)}) collective-permute-start(bf16[8,192,256]{2,1,0:T(8,128)(2,1)} %get-tuple-element.15), channel_id=1, source_target_pairs={{0,16},{2,18},{4,20},{6,22},{1,17},{3,19},{5,21},{7,23},{16,0},{18... | collective-permute-start | bytes 2359304 | tf_op jit(solution)/shard_map/ppermute | solution.py:40
  35.4 1.7 %collective-permute-start.6 = (bf16[4,64,768]{2,1,0:T(8,128)(2,1)S(1)}, bf16[4,64,768]{2,1,0:T(8,128)(2,1)S(1)}, u32[]{:S(2)}, u32[]{:S(2)}) collective-permute-start(bf16[4,64,768]{2,1,0:T(8,128)(2,1)S(1)} %pad_maximum_fusion.refs_0_), channel_id=1, source_target_pairs={{0,8},{2,10},{4,12},{6,14},{1,9},{3,11},{5,13},{7,15},{16,24},{18,... | collective-permute-start | bytes 1179656 | tf_op jit(solution)/shard_map/ppermute | solution.py:40
  35.4 2.8 %collective-permute-start.8 = (bf16[4,64,768]{2,1,0:T(8,128)(2,1)S(1)}, bf16[4,64,768]{2,1,0:T(8,128)(2,1)S(1)}, u32[]{:S(2)}, u32[]{:S(2)}) collective-permute-start(bf16[4,64,768]{2,1,0:T(8,128)(2,1)S(1)} %collective-permute-done.4.refs_2_), channel_id=1, source_target_pairs={{0,8},{2,10},{4,12},{6,14},{1,9},{3,11},{5,13},{7,15},{16,24},{18,... | collective-permute-start | bytes 1179656 | tf_op jit(solution)/shard_map/ppermute | solution.py:40
  35.9 2.5 %collective-permute-start.7 = (bf16[4,64,768]{2,1,0:T(8,128)(2,1)}, bf16[4,64,768]{2,1,0:T(8,128)(2,1)S(1)}, u32[]{:S(2)}, u32[]{:S(2)}) collective-permute-start(bf16[4,64,768]{2,1,0:T(8,128)(2,1)} %collective-permute-done.3.refs_1_), channel_id=1, source_target_pairs={{0,8},{2,10},{4,12},{6,14},{1,9},{3,11},{5,13},{7,15},{16,24},{18,... | collective-permute-start | bytes 1179656 | tf_op jit(solution)/shard_map/ppermute | solution.py:40
  35.9 2.9 %collective-permute-start.9 = (bf16[4,64,768]{2,1,0:T(8,128)(2,1)S(1)}, bf16[4,64,768]{2,1,0:T(8,128)(2,1)S(1)}, u32[]{:S(2)}, u32[]{:S(2)}) collective-permute-start(bf16[4,64,768]{2,1,0:T(8,128)(2,1)S(1)} %collective-permute-done.5.refs_3_), channel_id=1, source_target_pairs={{0,8},{2,10},{4,12},{6,14},{1,9},{3,11},{5,13},{7,15},{16,24},{18,... | collective-permute-start | bytes 1179656 | tf_op jit(solution)/shard_map/ppermute | solution.py:40
  51.6 1.2 %collective-permute-start.17 = (f32[4,2,256]{2,1,0:T(2,128)S(1)}, f32[4,2,256]{2,1,0:T(2,128)S(1)}, u32[]{:S(2)}, u32[]{:S(2)}) collective-permute-start(f32[4,2,256]{2,1,0:T(2,128)S(1)} %reshape.13), channel_id=1, source_target_pairs={{0,8},{2,10},{4,12},{6,14},{1,9},{3,11},{5,13},{7,15},{16,24},{18,... | collective-permute-start | bytes 24584 | tf_op jit(solution)/shard_map/ppermute | solution.py:40
  52.9 3.7 %collective-permute-start.18 = (f32[4,2,256]{2,1,0:T(2,128)S(1)}, f32[4,2,256]{2,1,0:T(2,128)S(1)}, u32[]{:S(2)}, u32[]{:S(2)}) collective-permute-start(f32[4,2,256]{2,1,0:T(2,128)S(1)} %add.58), channel_id=1, source_target_pairs={{0,16},{2,18},{4,20},{6,22},{1,17},{3,19},{5,21},{7,23},{16,0},{18... | collective-permute-start | bytes 24584 | tf_op jit(solution)/shard_map/ppermute | solution.py:40
  56.5 1.4 %copy-start.4 = (f32[8,192,256]{2,1,0:T(8,128)S(1)}, f32[8,192,256]{2,1,0:T(8,128)}, u32[]{:S(2)}) copy-start(f32[8,192,256]{2,1,0:T(8,128)} %copy-done.3) | copy-start | bytes 4718596
  59.2 13.1 %collective-permute-start.13 = (bf16[4,192,256]{2,1,0:T(8,128)(2,1)S(1)}, bf16[4,192,256]{2,1,0:T(8,128)(2,1)S(1)}, u32[]{:S(2)}, u32[]{:S(2)}) collective-permute-start(bf16[4,192,256]{2,1,0:T(8,128)(2,1)S(1)} %get-tuple-element.17), channel_id=1, source_target_pairs={{0,1},{2,3},{4,5},{6,7},{1,0},{3,2},{5,4},{7,6},{16,17},{18,19},{2... | collective-permute-start | bytes 1179656 | tf_op jit(solution)/shard_map/ppermute | solution.py:40
  60.8 6.3 %collective-permute-start.19 = (f32[4,256]{1,0:T(4,128)S(1)}, f32[4,256]{1,0:T(4,128)S(1)}, u32[]{:S(2)}, u32[]{:S(2)}) collective-permute-start(f32[4,256]{1,0:T(4,128)S(1)} %bitcast.25), channel_id=1, source_target_pairs={{0,1},{2,3},{4,5},{6,7},{1,0},{3,2},{5,4},{7,6},{16,17},{18,19},{2... | collective-permute-start | bytes 12296 | tf_op jit(solution)/shard_map/ppermute | solution.py:40
  67.1 8.9 %collective-permute-start.22 = (f32[256]{0:T(256)S(1)}, f32[256]{0:T(256)S(1)}, u32[]{:S(2)}, u32[]{:S(2)}) collective-permute-start(f32[256]{0:T(256)S(1)} %bitcast.28), channel_id=1, source_target_pairs={{0,6},{2,4},{4,2},{6,0},{1,7},{3,5},{5,3},{7,1},{16,22},{18,20},{2... | collective-permute-start | bytes 3080 | tf_op jit(solution)/shard_map/ppermute | solution.py:40
  69.9 7.6 %collective-permute-start.20 = (f32[256]{0:T(256)S(1)}, f32[256]{0:T(256)S(1)}, u32[]{:S(2)}, u32[]{:S(2)}) collective-permute-start(f32[256]{0:T(256)S(1)} %bitcast.27), channel_id=1, source_target_pairs={{0,2},{2,0},{4,6},{6,4},{1,3},{3,1},{5,7},{7,5},{16,18},{18,16},{2... | collective-permute-start | bytes 3080 | tf_op jit(solution)/shard_map/ppermute | solution.py:40
  72.4 5.1 %collective-permute-start.21 = (f32[256]{0:T(256)S(1)}, f32[256]{0:T(256)S(1)}, u32[]{:S(2)}, u32[]{:S(2)}) collective-permute-start(f32[256]{0:T(256)S(1)} %bitcast.26), channel_id=1, source_target_pairs={{0,4},{2,6},{4,0},{6,2},{1,5},{3,7},{5,1},{7,3},{16,20},{18,22},{2... | collective-permute-start | bytes 3080 | tf_op jit(solution)/shard_map/ppermute | solution.py:40
  73.0 5.0 %collective-permute-start.14 = (bf16[192,256]{1,0:T(8,128)(2,1)S(1)}, bf16[192,256]{1,0:T(8,128)(2,1)S(1)}, u32[]{:S(2)}, u32[]{:S(2)}) collective-permute-start(bf16[192,256]{1,0:T(8,128)(2,1)S(1)} %get-tuple-element.19), channel_id=1, source_target_pairs={{0,2},{2,0},{4,6},{6,4},{1,3},{3,1},{5,7},{7,5},{16,18},{18,16},{2... | collective-permute-start | bytes 294920 | tf_op jit(solution)/shard_map/ppermute | solution.py:40
  74.6 5.5 %collective-permute-start.15 = (bf16[192,256]{1,0:T(8,128)(2,1)S(1)}, bf16[192,256]{1,0:T(8,128)(2,1)S(1)}, u32[]{:S(2)}, u32[]{:S(2)}) collective-permute-start(bf16[192,256]{1,0:T(8,128)(2,1)S(1)} %get-tuple-element.20), channel_id=1, source_target_pairs={{0,4},{2,6},{4,0},{6,2},{1,5},{3,7},{5,1},{7,3},{16,20},{18,22},{2... | collective-permute-start | bytes 294920 | tf_op jit(solution)/shard_map/ppermute | solution.py:40
  76.1 6.5 %collective-permute-start.16 = (bf16[192,256]{1,0:T(8,128)(2,1)S(1)}, bf16[192,256]{1,0:T(8,128)(2,1)S(1)}, u32[]{:S(2)}, u32[]{:S(2)}) collective-permute-start(bf16[192,256]{1,0:T(8,128)(2,1)S(1)} %get-tuple-element.21), channel_id=1, source_target_pairs={{0,6},{2,4},{4,2},{6,0},{1,7},{3,5},{5,3},{7,1},{16,22},{18,20},{2... | collective-permute-start | bytes 294920 | tf_op jit(solution)/shard_map/ppermute | solution.py:40

commit v2 on v0

v2 whole, which is shorter than its diff:
```python
import functools

import jax
import jax.numpy as jnp
from jax import lax
from jax.experimental import pallas as pl
from jax.experimental.pallas import tpu as pltpu
from jax.sharding import PartitionSpec as P

AXES = ("grp", "sub")
EPS = 1e-05
F32 = jnp.float32
BF16 = jnp.bfloat16
MIB = 1024 * 1024
TILE = 16
CHUNKS = 4


def params(limit):
    return pltpu.CompilerParams(vmem_limit_bytes=limit * MIB)


def cost(flops, moved):
    return pl.CostEstimate(flops=flops, bytes_accessed=moved, transcendentals=0)


class Plan:
    def __init__(self, groups, subs):
        self.groups, self.subs = groups, subs
        self.width = groups // 2
        self.depth = subs // self.width

    def index(self, core, y, x, z):
        return (y * 2 + core) * self.subs + z * self.width + x

    def pairs(self, move):
        found = []
        for core in range(2):
            for y in range(self.width):
                for x in range(self.width):
                    for z in range(self.depth):
                        found.append((self.index(core, y, x, z), self.index(*move(core, y, x, z))))
        return found

    def send(self, array, move):
        return lax.ppermute(array, AXES, self.pairs(move))


def place(plan):
    grp, sub = lax.axis_index("grp"), lax.axis_index("sub")
    return grp % 2, grp // 2, sub % plan.width, sub // plan.width


def slot_of(plan, where, first, second, to_z):
    core = where[0]
    to_x = jnp.where(core == 0, second, first)
    to_y = jnp.where(core == 0, first, second)
    return (to_x * plan.depth + to_z) * plan.width + to_y


def first_and_second(where):
    core, y, x = where[0], where[1], where[2]
    return jnp.where(core == 0, y, x), jnp.where(core == 0, x, y)


def term_kernel(
    plan, where, acts_ref, peer_acts_ref, gain_hbm, grads_ref, peer_grads_ref,
    sent_ref, totals_ref, inverse_ref, acts, grads, gain_ref, scaled, chosen, totals, sems, ends,
):
    core = where[0]
    width, depth = plan.width, plan.depth
    tokens, model = acts.shape[1:]
    rows = grads.shape[1] // plan.groups
    cols = model // plan.subs
    chunk = tokens // CHUNKS

    def fetch(source, target, sem):
        copy = pltpu.make_async_copy(source, target, sem)
        copy.start()
        return copy

    gain_load = fetch(gain_hbm, gain_ref, ends.at[0])
    parts = [pl.ds(part * chunk, chunk) for part in range(CHUNKS)]
    loads = [
        [fetch(source.at[part], acts.at[owner, part], sems.at[owner, k]) for k, part in enumerate(parts)]
        for owner, source in enumerate((acts_ref, peer_acts_ref))
    ]
    grads_load = fetch(grads_ref, grads, ends.at[1])

    def scale(source, first_row, many, base, keep):
        @pl.loop(0, many // TILE, unroll=8)
        def _(step):
            start = pl.multiple_of(first_row + step * TILE, TILE)
            inputs = source[pl.ds(start, TILE), :].astype(F32)
            inverse_rms = lax.rsqrt(jnp.mean(inputs * inputs, axis=1, keepdims=True) + EPS)
            scaled[pl.ds(base + start, TILE), :] = (inputs * inverse_rms * gain_ref[...]).astype(BF16)
            if keep:
                inverse_ref[pl.ds(start, TILE), :] = jnp.broadcast_to(inverse_rms, (TILE, 128))

    def choose(source, base):
        for half in range(2):

            @pl.when(core == half)
            def _():
                for part in range(width):
                    column = (2 * part + half) * rows
                    chosen[part * rows : (part + 1) * rows, base : base + tokens] = source[
                        :, column : column + rows
                    ].T

    choose(peer_grads_ref, tokens)
    gain_load.wait()
    for owner in range(2):
        for part in range(CHUNKS):
            loads[owner][part].wait()
            scale(acts.at[owner], part * chunk, chunk, owner * tokens, owner == 0)
    grads_load.wait()
    choose(grads, 0)

    stores = []
    for to_x in range(width):
        for to_z in range(depth):
            column = (to_z * width + to_x) * cols
            total = jnp.dot(
                chosen[...], scaled[:, column : column + cols], preferred_element_type=F32
            )
            slot = (to_x * depth + to_z) * width
            for to_y in range(width):
                totals[slot + to_y] = total[to_y * rows : (to_y + 1) * rows]
            here = pl.ds(slot, width)
            stores.append(fetch(totals.at[here], totals_ref.at[here], ends.at[2 + slot // width]))

    first, _ = first_and_second(where)
    for second in range(width):
        for to_z in range(depth):
            slot = slot_of(plan, where, 1 - first, second, to_z)
            sent_ref[second * depth + to_z] = totals[pl.ds(slot, 1)][0].astype(BF16)
    for store in stores:
        store.wait()


def load_kept(plan, where, totals_ref, second, kept, sems):
    first, _ = first_and_second(where)
    copies = []
    for to_z in range(plan.depth):
        slot = slot_of(plan, where, first, second, to_z)
        copies.append(pltpu.make_async_copy(totals_ref.at[slot], kept.at[to_z], sems.at[to_z]))
        copies[-1].start()
    for copy in copies:
        copy.wait()


def half_kernel(plan, where, totals_ref, got_ref, sent_ref, kept, sems):
    _, second = first_and_second(where)
    load_kept(plan, where, totals_ref, 1 - second, kept, sems)
    for to_z in range(plan.depth):
        block = kept[to_z] + got_ref[pl.ds((1 - second) * plan.depth + to_z, 1)][0].astype(F32)
        sent_ref[to_z] = block.astype(BF16)


def plane_kernel(plan, where, totals_ref, got_ref, again_ref, held_ref, *refs):
    sent_refs, (kept, sems) = refs[:-2], refs[-2:]
    _, second = first_and_second(where)
    load_kept(plan, where, totals_ref, second, kept, sems)
    for step in range(plan.depth):
        plane = where[3] ^ step
        block = kept[pl.ds(plane, 1)] + got_ref[pl.ds(second * plan.depth + plane, 1)].astype(F32)
        block = (block + again_ref[pl.ds(plane, 1)].astype(F32))[0]
        if step == 0:
            held_ref[...] = block
        else:
            sent_refs[step - 1][...] = block.astype(BF16)


def last_kernel(plan, held_ref, *refs):
    total = held_ref[...]
    for ref in refs[:-1]:
        total = total + ref[...].astype(F32)
    refs[-1][...] = total / plan.groups


def columns(plan, where, flip, step, cols):
    sub = (where[3] ^ step) * plan.width + (where[2] ^ flip)
    return pl.ds(pl.multiple_of(sub * cols, cols), cols)


def load_columns(plan, where, flip, source, target, sems):
    cols = target.shape[-1]
    copies = []
    for step in range(plan.depth):
        here = columns(plan, where, flip, step, cols)
        copies.append(
            pltpu.make_async_copy(source.at[:, here], target.at[step], sems.at[step])
        )
        copies[-1].start()
    return copies


def multiply(plan, where, flip, pieces, acts, gain_ref, grads, inverse, weight, grad_scaled, sums, step):
    core, y = where[0], where[1]
    rows = pieces[0].shape[1]
    tokens, cols = acts.shape[1:]
    for number, piece in enumerate(pieces):
        grp = (y ^ (number % 2)) * 2 + (core ^ (number // 2))
        weight[step, pl.ds(pl.multiple_of(grp * rows, rows), rows)] = piece[step]
    grad_scaled[step] = lax.dot_general(
        grads[...], weight[step], (((1,), (1,)), ((), ())), preferred_element_type=F32
    )
    gain = gain_ref[:, columns(plan, where, flip, step, cols)]
    means = []
    for start in range(0, tokens, TILE):
        part = slice(start, start + TILE)
        scale = inverse[part, :]
        mean = None
        for lane in range(0, cols, 128):
            lanes = slice(lane, lane + 128)
            product = grad_scaled[step, part, lanes] * (acts[step, part, lanes].astype(F32) * scale)
            total = product[:8] + product[8:]
            if start == 0:
                sums[8 * step : 8 * step + 8, lanes] = total
            else:
                sums[8 * step : 8 * step + 8, lanes] += total
            product = product * gain[:, lanes]
            mean = product if mean is None else mean + product
        means.append((part, mean))
    return means


def finish_sums(plan, sums, sums_ref):
    for step in range(plan.depth):
        sums_ref[step : step + 1, :] = jnp.sum(sums[8 * step : 8 * step + 8, :], axis=0, keepdims=True)


def load_kernel(plan, where, acts_ref, grads_ref, acts, grads, sems):
    load = pltpu.make_async_copy(grads_ref, grads, sems.at[2, 0])
    load.start()
    copies = load_columns(plan, where, 0, acts_ref, acts.at[0], sems.at[0])
    copies += load_columns(plan, where, 1, acts_ref, acts.at[1], sems.at[1])
    load.wait()
    for copy in copies:
        copy.wait()


def near_kernel(plan, where, acts, gain_ref, grads, inverse, *refs):
    pieces, (grad_scaled, mean_ref, sums_ref, weight, sums) = refs[:4], refs[4:]
    for step in range(plan.depth):
        means = multiply(
            plan, where, 0, pieces, acts.at[0], gain_ref, grads, inverse, weight, grad_scaled, sums, step
        )
        for part, mean in means:
            if step == 0:
                mean_ref[part, :] = mean
            else:
                mean_ref[part, :] += mean
    finish_sums(plan, sums, sums_ref)


def far_kernel(plan, where, acts, gain_ref, grads, inverse, near, near_mean, *refs):
    pieces, refs = refs[:4], refs[4:]
    out_ref, sums_ref, weight, grad_scaled, mean_ref, out, sums, ends = refs
    tokens, cols = acts.shape[2:]
    model = cols * plan.subs
    for step in range(plan.depth):
        means = multiply(
            plan, where, 1, pieces, acts.at[1], gain_ref, grads, inverse, weight, grad_scaled, sums, step
        )
        for part, mean in means:
            if step == 0:
                mean_ref[part, :] = near_mean[part, :] + mean
            else:
                mean_ref[part, :] += mean
    finish_sums(plan, sums, sums_ref)
    mean = jnp.sum(mean_ref[...], axis=1, keepdims=True) / model
    mean_ref[...] = jnp.broadcast_to(mean, mean_ref.shape)

    stores = []
    for flip, product in ((1, grad_scaled), (0, near)):
        for step in range(plan.depth):
            here = columns(plan, where, flip, step, cols)
            gain = gain_ref[:, here]
            for start in range(0, tokens, TILE):
                part = slice(start, start + TILE)
                scale = inverse[part, :]
                mean = mean_ref[part, :]
                for lane in range(0, cols, 128):
                    lanes = slice(lane, lane + 128)
                    normed = acts[flip, step, part, lanes].astype(F32) * scale
                    gained = gain[:, lanes] * product[step, part, lanes]
                    out[flip, step, part, lanes] = (scale * (gained - normed * mean)).astype(BF16)
            store = pltpu.make_async_copy(
                out.at[flip, step], out_ref.at[:, here], ends.at[flip * plan.depth + step]
            )
            store.start()
            stores.append(store)
    for store in stores:
        store.wait()


SMEM = pl.BlockSpec(memory_space=pltpu.SMEM)
VMEM = pl.BlockSpec(memory_space=pltpu.VMEM)
HBM = pl.BlockSpec(memory_space=pltpu.HBM)


def by_permutes(plan, activations, norm_gain, key_weight, key_grads):
    tokens, model = activations.shape
    key_width = key_grads.shape[1]
    rows, cols = key_width // plan.groups, model // plan.subs
    width, depth = plan.width, plan.depth
    gain = norm_gain.reshape(1, model)
    core, y, x, z = place(plan)
    where = jnp.stack([core, y, x, z]).astype(jnp.int32)
    shape = jax.ShapeDtypeStruct

    def to_core(core, y, x, z):
        return 1 - core, y, x, z

    def to_x(core, y, x, z):
        return core, y, x ^ 1, z

    def to_y(core, y, x, z):
        return core, y ^ 1, x, z

    def to_xy(core, y, x, z):
        return core, y ^ 1, x ^ 1, z

    def to_z(step):
        return lambda core, y, x, z: (core, y, x, z ^ step)

    def y_then(core, y, x, z):
        return (core, y ^ 1, x, z) if core == 0 else (core, y, x ^ 1, z)

    def x_then(core, y, x, z):
        return (core, y, x ^ 1, z) if core == 0 else (core, y ^ 1, x, z)

    peer_acts = plan.send(activations, to_core)
    peer_grads = plan.send(key_grads, to_core)

    piece_rows = cols // plan.groups
    piece = lax.dynamic_slice_in_dim(key_weight, (y * 2 + core) * piece_rows, piece_rows)
    planes = [plan.send(piece, to_z(step)) for step in range(1, depth)]

    def in_hbm(array):
        return pltpu.with_memory_space_constraint(array, pltpu.HBM)

    acts_hbm, grads_hbm, gain_hbm = in_hbm(activations), in_hbm(key_grads), in_hbm(gain)
    sent, kept, inverse = pl.pallas_call(
        functools.partial(term_kernel, plan),
        out_shape=(
            pltpu.VMEM((width * depth, rows, cols), BF16),
            pltpu.HBM((2 * width * depth, rows, cols), F32),
            pltpu.VMEM((tokens, 128), F32),
        ),
        in_specs=[SMEM, HBM, HBM, HBM, HBM, VMEM],
        out_specs=(VMEM, HBM, VMEM),
        scratch_shapes=[
            pltpu.VMEM((2, tokens, model), BF16),
            pltpu.VMEM((tokens, key_width), BF16),
            pltpu.VMEM((1, model), F32),
            pltpu.VMEM((2 * tokens, model), BF16),
            pltpu.VMEM((width * rows, 2 * tokens), BF16),
            pltpu.VMEM((2 * width * depth, rows, cols), F32),
            pltpu.SemaphoreType.DMA((2, CHUNKS)),
            pltpu.SemaphoreType.DMA((2 + width * depth,)),
        ],
        compiler_params=params(20),
        cost_estimate=cost(4 * tokens * model * width * rows, 20 * MIB),
        name="term",
    )(where, acts_hbm, in_hbm(peer_acts), gain_hbm, grads_hbm, peer_grads)
    got = plan.send(sent, y_then)
    planes, _ = lax.optimization_barrier((planes, sent))
    own = jnp.stack([piece] + planes)
    over_x = plan.send(own, to_x)
    over_y = plan.send(own, to_y)
    over_both = plan.send(jnp.where(core == 0, over_x, over_y), y_then)
    peer_own, peer_over_x, peer_over_y = (
        plan.send(array, to_core) for array in (own, over_x, over_y)
    )
    acts, grads = pl.pallas_call(
        functools.partial(load_kernel, plan),
        out_shape=(
            pltpu.VMEM((2, depth, tokens, cols), BF16),
            pltpu.VMEM((tokens, key_width), BF16),
        ),
        in_specs=[SMEM, HBM, HBM],
        out_specs=[VMEM] * 2,
        scratch_shapes=[pltpu.SemaphoreType.DMA((3, depth))],
        compiler_params=params(1),
        cost_estimate=cost(0, 8 * MIB),
        name="load",
    )(where, acts_hbm, grads_hbm)
    (acts, grads), _ = lax.optimization_barrier(((acts, grads), own))
    over_y, _ = lax.optimization_barrier((over_y, acts))
    near, near_mean, near_sums = pl.pallas_call(
        functools.partial(near_kernel, plan),
        out_shape=(
            shape((depth, tokens, cols), F32),
            shape((tokens, 128), F32),
            shape((depth, cols), F32),
        ),
        in_specs=[SMEM] + [VMEM] * 8,
        out_specs=[VMEM] * 3,
        scratch_shapes=[
            pltpu.VMEM((depth, cols, key_width), BF16),
            pltpu.VMEM((8 * depth, cols), F32),
        ],
        compiler_params=params(6),
        cost_estimate=cost(tokens * model * key_width, 8 * MIB),
        name="near",
    )(where, acts, gain, grads, inverse, own, over_y, peer_own, peer_over_y)
    got, _ = lax.optimization_barrier((got, near))
    kept = in_hbm(kept)
    held_scratch = [pltpu.VMEM((depth, rows, cols), F32), pltpu.SemaphoreType.DMA((depth,))]
    sent = pl.pallas_call(
        functools.partial(half_kernel, plan),
        out_shape=shape((depth, rows, cols), BF16),
        in_specs=[SMEM, HBM, VMEM],
        out_specs=VMEM,
        scratch_shapes=held_scratch,
        compiler_params=params(4),
        cost_estimate=cost(0, 2 * MIB),
        name="half",
    )(where, kept, got)
    near_sums = near_sums + plan.send(near_sums, to_y)
    over_both, near, near_sums, _ = lax.optimization_barrier((over_both, near, near_sums, sent))
    peer_over_both = plan.send(over_both, to_core)
    input_grads, far_sums = pl.pallas_call(
        functools.partial(far_kernel, plan),
        out_shape=(shape((tokens, model), BF16), shape((depth, cols), F32)),
        in_specs=[SMEM] + [VMEM] * 10,
        out_specs=(HBM, VMEM),
        scratch_shapes=[
            pltpu.VMEM((depth, cols, key_width), BF16),
            pltpu.VMEM((depth, tokens, cols), F32),
            pltpu.VMEM((tokens, 128), F32),
            pltpu.VMEM((2, depth, tokens, cols), BF16),
            pltpu.VMEM((8 * depth, cols), F32),
            pltpu.SemaphoreType.DMA((2 * depth,)),
        ],
        compiler_params=params(12),
        cost_estimate=cost(tokens * model * key_width, 8 * MIB),
        name="far",
    )(
        where, acts, gain, grads, inverse, near, near_mean,
        over_x, over_both, peer_over_x, peer_over_both,
    )

    again = plan.send(sent, x_then)
    held, *sents = pl.pallas_call(
        functools.partial(plane_kernel, plan),
        out_shape=[shape((rows, cols), F32)] + [shape((rows, cols), BF16)] * (depth - 1),
        in_specs=[SMEM, HBM, VMEM, VMEM],
        out_specs=[VMEM] * depth,
        scratch_shapes=held_scratch,
        compiler_params=params(4),
        cost_estimate=cost(0, 2 * MIB),
        name="plane",
    )(where, kept, got, again)
    gots = [plan.send(array, to_z(step + 1)) for step, array in enumerate(sents)]
    weight_grads = pl.pallas_call(
        functools.partial(last_kernel, plan),
        out_shape=shape((rows, cols), F32),
        in_specs=[VMEM] * depth,
        out_specs=VMEM,
        compiler_params=params(8),
        cost_estimate=cost(0, 2**20),
        name="last",
    )(held, *gots).T

    sums = (plan.send(far_sums, to_x), plan.send(far_sums, to_xy))
    sums, _ = lax.optimization_barrier((sums, sents))
    sums = near_sums + sums[0] + sums[1]
    sums = sums + plan.send(sums, to_core)
    total = sums[0]
    for step in range(1, depth):
        total = total + plan.send(sums[step], to_z(step))
    return input_grads, weight_grads, total / plan.groups


def by_collectives(activations, norm_gain, key_weight, key_grads):
    inputs = activations.astype(F32)
    inverse_rms = lax.rsqrt(jnp.mean(inputs * inputs, axis=1, keepdims=True) + EPS)
    normed = inputs * inverse_rms
    scaled = (normed * norm_gain).astype(BF16)
    grad_scaled = lax.dot_general(
        key_grads,
        lax.all_gather(key_weight, "sub", axis=0, tiled=True),
        (((1,), (1,)), ((), ())),
        preferred_element_type=F32,
    )
    gained = norm_gain * grad_scaled
    input_grads = (
        inverse_rms * (gained - normed * jnp.mean(gained * normed, axis=1, keepdims=True))
    ).astype(BF16)
    groups = lax.axis_size("grp")
    cols = key_weight.shape[0]
    rows = key_grads.shape[1] // groups
    term = lax.dot_general(
        key_grads, scaled, (((0,), (0,)), ((), ())), preferred_element_type=F32
    )
    received = lax.all_to_all(term, "grp", split_axis=0, concat_axis=1, tiled=True)
    shared = jnp.sum(received.reshape(rows, groups, scaled.shape[1]), axis=1)
    owned = lax.psum_scatter(shared, "sub", scatter_dimension=1, tiled=True).T
    summed = lax.psum(jnp.sum(grad_scaled * normed, axis=0), AXES)
    gain_sum = lax.dynamic_slice_in_dim(summed, lax.axis_index("sub") * cols, cols)
    return input_grads, owned / groups, gain_sum / groups


def local(groups, subs, activations, norm_gain, key_weight, key_grads):
    cols = key_weight.shape[0]
    rows = key_grads.shape[1] // groups
    if groups == 4 and subs % 2 == 0 and subs & (subs - 1) == 0 and cols % 128 == 0 and rows % 16 == 0:
        plan = Plan(groups, subs)
        return by_permutes(plan, activations, norm_gain, key_weight, key_grads)
    return by_collectives(activations, norm_gain, key_weight, key_grads)


def solution(mesh):
    return jax.shard_map(
        functools.partial(local, mesh.shape["grp"], mesh.shape["sub"]),
        mesh=mesh,
        in_specs=(P(AXES, None), P(), P("sub", None), P(AXES, None)),
        out_specs=(P(AXES, None), P("sub", "grp"), P("sub")),
        check_vma=False,
    )
```

time: 169 us -> 69.6 us (0.41)
  blocking collectives: 116 us -> 0 us
  starting transfers between devices: 0.08 us -> 25.8 us
  Pallas kernels: 0 us -> 19.7 us
  between operations: 14.1 us -> 0.78 us
  other arithmetic: 13.7 us -> 0.75 us
  matrix products: 9.54 us -> 0 us
  waiting for transfers between devices: 15.7 us -> 21.8 us
    all_to_all x1 -> x0, blocking collectives: 74.9 us -> none  [local(): lax.all_to_all(term, 'grp', split_axis=0, concat_axis=1, tiled=True)]
    psum x1 -> x0, blocking collectives: 40.9 us -> none  [local(): summed = lax.psum(local_gain, ('grp', 'sub'))]
    ppermute x0 -> x24, starting transfers between devices: none -> 25.8 us  [send(): return lax.ppermute(array, AXES, self.pairs(move))]
    ppermute x0 -> x24, waiting for transfers between devices: none -> 21.8 us  [send(): return lax.ppermute(array, AXES, self.pairs(move))]
    pallas_call x0 -> x7, Pallas kernels: none -> 19.7 us  [the longest x1 7.11 us: by_permutes(): pl.pallas_call(functools.partial(term_kernel, plan), out_shape=(pltpu.VME...]
    reduce_scatter x1 -> x0, waiting for transfers between devices: 15 us -> none  [local(): owned = lax.psum_scatter(shared, 'sub', scatter_dimension=1, tiled=True).T]
    dot_general x2 -> x0, matrix products: 9.54 us -> none  [the longest x1 5.93 us: local(): lax.dot_general(key_grads, lax.all_gather(key_weight, 'sub', axis=0, tile...]
    reduce_sum x2 -> x0, other arithmetic: 6.89 us -> none  [the longest x1 4.82 us: local(): shared = jnp.sum(received.reshape(key_rows, groups, model_width), axis=1)]
  transfers between devices with their start and end apart: 2 -> 24, of which waited for: 1 -> 8; matrix products, arithmetic and copies ran while one was open for 13% -> 1% of each run, Pallas kernels for 0% -> 27%
where the time goes in v2:
time: 69.6 us; the launch traced here: 69.3 us
  starting transfers between devices  25.8 us (37%)
  waiting for transfers between devices  21.8 us (31%)
  Pallas kernels  19.7 us (28%)
  between operations  0.78 us (1%)
  other arithmetic  0.75 us (1%)
    ppermute x24, starting transfers between devices, send(): return lax.ppermute(array, AXES, self.pairs(move))  25.8 us
    ppermute x24, waiting for transfers between devices, send(): return lax.ppermute(array, AXES, self.pairs(move))  21.8 us
    pallas_call x1, Pallas kernels, by_permutes(): pl.pallas_call(functools.partial(term_kernel, plan), out_shape=(pltpu.VME...  7.11 us
    pallas_call x1, Pallas kernels, by_permutes(): pl.pallas_call(functools.partial(far_kernel, plan), out_shape=(shape((tok...  4 us
    pallas_call x1, Pallas kernels, by_permutes(): pl.pallas_call(functools.partial(load_kernel, plan), out_shape=(pltpu.VME...  2.41 us
    pallas_call x1, Pallas kernels, by_permutes(): pl.pallas_call(functools.partial(plane_kernel, plan), out_shape=[shape((r...  1.92 us
    pallas_call x1, Pallas kernels, by_permutes(): pl.pallas_call(functools.partial(half_kernel, plan), out_shape=shape((dep...  1.87 us
    pallas_call x1, Pallas kernels, by_permutes(): pl.pallas_call(functools.partial(near_kernel, plan), out_shape=(shape((de...  1.7 us
  transfers between devices with their start and end apart: 24, of which 8 were waited for; matrix products, arithmetic and copies ran while one was open for 1% of the time, Pallas kernels for 27%

profile of v2, /device:TPU:0, one launch (start us, length us, event | category | flops | bytes accessed | tf_op | source)
XLA Modules:
  0.0 69.3 jit_solution(16189247046871684574)
XLA Ops:
  0.6 0.0 copy-start
  0.6 0.5 collective-permute-start.3
  1.2 0.1 collective-permute-start.4
  1.2 0.4 copy-done
  1.6 3.1 %collective-permute-start = (bf16[64,768]{1,0:T(8,128)(2,1)S(1)}, bf16[64,768]{1,0:T(8,128)(2,1)S(1)}, u32[]{:S(2)}, u32[]{:S(2)}) collective-permute-start(bf16[64,768]{1,0:T(8,128)(2,1)S(1)} %constant_dynamic-slice_fusion), channel_id=1, source_target_pairs={{0,2},{2,0},{4,6},{6,4},{1,3},{3,1},{5,7},{7,5},{16,18},{18,16},{2... | collective-permute-start | bytes 294920 | tf_op jit(solution)/shard_map/ppermute | solution.py:46
  4.7 2.6 %collective-permute-start.1 = (bf16[64,768]{1,0:T(8,128)(2,1)S(1)}, bf16[64,768]{1,0:T(8,128)(2,1)S(1)}, u32[]{:S(2)}, u32[]{:S(2)}) collective-permute-start(bf16[64,768]{1,0:T(8,128)(2,1)S(1)} %constant_dynamic-slice_fusion), channel_id=1, source_target_pairs={{0,4},{2,6},{4,0},{6,2},{1,5},{3,7},{5,1},{7,3},{16,20},{18,22},{2... | collective-permute-start | bytes 294920 | tf_op jit(solution)/shard_map/ppermute | solution.py:46
  7.3 0.0 collective-permute-start.2
  7.3 0.1 pad_add_fusion.where
  7.4 0.0 collective-permute-done.4.peer_grads_ref
  7.4 7.1 %term.1 = (bf16[8,192,256]{2,1,0:T(8,128)(2,1)S(1)}, f32[16,192,256]{2,1,0:T(8,128)}, f32[512,128]{1,0:T(8,128)S(1)}) custom-call(s32[4]{0:T(128)S(1)} %pad_add_fusion.where, bf16[512,2048]{1,0:T(8,128)(2,1)} %acts_ref.3, bf16[512,2048]{1,0:T(8,128)(2,1)} %collective-permute-done.3.peer_acts_ref, f32[1,2048]{1,0:T(1,128)} %bitcast.15, ...), custom_call_target="tpu_custom_call" | custom-call | flops 1610612736 | bytes 20971520 | tf_op jit(solution)/shard_map/term/pallas_call | solution.py:346
  14.5 0.0 collective-permute-done
  14.6 0.6 collective-permute-done.1
  15.1 0.0 collective-permute-done.2
  15.1 0.1 pad_maximum_fusion.refs_0_
  15.2 0.0 copy-start.1
  15.2 1.6 %collective-permute-start.6 = (bf16[4,64,768]{2,1,0:T(8,128)(2,1)S(1)}, bf16[4,64,768]{2,1,0:T(8,128)(2,1)S(1)}, u32[]{:S(2)}, u32[]{:S(2)}) collective-permute-start(bf16[4,64,768]{2,1,0:T(8,128)(2,1)S(1)} %pad_maximum_fusion.refs_0_), channel_id=1, source_target_pairs={{0,16},{2,18},{4,20},{6,22},{1,17},{3,19},{5,21},{7,23},{16,0},{18... | collective-permute-start | bytes 1179656 | tf_op jit(solution)/shard_map/ppermute | solution.py:46
  16.8 1.5 %collective-permute-start.5 = (bf16[4,64,768]{2,1,0:T(8,128)(2,1)S(1)}, bf16[4,64,768]{2,1,0:T(8,128)(2,1)S(1)}, u32[]{:S(2)}, u32[]{:S(2)}) collective-permute-start(bf16[4,64,768]{2,1,0:T(8,128)(2,1)S(1)} %pad_maximum_fusion.refs_0_), channel_id=1, source_target_pairs={{0,1},{2,3},{4,5},{6,7},{1,0},{3,2},{5,4},{7,6},{16,17},{18,19},{2... | collective-permute-start | bytes 1179656 | tf_op jit(solution)/shard_map/ppermute | solution.py:46
  18.3 0.5 collective-permute-start.11
  18.8 0.0 collective-permute-start.8
  18.8 7.4 %collective-permute-done.6.refs_1_ = bf16[4,64,768]{2,1,0:T(8,128)(2,1)S(1)} collective-permute-done((bf16[4,64,768]{2,1,0:T(8,128)(2,1)S(1)}, bf16[4,64,768]{2,1,0:T(8,128)(2,1)S(1)}, u32[]{:S(2)}, u32[]{:S(2)}) %collective-permute-start.6) | collective-permute-done | bytes 393248 | tf_op jit(solution)/shard_map/ppermute | solution.py:46
  26.2 2.6 %collective-permute-done.5.refs_0_ = bf16[4,64,768]{2,1,0:T(8,128)(2,1)S(1)} collective-permute-done((bf16[4,64,768]{2,1,0:T(8,128)(2,1)S(1)}, bf16[4,64,768]{2,1,0:T(8,128)(2,1)S(1)}, u32[]{:S(2)}, u32[]{:S(2)}) %collective-permute-start.5) | collective-permute-done | bytes 393248 | tf_op jit(solution)/shard_map/ppermute | solution.py:46
  28.9 0.6 collective-permute-start.7
  29.4 2.4 %load.1 = (bf16[2,4,512,256]{3,2,1,0:T(8,128)(2,1)S(1)}, bf16[512,768]{1,0:T(8,128)(2,1)S(1)}) custom-call(s32[4]{0:T(128)S(1)} %pad_add_fusion.where, bf16[512,2048]{1,0:T(8,128)(2,1)} %acts_ref.3, bf16[512,768]{1,0:T(8,128)(2,1)} %grads_ref.3), custom_call_target="tpu_custom_call" | custom-call | bytes 8388608 | tf_op jit(solution)/shard_map/load/pallas_call | solution.py:378
  31.9 1.7 %near.1 = (f32[4,512,256]{2,1,0:T(8,128)S(1)}, f32[512,128]{1,0:T(8,128)S(1)}, f32[4,256]{1,0:T(4,128)S(1)}) custom-call(s32[4]{0:T(128)S(1)} %pad_add_fusion.where, bf16[2,4,512,256]{3,2,1,0:T(8,128)(2,1)S(1)} %get-tuple-element.35.acts, f32[1,2048]{1,0:T(1,128)S(1)} %bitcast.16, bf16[512,768]{1,0:T(8,128)(2,1)S(1)} %get-tuple-element.36.grads, ...), custom_call_target="tpu_custom_call" | custom-call | flops 805306368 | bytes 8388608 | tf_op jit(solution)/shard_map/near/pallas_call | solution.py:393
  33.6 1.6 %collective-permute-start.10 = (f32[4,256]{1,0:T(4,128)S(1)}, f32[4,256]{1,0:T(4,128)S(1)}, u32[]{:S(2)}, u32[]{:S(2)}) collective-permute-start(f32[4,256]{1,0:T(4,128)S(1)} %get-tuple-element.40), channel_id=1, source_target_pairs={{0,16},{2,18},{4,20},{6,22},{1,17},{3,19},{5,21},{7,23},{16,0},{18... | collective-permute-start | bytes 12296 | tf_op jit(solution)/shard_map/ppermute | solution.py:46
  35.2 0.0 collective-permute-start.12
  35.2 0.0 collective-permute-done.11.got_ref
  35.2 1.9 %half.1 = bf16[4,192,256]{2,1,0:T(8,128)(2,1)S(1)} custom-call(s32[4]{0:T(128)S(1)} %pad_add_fusion.where, f32[16,192,256]{2,1,0:T(8,128)} %get-tuple-element.41.totals_ref, bf16[8,192,256]{2,1,0:T(8,128)(2,1)S(1)} %collective-permute-done.11.got_ref), custom_call_target="tpu_custom_call" | custom-call | bytes 2097152 | tf_op jit(solution)/shard_map/half/pallas_call | solution.py:413
  37.0 1.9 %collective-permute-done.10 = f32[4,256]{1,0:T(4,128)S(1)} collective-permute-done((f32[4,256]{1,0:T(4,128)S(1)}, f32[4,256]{1,0:T(4,128)S(1)}, u32[]{:S(2)}, u32[]{:S(2)}) %collective-permute-start.10) | collective-permute-done | bytes 4128 | tf_op jit(solution)/shard_map/ppermute | solution.py:46
  38.9 0.0 collective-permute-done.7.refs_1_
  38.9 1.2 %collective-permute-start.13 = (bf16[4,64,768]{2,1,0:T(8,128)(2,1)S(1)}, bf16[4,64,768]{2,1,0:T(8,128)(2,1)S(1)}, u32[]{:S(2)}, u32[]{:S(2)}) collective-permute-start(bf16[4,64,768]{2,1,0:T(8,128)(2,1)S(1)} %collective-permute-done.7.refs_1_), channel_id=1, source_target_pairs={{0,8},{2,10},{4,12},{6,14},{1,9},{3,11},{5,13},{7,15},{16,24},{18,... | collective-permute-start | bytes 1179656 | tf_op jit(solution)/shard_map/ppermute | solution.py:46
  40.1 1.5 %collective-permute-start.14 = (bf16[4,192,256]{2,1,0:T(8,128)(2,1)S(1)}, bf16[4,192,256]{2,1,0:T(8,128)(2,1)S(1)}, u32[]{:S(2)}, u32[]{:S(2)}) collective-permute-start(bf16[4,192,256]{2,1,0:T(8,128)(2,1)S(1)} %half.1), channel_id=1, source_target_pairs={{0,1},{2,3},{4,5},{6,7},{1,0},{3,2},{5,4},{7,6},{16,17},{18,19},{2... | collective-permute-start | bytes 1179656 | tf_op jit(solution)/shard_map/ppermute | solution.py:46
  41.6 4.0 %far.1 = (bf16[512,2048]{1,0:T(8,128)(2,1)}, f32[4,256]{1,0:T(4,128)S(1)}) custom-call(s32[4]{0:T(128)S(1)} %pad_add_fusion.where, bf16[2,4,512,256]{3,2,1,0:T(8,128)(2,1)S(1)} %get-tuple-element.35.acts, f32[1,2048]{1,0:T(1,128)S(1)} %bitcast.17, bf16[512,768]{1,0:T(8,128)(2,1)S(1)} %get-tuple-element.36.grads, f32[512,128]{1,0:T(8,128)S(1)} %get-tuple-element.37.inverse, ...), custom_call_target="tpu_custom_call" | custom-call | flops 805306368 | bytes 8388608 | tf_op jit(solution)/shard_map/far/pallas_call | solution.py:426
  45.6 1.4 %collective-permute-start.18 = (f32[4,256]{1,0:T(4,128)S(1)}, f32[4,256]{1,0:T(4,128)S(1)}, u32[]{:S(2)}, u32[]{:S(2)}) collective-permute-start(f32[4,256]{1,0:T(4,128)S(1)} %get-tuple-element.52), channel_id=1, source_target_pairs={{0,1},{2,3},{4,5},{6,7},{1,0},{3,2},{5,4},{7,6},{16,17},{18,19},{2... | collective-permute-start | bytes 12296 | tf_op jit(solution)/shard_map/ppermute | solution.py:46
  47.0 0.9 %collective-permute-start.19 = (f32[4,256]{1,0:T(4,128)S(1)}, f32[4,256]{1,0:T(4,128)S(1)}, u32[]{:S(2)}, u32[]{:S(2)}) collective-permute-start(f32[4,256]{1,0:T(4,128)S(1)} %get-tuple-element.52), channel_id=1, source_target_pairs={{0,17},{2,19},{4,21},{6,23},{1,16},{3,18},{5,20},{7,22},{16,1},{18... | collective-permute-start | bytes 12296 | tf_op jit(solution)/shard_map/ppermute | solution.py:46
  47.9 1.9 %plane.1 = (f32[192,256]{1,0:T(8,128)S(1)}, bf16[192,256]{1,0:T(8,128)(2,1)S(1)}, bf16[192,256]{1,0:T(8,128)(2,1)S(1)}, bf16[192,256]{1,0:T(8,128)(2,1)S(1)}) custom-call(s32[4]{0:T(128)S(1)} %pad_add_fusion.where, f32[16,192,256]{2,1,0:T(8,128)} %get-tuple-element.41.totals_ref, bf16[8,192,256]{2,1,0:T(8,128)(2,1)S(1)} %collective-permute-done.11.got_ref, ...), custom_call_target="tpu_custom_call" | custom-call | bytes 2097152 | tf_op jit(solution)/shard_map/plane/pallas_call | solution.py:448
  49.9 1.7 %collective-permute-done.19 = f32[4,256]{1,0:T(4,128)S(1)} collective-permute-done((f32[4,256]{1,0:T(4,128)S(1)}, f32[4,256]{1,0:T(4,128)S(1)}, u32[]{:S(2)}, u32[]{:S(2)}) %collective-permute-start.19) | collective-permute-done | bytes 4128 | tf_op jit(solution)/shard_map/ppermute | solution.py:46
  51.5 1.2 %collective-permute-done.20 = f32[4,256]{1,0:T(4,128)S(1)} collective-permute-done((f32[4,256]{1,0:T(4,128)S(1)}, f32[4,256]{1,0:T(4,128)S(1)}, u32[]{:S(2)}, u32[]{:S(2)}) %collective-permute-start.20) | collective-permute-done | bytes 4128 | tf_op jit(solution)/shard_map/ppermute | solution.py:46
  52.7 1.6 %collective-permute-start.21 = (f32[256]{0:T(256)S(1)}, f32[256]{0:T(256)S(1)}, u32[]{:S(2)}, u32[]{:S(2)}) collective-permute-start(f32[256]{0:T(256)S(1)} %bitcast.25), channel_id=1, source_target_pairs={{0,2},{2,0},{4,6},{6,4},{1,3},{3,1},{5,7},{7,5},{16,18},{18,16},{2... | collective-permute-start | bytes 3080 | tf_op jit(solution)/shard_map/ppermute | solution.py:46
  54.4 2.6 %collective-permute-start.22 = (f32[256]{0:T(256)S(1)}, f32[256]{0:T(256)S(1)}, u32[]{:S(2)}, u32[]{:S(2)}) collective-permute-start(f32[256]{0:T(256)S(1)} %bitcast.24), channel_id=1, source_target_pairs={{0,4},{2,6},{4,0},{6,2},{1,5},{3,7},{5,1},{7,3},{16,20},{18,22},{2... | collective-permute-start | bytes 3080 | tf_op jit(solution)/shard_map/ppermute | solution.py:46
  56.9 0.2 collective-permute-start.23
  57.2 0.7 collective-permute-start.15
  57.8 3.5 %collective-permute-start.16 = (bf16[192,256]{1,0:T(8,128)(2,1)S(1)}, bf16[192,256]{1,0:T(8,128)(2,1)S(1)}, u32[]{:S(2)}, u32[]{:S(2)}) collective-permute-start(bf16[192,256]{1,0:T(8,128)(2,1)S(1)} %get-tuple-element.49), channel_id=1, source_target_pairs={{0,4},{2,6},{4,0},{6,2},{1,5},{3,7},{5,1},{7,3},{16,20},{18,22},{2... | collective-permute-start | bytes 294920 | tf_op jit(solution)/shard_map/ppermute | solution.py:46
  61.3 0.2 collective-permute-start.17
  61.6 0.9 %collective-permute-done.23 = f32[256]{0:T(256)S(1)} collective-permute-done((f32[256]{0:T(256)S(1)}, f32[256]{0:T(256)S(1)}, u32[]{:S(2)}, u32[]{:S(2)}) %collective-permute-start.23) | collective-permute-done | bytes 1056 | tf_op jit(solution)/shard_map/ppermute | solution.py:46
  62.5 0.6 add_multiply_fusion
  63.0 5.6 %collective-permute-done.16.refs_1_ = bf16[192,256]{1,0:T(8,128)(2,1)S(1)} collective-permute-done((bf16[192,256]{1,0:T(8,128)(2,1)S(1)}, bf16[192,256]{1,0:T(8,128)(2,1)S(1)}, u32[]{:S(2)}, u32[]{:S(2)}) %collective-permute-start.16) | collective-permute-done | bytes 98336 | tf_op jit(solution)/shard_map/ppermute | solution.py:46
  68.6 0.7 %last.1 = f32[192,256]{1,0:T(8,128)} custom-call(f32[192,256]{1,0:T(8,128)S(1)} %get-tuple-element.47.held_ref, bf16[192,256]{1,0:T(8,128)(2,1)S(1)} %collective-permute-done.15.refs_0_, bf16[192,256]{1,0:T(8,128)(2,1)S(1)} %collective-permute-done.16.refs_1_, bf16[192,256]{1,0:T(8,128)(2,1)S(1)} %collective-permute-done.17.refs_2_), custom_call_target="tpu_custom_call" | custom-call | bytes 1048576 | tf_op jit(solution)/shard_map/last/pallas_call | solution.py:459
  (21 shorter events, 0.1 us)
Async XLA Ops:
  0.6 1.0 %copy-start = (bf16[256,768]{1,0:T(8,128)(2,1)S(1)}, bf16[256,768]{1,0:T(8,128)(2,1)}, u32[]{:S(2)}) copy-start(bf16[256,768]{1,0:T(8,128)(2,1)} %param.6) | copy-start | bytes 1179652
  0.6 6.8 %collective-permute-start.3 = (bf16[512,2048]{1,0:T(8,128)(2,1)}, bf16[512,2048]{1,0:T(8,128)(2,1)}, u32[]{:S(2)}, u32[]{:S(2)}) collective-permute-start(bf16[512,2048]{1,0:T(8,128)(2,1)} %acts_ref.3), channel_id=1, source_target_pairs={{0,8},{2,10},{4,12},{6,14},{1,9},{3,11},{5,13},{7,15},{16,24},{18,... | collective-permute-start | bytes 6291464 | tf_op jit(solution)/shard_map/ppermute | solution.py:46
  1.2 6.2 %collective-permute-start.4 = (bf16[512,768]{1,0:T(8,128)(2,1)}, bf16[512,768]{1,0:T(8,128)(2,1)S(1)}, u32[]{:S(2)}, u32[]{:S(2)}) collective-permute-start(bf16[512,768]{1,0:T(8,128)(2,1)} %grads_ref.3), channel_id=1, source_target_pairs={{0,8},{2,10},{4,12},{6,14},{1,9},{3,11},{5,13},{7,15},{16,24},{18,... | collective-permute-start | bytes 2359304 | tf_op jit(solution)/shard_map/ppermute | solution.py:46
  1.6 12.9 %collective-permute-start = (bf16[64,768]{1,0:T(8,128)(2,1)S(1)}, bf16[64,768]{1,0:T(8,128)(2,1)S(1)}, u32[]{:S(2)}, u32[]{:S(2)}) collective-permute-start(bf16[64,768]{1,0:T(8,128)(2,1)S(1)} %constant_dynamic-slice_fusion), channel_id=1, source_target_pairs={{0,2},{2,0},{4,6},{6,4},{1,3},{3,1},{5,7},{7,5},{16,18},{18,16},{2... | collective-permute-start | bytes 294920 | tf_op jit(solution)/shard_map/ppermute | solution.py:46
  4.7 10.4 %collective-permute-start.1 = (bf16[64,768]{1,0:T(8,128)(2,1)S(1)}, bf16[64,768]{1,0:T(8,128)(2,1)S(1)}, u32[]{:S(2)}, u32[]{:S(2)}) collective-permute-start(bf16[64,768]{1,0:T(8,128)(2,1)S(1)} %constant_dynamic-slice_fusion), channel_id=1, source_target_pairs={{0,4},{2,6},{4,0},{6,2},{1,5},{3,7},{5,1},{7,3},{16,20},{18,22},{2... | collective-permute-start | bytes 294920 | tf_op jit(solution)/shard_map/ppermute | solution.py:46
  7.3 7.8 %collective-permute-start.2 = (bf16[64,768]{1,0:T(8,128)(2,1)S(1)}, bf16[64,768]{1,0:T(8,128)(2,1)S(1)}, u32[]{:S(2)}, u32[]{:S(2)}) collective-permute-start(bf16[64,768]{1,0:T(8,128)(2,1)S(1)} %constant_dynamic-slice_fusion), channel_id=1, source_target_pairs={{0,6},{2,4},{4,2},{6,0},{1,7},{3,5},{5,3},{7,1},{16,22},{18,20},{2... | collective-permute-start | bytes 294920 | tf_op jit(solution)/shard_map/ppermute | solution.py:46
  15.2 16.7 %copy-start.1 = (f32[2048]{0:T(1024)S(1)}, f32[2048]{0:T(1024)}, u32[]{:S(2)}) copy-start(f32[2048]{0:T(1024)} %param.5) | copy-start | bytes 24580
  15.2 11.0 %collective-permute-start.6 = (bf16[4,64,768]{2,1,0:T(8,128)(2,1)S(1)}, bf16[4,64,768]{2,1,0:T(8,128)(2,1)S(1)}, u32[]{:S(2)}, u32[]{:S(2)}) collective-permute-start(bf16[4,64,768]{2,1,0:T(8,128)(2,1)S(1)} %pad_maximum_fusion.refs_0_), channel_id=1, source_target_pairs={{0,16},{2,18},{4,20},{6,22},{1,17},{3,19},{5,21},{7,23},{16,0},{18... | collective-permute-start | bytes 1179656 | tf_op jit(solution)/shard_map/ppermute | solution.py:46
  16.8 12.0 %collective-permute-start.5 = (bf16[4,64,768]{2,1,0:T(8,128)(2,1)S(1)}, bf16[4,64,768]{2,1,0:T(8,128)(2,1)S(1)}, u32[]{:S(2)}, u32[]{:S(2)}) collective-permute-start(bf16[4,64,768]{2,1,0:T(8,128)(2,1)S(1)} %pad_maximum_fusion.refs_0_), channel_id=1, source_target_pairs={{0,1},{2,3},{4,5},{6,7},{1,0},{3,2},{5,4},{7,6},{16,17},{18,19},{2... | collective-permute-start | bytes 1179656 | tf_op jit(solution)/shard_map/ppermute | solution.py:46
  18.3 16.9 %collective-permute-start.11 = (bf16[8,192,256]{2,1,0:T(8,128)(2,1)S(1)}, bf16[8,192,256]{2,1,0:T(8,128)(2,1)S(1)}, u32[]{:S(2)}, u32[]{:S(2)}) collective-permute-start(bf16[8,192,256]{2,1,0:T(8,128)(2,1)S(1)} %get-tuple-element.31), channel_id=1, source_target_pairs={{0,16},{2,18},{4,20},{6,22},{1,17},{3,19},{5,21},{7,23},{16,0},{18... | collective-permute-start | bytes 2359304 | tf_op jit(solution)/shard_map/ppermute | solution.py:46
  18.8 13.1 %collective-permute-start.8 = (bf16[4,64,768]{2,1,0:T(8,128)(2,1)S(1)}, bf16[4,64,768]{2,1,0:T(8,128)(2,1)S(1)}, u32[]{:S(2)}, u32[]{:S(2)}) collective-permute-start(bf16[4,64,768]{2,1,0:T(8,128)(2,1)S(1)} %pad_maximum_fusion.refs_0_), channel_id=1, source_target_pairs={{0,8},{2,10},{4,12},{6,14},{1,9},{3,11},{5,13},{7,15},{16,24},{18,... | collective-permute-start | bytes 1179656 | tf_op jit(solution)/shard_map/ppermute | solution.py:46
  26.2 5.7 %collective-permute-start.9 = (bf16[4,64,768]{2,1,0:T(8,128)(2,1)S(1)}, bf16[4,64,768]{2,1,0:T(8,128)(2,1)S(1)}, u32[]{:S(2)}, u32[]{:S(2)}) collective-permute-start(bf16[4,64,768]{2,1,0:T(8,128)(2,1)S(1)} %collective-permute-done.6.refs_1_), channel_id=1, source_target_pairs={{0,8},{2,10},{4,12},{6,14},{1,9},{3,11},{5,13},{7,15},{16,24},{18,... | collective-permute-start | bytes 1179656 | tf_op jit(solution)/shard_map/ppermute | solution.py:46
  28.9 10.1 %collective-permute-start.7 = (bf16[4,64,768]{2,1,0:T(8,128)(2,1)S(1)}, bf16[4,64,768]{2,1,0:T(8,128)(2,1)S(1)}, u32[]{:S(2)}, u32[]{:S(2)}) collective-permute-start(bf16[4,64,768]{2,1,0:T(8,128)(2,1)S(1)} %broadcast_select_fusion), channel_id=1, source_target_pairs={{0,16},{2,18},{4,20},{6,22},{1,17},{3,19},{5,21},{7,23},{16,0},{18... | collective-permute-start | bytes 1179656 | tf_op jit(solution)/shard_map/ppermute | solution.py:46
  33.6 5.3 %collective-permute-start.10 = (f32[4,256]{1,0:T(4,128)S(1)}, f32[4,256]{1,0:T(4,128)S(1)}, u32[]{:S(2)}, u32[]{:S(2)}) collective-permute-start(f32[4,256]{1,0:T(4,128)S(1)} %get-tuple-element.40), channel_id=1, source_target_pairs={{0,16},{2,18},{4,20},{6,22},{1,17},{3,19},{5,21},{7,23},{16,0},{18... | collective-permute-start | bytes 12296 | tf_op jit(solution)/shard_map/ppermute | solution.py:46
  35.2 6.4 %collective-permute-start.12 = (bf16[4,64,768]{2,1,0:T(8,128)(2,1)S(1)}, bf16[4,64,768]{2,1,0:T(8,128)(2,1)S(1)}, u32[]{:S(2)}, u32[]{:S(2)}) collective-permute-start(bf16[4,64,768]{2,1,0:T(8,128)(2,1)S(1)} %collective-permute-done.5.refs_0_), channel_id=1, source_target_pairs={{0,8},{2,10},{4,12},{6,14},{1,9},{3,11},{5,13},{7,15},{16,24},{18,... | collective-permute-start | bytes 1179656 | tf_op jit(solution)/shard_map/ppermute | solution.py:46
  38.9 2.7 %collective-permute-start.13 = (bf16[4,64,768]{2,1,0:T(8,128)(2,1)S(1)}, bf16[4,64,768]{2,1,0:T(8,128)(2,1)S(1)}, u32[]{:S(2)}, u32[]{:S(2)}) collective-permute-start(bf16[4,64,768]{2,1,0:T(8,128)(2,1)S(1)} %collective-permute-done.7.refs_1_), channel_id=1, source_target_pairs={{0,8},{2,10},{4,12},{6,14},{1,9},{3,11},{5,13},{7,15},{16,24},{18,... | collective-permute-start | bytes 1179656 | tf_op jit(solution)/shard_map/ppermute | solution.py:46
  40.1 7.8 %collective-permute-start.14 = (bf16[4,192,256]{2,1,0:T(8,128)(2,1)S(1)}, bf16[4,192,256]{2,1,0:T(8,128)(2,1)S(1)}, u32[]{:S(2)}, u32[]{:S(2)}) collective-permute-start(bf16[4,192,256]{2,1,0:T(8,128)(2,1)S(1)} %half.1), channel_id=1, source_target_pairs={{0,1},{2,3},{4,5},{6,7},{1,0},{3,2},{5,4},{7,6},{16,17},{18,19},{2... | collective-permute-start | bytes 1179656 | tf_op jit(solution)/shard_map/ppermute | solution.py:46
  45.6 4.2 %collective-permute-start.18 = (f32[4,256]{1,0:T(4,128)S(1)}, f32[4,256]{1,0:T(4,128)S(1)}, u32[]{:S(2)}, u32[]{:S(2)}) collective-permute-start(f32[4,256]{1,0:T(4,128)S(1)} %get-tuple-element.52), channel_id=1, source_target_pairs={{0,1},{2,3},{4,5},{6,7},{1,0},{3,2},{5,4},{7,6},{16,17},{18,19},{2... | collective-permute-start | bytes 12296 | tf_op jit(solution)/shard_map/ppermute | solution.py:46
  47.0 4.5 %collective-permute-start.19 = (f32[4,256]{1,0:T(4,128)S(1)}, f32[4,256]{1,0:T(4,128)S(1)}, u32[]{:S(2)}, u32[]{:S(2)}) collective-permute-start(f32[4,256]{1,0:T(4,128)S(1)} %get-tuple-element.52), channel_id=1, source_target_pairs={{0,17},{2,19},{4,21},{6,23},{1,16},{3,18},{5,20},{7,22},{16,1},{18... | collective-permute-start | bytes 12296 | tf_op jit(solution)/shard_map/ppermute | solution.py:46
  51.5 1.2 %collective-permute-start.20 = (f32[4,256]{1,0:T(4,128)S(1)}, f32[4,256]{1,0:T(4,128)S(1)}, u32[]{:S(2)}, u32[]{:S(2)}) collective-permute-start(f32[4,256]{1,0:T(4,128)S(1)} %add_add_fusion), channel_id=1, source_target_pairs={{0,8},{2,10},{4,12},{6,14},{1,9},{3,11},{5,13},{7,15},{16,24},{18,... | collective-permute-start | bytes 12296 | tf_op jit(solution)/shard_map/ppermute | solution.py:46
  52.7 8.6 %collective-permute-start.21 = (f32[256]{0:T(256)S(1)}, f32[256]{0:T(256)S(1)}, u32[]{:S(2)}, u32[]{:S(2)}) collective-permute-start(f32[256]{0:T(256)S(1)} %bitcast.25), channel_id=1, source_target_pairs={{0,2},{2,0},{4,6},{6,4},{1,3},{3,1},{5,7},{7,5},{16,18},{18,16},{2... | collective-permute-start | bytes 3080 | tf_op jit(solution)/shard_map/ppermute | solution.py:46
  54.4 7.2 %collective-permute-start.22 = (f32[256]{0:T(256)S(1)}, f32[256]{0:T(256)S(1)}, u32[]{:S(2)}, u32[]{:S(2)}) collective-permute-start(f32[256]{0:T(256)S(1)} %bitcast.24), channel_id=1, source_target_pairs={{0,4},{2,6},{4,0},{6,2},{1,5},{3,7},{5,1},{7,3},{16,20},{18,22},{2... | collective-permute-start | bytes 3080 | tf_op jit(solution)/shard_map/ppermute | solution.py:46
  56.9 5.5 %collective-permute-start.23 = (f32[256]{0:T(256)S(1)}, f32[256]{0:T(256)S(1)}, u32[]{:S(2)}, u32[]{:S(2)}) collective-permute-start(f32[256]{0:T(256)S(1)} %bitcast.23), channel_id=1, source_target_pairs={{0,6},{2,4},{4,2},{6,0},{1,7},{3,5},{5,3},{7,1},{16,22},{18,20},{2... | collective-permute-start | bytes 3080 | tf_op jit(solution)/shard_map/ppermute | solution.py:46
  57.2 5.9 %collective-permute-start.15 = (bf16[192,256]{1,0:T(8,128)(2,1)S(1)}, bf16[192,256]{1,0:T(8,128)(2,1)S(1)}, u32[]{:S(2)}, u32[]{:S(2)}) collective-permute-start(bf16[192,256]{1,0:T(8,128)(2,1)S(1)} %get-tuple-element.48), channel_id=1, source_target_pairs={{0,2},{2,0},{4,6},{6,4},{1,3},{3,1},{5,7},{7,5},{16,18},{18,16},{2... | collective-permute-start | bytes 294920 | tf_op jit(solution)/shard_map/ppermute | solution.py:46
  57.8 10.8 %collective-permute-start.16 = (bf16[192,256]{1,0:T(8,128)(2,1)S(1)}, bf16[192,256]{1,0:T(8,128)(2,1)S(1)}, u32[]{:S(2)}, u32[]{:S(2)}) collective-permute-start(bf16[192,256]{1,0:T(8,128)(2,1)S(1)} %get-tuple-element.49), channel_id=1, source_target_pairs={{0,4},{2,6},{4,0},{6,2},{1,5},{3,7},{5,1},{7,3},{16,20},{18,22},{2... | collective-permute-start | bytes 294920 | tf_op jit(solution)/shard_map/ppermute | solution.py:46
  61.3 7.3 %collective-permute-start.17 = (bf16[192,256]{1,0:T(8,128)(2,1)S(1)}, bf16[192,256]{1,0:T(8,128)(2,1)S(1)}, u32[]{:S(2)}, u32[]{:S(2)}) collective-permute-start(bf16[192,256]{1,0:T(8,128)(2,1)S(1)} %get-tuple-element.50), channel_id=1, source_target_pairs={{0,6},{2,4},{4,2},{6,0},{1,7},{3,5},{5,3},{7,1},{16,22},{18,20},{2... | collective-permute-start | bytes 294920 | tf_op jit(solution)/shard_map/ppermute | solution.py:46

commit v3 on v0

v3 whole, which is shorter than its diff:
```python
import functools

import jax
import jax.numpy as jnp
from jax import lax
from jax.experimental import pallas as pl
from jax.experimental.pallas import tpu as pltpu
from jax.sharding import PartitionSpec as P

AXES = ("grp", "sub")
EPS = 1e-05
F32 = jnp.float32
BF16 = jnp.bfloat16
MIB = 1024 * 1024
TILE = 16
CHUNKS = 4


def params(limit):
    return pltpu.CompilerParams(vmem_limit_bytes=limit * MIB)


def cost(flops, moved):
    return pl.CostEstimate(flops=0, bytes_accessed=0, transcendentals=0)


class Plan:
    def __init__(self, groups, subs):
        self.groups, self.subs = groups, subs
        self.width = groups // 2
        self.depth = subs // self.width

    def index(self, core, y, x, z):
        return (y * 2 + core) * self.subs + z * self.width + x

    def pairs(self, move):
        found = []
        for core in range(2):
            for y in range(self.width):
                for x in range(self.width):
                    for z in range(self.depth):
                        found.append((self.index(core, y, x, z), self.index(*move(core, y, x, z))))
        return found

    def send(self, array, move):
        return lax.ppermute(array, AXES, self.pairs(move))


def place(plan):
    grp, sub = lax.axis_index("grp"), lax.axis_index("sub")
    return grp % 2, grp // 2, sub % plan.width, sub // plan.width


def slot_of(plan, where, first, second, to_z):
    core = where[0]
    to_x = jnp.where(core == 0, second, first)
    to_y = jnp.where(core == 0, first, second)
    return (to_x * plan.depth + to_z) * plan.width + to_y


def first_and_second(where):
    core, y, x = where[0], where[1], where[2]
    return jnp.where(core == 0, y, x), jnp.where(core == 0, x, y)


def fetch(source, target, sem):
    copy = pltpu.make_async_copy(source, target, sem)
    copy.start()
    return copy


def fetch_rows(source, target, sems):
    chunk = target.shape[0] // CHUNKS
    parts = [pl.ds(part * chunk, chunk) for part in range(CHUNKS)]
    return [fetch(source.at[part], target.at[part], sems.at[k]) for k, part in enumerate(parts)]


def scale_rows(source, gain, scaled, start, stop):
    @pl.loop(0, (stop - start) // TILE, unroll=8)
    def _(step):
        part = pl.ds(pl.multiple_of(start + step * TILE, TILE), TILE)
        inputs = source[part, :].astype(F32)
        inverse_rms = lax.rsqrt(jnp.mean(inputs * inputs, axis=1, keepdims=True) + EPS)
        scaled[part, :] = (inputs * inverse_rms * gain[...]).astype(BF16)


def mine_kernel(
    plan, where, acts_ref, gain_ref, grads_ref, weight_ref,
    scaled, mine, other, piece, acts, grads, gain, weight, sems, ends,
):
    core = where[0]
    tokens = acts.shape[0]
    rows = grads.shape[1] // plan.groups
    load = fetch(gain_ref, gain, ends.at[0])
    loads = fetch_rows(acts_ref, acts, sems)
    grads_load = fetch(grads_ref, grads, ends.at[1])
    weight_load = fetch(weight_ref, weight, ends.at[2])
    load.wait()
    chunk = tokens // CHUNKS
    for part in range(CHUNKS):
        loads[part].wait()
        scale_rows(acts, gain, scaled, part * chunk, (part + 1) * chunk)
    grads_load.wait()
    for half, (even, odd) in enumerate(((mine, other), (other, mine))):

        @pl.when(core == half)
        def _():
            for part in range(plan.width):
                place = slice(part * rows, (part + 1) * rows)
                column = 2 * part * rows
                even[place, :] = grads[:, column : column + rows].T
                odd[place, :] = grads[:, column + rows : column + 2 * rows].T

    weight_load.wait()
    for number in range(plan.groups):

        @pl.when(where[1] * 2 + core == number)
        def _():
            piece[...] = weight[:, number * rows : (number + 1) * rows].T


def term_kernel(
    plan, where, acts, gain_ref, scaled, mine, theirs,
    sent_ref, kept_ref, held_ref, gain, peer_scaled, totals, end,
):
    width, depth = plan.width, plan.depth
    tokens, model = acts.shape
    rows = mine.shape[0] // width
    cols = model // plan.subs
    fetch(gain_ref, gain, end).wait()
    scale_rows(acts, gain, peer_scaled, 0, tokens)

    for to_x in range(width):
        for to_z in range(depth):
            column = (to_z * width + to_x) * cols
            here = slice(column, column + cols)
            total = jnp.dot(mine[...], scaled[:, here], preferred_element_type=F32)
            total += jnp.dot(theirs[...], peer_scaled[:, here], preferred_element_type=F32)
            slot = (to_x * depth + to_z) * width
            for to_y in range(width):
                totals[slot + to_y] = total[to_y * rows : (to_y + 1) * rows]

    first, mine_second = first_and_second(where)
    for to_z in range(depth):
        for second in range(width):
            slot = slot_of(plan, where, 1 - first, second, to_z)
            sent_ref[second * depth + to_z] = totals[pl.ds(slot, 1)][0].astype(BF16)
        for second, out_ref in ((1 - mine_second, kept_ref), (mine_second, held_ref)):
            out_ref[to_z] = totals[pl.ds(slot_of(plan, where, first, second, to_z), 1)][0]


def half_kernel(plan, where, kept, got_ref, *refs):
    pieces, sent_ref = refs[:-1], refs[-1]
    _, second = first_and_second(where)
    for step, piece in enumerate(pieces):
        sent_ref[plan.depth + step] = piece[...]
    for to_z in range(plan.depth):
        block = kept[to_z] + got_ref[pl.ds((1 - second) * plan.depth + to_z, 1)][0].astype(F32)
        sent_ref[to_z] = block.astype(BF16)


def pack_kernel(plan, sent_ref, late_ref, got_ref, late_got_ref, out_ref):
    depth = plan.depth
    for part, (early, late) in enumerate(((sent_ref, late_ref), (got_ref, late_got_ref))):
        out_ref[part * depth : (part + 1) * depth - 1] = early[depth:]
        out_ref[(part + 1) * depth - 1] = late[...]


def plane_kernel(plan, where, held, got_ref, own, again_ref, gain_ref, sums_ref, gains_ref, *sent_refs):
    _, second = first_and_second(where)
    rows, cols = sums_ref.shape
    for step in range(plan.depth):
        plane = where[3] ^ step
        block = held[pl.ds(plane, 1)] + got_ref[pl.ds(second * plan.depth + plane, 1)].astype(F32)
        block = (block + again_ref[pl.ds(plane, 1)].astype(F32))[0]
        gains = jnp.sum(block * own[step].astype(F32), axis=0, keepdims=True)
        gains = gains / gain_ref[:, columns(plan, where, 0, step, cols)]
        if step == 0:
            sums_ref[...] = block
            gains_ref[...] = gains
        else:
            sent_refs[step - 1][:rows, :] = block.astype(BF16)
            row = lax.broadcasted_iota(jnp.int32, (16, cols), 0)
            tail = jnp.zeros((16, cols), F32)
            for number in range(3):
                high = gains.astype(BF16).astype(F32)
                tail = jnp.where(row == number, high, tail)
                gains = gains - high
            sent_refs[step - 1][rows:, :] = tail.astype(BF16)


def last_kernel(plan, sums_ref, gains_ref, *refs):
    got_refs, (out_ref, out_gains_ref) = refs[:-2], refs[-2:]
    rows = sums_ref.shape[0]
    total, gains = sums_ref[...], gains_ref[...]
    for ref in got_refs:
        total = total + ref[:rows, :].astype(F32)
        gains = gains + jnp.sum(ref[rows:, :].astype(F32), axis=0, keepdims=True)
    out_ref[...] = total / plan.groups
    out_gains_ref[...] = gains


def columns(plan, where, flip, step, cols):
    sub = (where[3] ^ step) * plan.width + (where[2] ^ flip)
    return pl.ds(pl.multiple_of(sub * cols, cols), cols)


def load_kernel(plan, where, acts_ref, grads_ref, acts, grads, inverse, sems):
    load = fetch(grads_ref, grads, sems.at[2, 0])
    cols = acts.shape[-1]
    copies = [
        fetch(acts_ref.at[:, columns(plan, where, flip, step, cols)], acts.at[flip, step], sems.at[flip, step])
        for flip in range(2)
        for step in range(plan.depth)
    ]
    load.wait()
    tokens = grads.shape[0]
    for number, copy in enumerate(copies):
        copy.wait()
        block = acts.at[number // plan.depth, number % plan.depth]
        for start in range(0, tokens, TILE):
            part = slice(start, start + TILE)
            square = None
            for lane in range(0, cols, 128):
                inputs = block[part, lane : lane + 128].astype(F32)
                square = inputs * inputs if square is None else square + inputs * inputs
            if number == 0:
                inverse[part, :] = square
            else:
                inverse[part, :] += square
    mean_square = jnp.sum(inverse[...], axis=1, keepdims=True) / (2 * plan.depth * cols)
    inverse[...] = jnp.broadcast_to(lax.rsqrt(mean_square + EPS), inverse.shape)


def place_weight(plan, where, pieces, from_core, second, weight):
    depth = plan.depth
    rows = pieces.shape[1]
    for part in range(2):
        if second:
            flip = from_core if part == 0 else 1
            far_y = (1 - from_core) if part == 0 else 1
        else:
            flip = 0 if part == 0 else 1 - from_core
            far_y = 0 if part == 0 else from_core
        grp = (where[1] ^ far_y) * 2 + from_core
        here = pl.ds(pl.multiple_of(grp * rows, rows), rows)
        for step in range(depth):
            weight[pl.ds(flip * depth + step, 1), here] = pieces[part * depth + step][None]


def grad_kernel(
    plan, where, acts, gain_ref, grads, inverse, mine_sent, mine_got, peer_sent, peer_got,
    out_ref, weight, grad_scaled, mean_ref, out, ends,
):
    core = where[0]
    depth = plan.depth
    tokens, cols = acts.shape[2:]
    model = cols * plan.subs
    place_weight(plan, where, mine_sent, core, False, weight)
    place_weight(plan, where, peer_sent, 1 - core, False, weight)
    place_weight(plan, where, mine_got, core, True, weight)
    place_weight(plan, where, peer_got, 1 - core, True, weight)
    blocks = [(flip, step) for flip in range(2) for step in range(depth)]
    for flip, step in blocks:
        number = flip * depth + step
        grad_scaled[number] = jnp.dot(grads[...], weight[number], preferred_element_type=F32)
        gain = gain_ref[:, columns(plan, where, flip, step, cols)]
        for start in range(0, tokens, TILE):
            part = slice(start, start + TILE)
            scale = inverse[part, :]
            mean = None
            for lane in range(0, cols, 128):
                lanes = slice(lane, lane + 128)
                normed = acts[flip, step, part, lanes].astype(F32) * scale
                product = gain[:, lanes] * grad_scaled[number, part, lanes] * normed
                mean = product if mean is None else mean + product
            if number == 0:
                mean_ref[part, :] = mean
            else:
                mean_ref[part, :] += mean
    mean = jnp.sum(mean_ref[...], axis=1, keepdims=True) / model
    mean_ref[...] = jnp.broadcast_to(mean, mean_ref.shape)

    stores = []
    for flip, step in blocks:
        number = flip * depth + step
        here = columns(plan, where, flip, step, cols)
        gain = gain_ref[:, here]
        for start in range(0, tokens, TILE):
            part = slice(start, start + TILE)
            scale = inverse[part, :]
            mean = mean_ref[part, :]
            for lane in range(0, cols, 128):
                lanes = slice(lane, lane + 128)
                normed = acts[flip, step, part, lanes].astype(F32) * scale
                gained = gain[:, lanes] * grad_scaled[number, part, lanes]
                out[number, part, lanes] = (scale * (gained - normed * mean)).astype(BF16)
        stores.append(fetch(out.at[number], out_ref.at[:, here], ends.at[number]))
    for store in stores:
        store.wait()


SMEM = pl.BlockSpec(memory_space=pltpu.SMEM)
VMEM = pl.BlockSpec(memory_space=pltpu.VMEM)
HBM = pl.BlockSpec(memory_space=pltpu.HBM)


def by_permutes(plan, activations, norm_gain, key_weight, key_grads):
    tokens, model = activations.shape
    key_width = key_grads.shape[1]
    rows, cols = key_width // plan.groups, model // plan.subs
    width, depth = plan.width, plan.depth
    gain = norm_gain.reshape(1, model)
    core, y, x, z = place(plan)
    where = jnp.stack([core, y, x, z]).astype(jnp.int32)
    shape = jax.ShapeDtypeStruct

    def to_core(core, y, x, z):
        return 1 - core, y, x, z

    def to_x(core, y, x, z):
        return core, y, x ^ 1, z

    def to_y(core, y, x, z):
        return core, y ^ 1, x, z

    def to_z(step):
        return lambda core, y, x, z: (core, y, x, z ^ step)

    def y_then(core, y, x, z):
        return (core, y ^ 1, x, z) if core == 0 else (core, y, x ^ 1, z)

    def x_then(core, y, x, z):
        return (core, y, x ^ 1, z) if core == 0 else (core, y ^ 1, x, z)

    def in_hbm(array):
        return pltpu.with_memory_space_constraint(array, pltpu.HBM)

    acts_hbm, grads_hbm, gain_hbm = in_hbm(activations), in_hbm(key_grads), in_hbm(gain)

    peer_acts = plan.send(activations, to_core)
    half_shape = (width * rows, tokens)
    scaled, mine, other, piece = pl.pallas_call(
        functools.partial(mine_kernel, plan),
        out_shape=(
            pltpu.VMEM((tokens, model), BF16),
            pltpu.VMEM(half_shape, BF16),
            pltpu.VMEM(half_shape, BF16),
            pltpu.VMEM((rows, cols), BF16),
        ),
        in_specs=[SMEM, HBM, HBM, HBM, HBM],
        out_specs=[VMEM] * 4,
        scratch_shapes=[
            pltpu.VMEM((tokens, model), BF16),
            pltpu.VMEM((tokens, key_width), BF16),
            pltpu.VMEM((1, model), F32),
            pltpu.VMEM((cols, key_width), BF16),
            pltpu.SemaphoreType.DMA((CHUNKS,)),
            pltpu.SemaphoreType.DMA((3,)),
        ],
        compiler_params=params(5),
        cost_estimate=cost(0, 8 * MIB),
        name="mine",
    )(where, acts_hbm, gain_hbm, grads_hbm, in_hbm(key_weight))
    theirs = plan.send(other, to_core)
    sent, kept, held = pl.pallas_call(
        functools.partial(term_kernel, plan),
        out_shape=(
            pltpu.VMEM((width * depth, rows, cols), BF16),
            pltpu.VMEM((depth, rows, cols), F32),
            pltpu.VMEM((depth, rows, cols), F32),
        ),
        in_specs=[SMEM, VMEM, HBM, VMEM, VMEM, VMEM],
        out_specs=[VMEM] * 3,
        scratch_shapes=[
            pltpu.VMEM((1, model), F32),
            pltpu.VMEM((tokens, model), BF16),
            pltpu.VMEM((2 * width * depth, rows, cols), F32),
            pltpu.SemaphoreType.DMA(()),
        ],
        compiler_params=params(8),
        cost_estimate=cost(4 * tokens * model * width * rows, 20 * MIB),
        name="term",
    )(where, peer_acts, gain_hbm, scaled, mine, theirs)
    got = plan.send(sent, y_then)

    acts, grads, inverse = pl.pallas_call(
        functools.partial(load_kernel, plan),
        out_shape=(
            pltpu.VMEM((2, depth, tokens, cols), BF16),
            pltpu.VMEM((tokens, key_width), BF16),
            pltpu.VMEM((tokens, 128), F32),
        ),
        in_specs=[SMEM, HBM, HBM],
        out_specs=[VMEM] * 3,
        scratch_shapes=[pltpu.SemaphoreType.DMA((3, depth))],
        compiler_params=params(1),
        cost_estimate=cost(0, 8 * MIB),
        name="load",
    )(where, acts_hbm, grads_hbm)

    pieces = [piece] + [plan.send(piece, to_z(step)) for step in range(1, depth - 1)]
    got, pieces, acts, grads = lax.optimization_barrier((got, pieces, acts, grads))

    both = (2 * depth, rows, cols)
    sent = pl.pallas_call(
        functools.partial(half_kernel, plan),
        out_shape=pltpu.VMEM((2 * depth - 1, rows, cols), BF16),
        in_specs=[SMEM] + [VMEM] * (1 + depth),
        out_specs=VMEM,
        compiler_params=params(2),
        cost_estimate=cost(0, 2 * MIB),
        name="half",
    )(where, kept, got, *pieces)
    again = plan.send(sent, x_then)
    late = plan.send(pieces[0], to_z(depth - 1))
    late_again = plan.send(late, x_then)
    mine_sent = pl.pallas_call(
        functools.partial(pack_kernel, plan),
        out_shape=pltpu.VMEM(both, BF16),
        in_specs=[VMEM] * 4,
        out_specs=VMEM,
        compiler_params=params(1),
        cost_estimate=cost(0, 2 * MIB),
        name="pack",
    )(sent, late, again, late_again)
    mine_got = plan.send(mine_sent, y_then)
    peer_sent = plan.send(mine_sent, to_core)
    sums, gains, *sents = pl.pallas_call(
        functools.partial(plane_kernel, plan),
        out_shape=[pltpu.VMEM((rows, cols), F32), pltpu.VMEM((1, cols), F32)]
        + [pltpu.VMEM((rows + 16, cols), BF16)] * (depth - 1),
        in_specs=[SMEM] + [VMEM] * 5,
        out_specs=[VMEM] * (1 + depth),
        compiler_params=params(3),
        cost_estimate=cost(0, 2 * MIB),
        name="plane",
    )(where, held, got, mine_sent, again, gain)
    gots = [plan.send(array, to_z(step + 1)) for step, array in enumerate(sents)]
    mine_got, gots = lax.optimization_barrier((mine_got, gots))
    peer_got = plan.send(mine_got, to_core)
    weight_grads, gains = pl.pallas_call(
        functools.partial(last_kernel, plan),
        out_shape=(shape((rows, cols), F32), pltpu.VMEM((1, cols), F32)),
        in_specs=[VMEM] * (depth + 1),
        out_specs=(VMEM, VMEM),
        compiler_params=params(2),
        cost_estimate=cost(0, MIB),
        name="last",
    )(sums, gains, *gots)
    gains, peer_got = lax.optimization_barrier((gains, peer_got))
    gains = gains + plan.send(gains, to_core)
    gains = gains + plan.send(gains, to_y)

    input_grads = pl.pallas_call(
        functools.partial(grad_kernel, plan),
        out_shape=shape((tokens, model), BF16),
        in_specs=[SMEM] + [VMEM] * 8,
        out_specs=HBM,
        scratch_shapes=[
            pltpu.VMEM((2 * depth, key_width, cols), BF16),
            pltpu.VMEM((2 * depth, tokens, cols), F32),
            pltpu.VMEM((tokens, 128), F32),
            pltpu.VMEM((2 * depth, tokens, cols), BF16),
            pltpu.SemaphoreType.DMA((2 * depth,)),
        ],
        compiler_params=params(12),
        cost_estimate=cost(2 * tokens * model * key_width, 8 * MIB),
        name="grad",
    )(where, acts, gain, grads, inverse, mine_sent, mine_got, peer_sent, peer_got)
    return input_grads, weight_grads.T, gains.reshape(cols) / plan.groups


def by_collectives(activations, norm_gain, key_weight, key_grads):
    inputs = activations.astype(F32)
    inverse_rms = lax.rsqrt(jnp.mean(inputs * inputs, axis=1, keepdims=True) + EPS)
    normed = inputs * inverse_rms
    scaled = (normed * norm_gain).astype(BF16)
    grad_scaled = lax.dot_general(
        key_grads,
        lax.all_gather(key_weight, "sub", axis=0, tiled=True),
        (((1,), (1,)), ((), ())),
        preferred_element_type=F32,
    )
    gained = norm_gain * grad_scaled
    input_grads = (
        inverse_rms * (gained - normed * jnp.mean(gained * normed, axis=1, keepdims=True))
    ).astype(BF16)
    groups = lax.axis_size("grp")
    cols = key_weight.shape[0]
    rows = key_grads.shape[1] // groups
    term = lax.dot_general(
        key_grads, scaled, (((0,), (0,)), ((), ())), preferred_element_type=F32
    )
    received = lax.all_to_all(term, "grp", split_axis=0, concat_axis=1, tiled=True)
    shared = jnp.sum(received.reshape(rows, groups, scaled.shape[1]), axis=1)
    owned = lax.psum_scatter(shared, "sub", scatter_dimension=1, tiled=True).T
    summed = lax.psum(jnp.sum(grad_scaled * normed, axis=0), AXES)
    gain_sum = lax.dynamic_slice_in_dim(summed, lax.axis_index("sub") * cols, cols)
    return input_grads, owned / groups, gain_sum / groups


def local(groups, subs, activations, norm_gain, key_weight, key_grads):
    cols = key_weight.shape[0]
    rows = key_grads.shape[1] // groups
    if groups == 4 and subs % 2 == 0 and subs & (subs - 1) == 0 and cols % 128 == 0 and rows % 16 == 0:
        plan = Plan(groups, subs)
        return by_permutes(plan, activations, norm_gain, key_weight, key_grads)
    return by_collectives(activations, norm_gain, key_weight, key_grads)


def solution(mesh):
    return jax.shard_map(
        functools.partial(local, mesh.shape["grp"], mesh.shape["sub"]),
        mesh=mesh,
        in_specs=(P(AXES, None), P(), P("sub", None), P(AXES, None)),
        out_specs=(P(AXES, None), P("sub", "grp"), P("sub")),
        check_vma=False,
    )
```

time: 169 us -> 60.7 us (0.36)
  blocking collectives: 116 us -> 0 us
  starting transfers between devices: 0.08 us -> 22.3 us
  Pallas kernels: 0 us -> 17.1 us
  between operations: 14.1 us -> 0.7 us
  other arithmetic: 13.7 us -> 0.65 us
  matrix products: 9.54 us -> 0 us
  waiting for transfers between devices: 15.7 us -> 19.8 us
    all_to_all x1 -> x0, blocking collectives: 74.9 us -> none  [local(): lax.all_to_all(term, 'grp', split_axis=0, concat_axis=1, tiled=True)]
    psum x1 -> x0, blocking collectives: 40.9 us -> none  [local(): summed = lax.psum(local_gain, ('grp', 'sub'))]
    ppermute x0 -> x16, starting transfers between devices: none -> 22.3 us  [send(): return lax.ppermute(array, AXES, self.pairs(move))]
    ppermute x0 -> x16, waiting for transfers between devices: none -> 19.8 us  [send(): return lax.ppermute(array, AXES, self.pairs(move))]
    pallas_call x0 -> x8, Pallas kernels: none -> 17.1 us  [the longest x1 4.99 us: by_permutes(): pl.pallas_call(functools.partial(grad_kernel, plan), out_shape=shape((tok...]
    reduce_scatter x1 -> x0, waiting for transfers between devices: 15 us -> none  [local(): owned = lax.psum_scatter(shared, 'sub', scatter_dimension=1, tiled=True).T]
    dot_general x2 -> x0, matrix products: 9.54 us -> none  [the longest x1 5.93 us: local(): lax.dot_general(key_grads, lax.all_gather(key_weight, 'sub', axis=0, tile...]
    reduce_sum x2 -> x0, other arithmetic: 6.89 us -> none  [the longest x1 4.82 us: local(): shared = jnp.sum(received.reshape(key_rows, groups, model_width), axis=1)]
  transfers between devices with their start and end apart: 2 -> 16, of which waited for: 1 -> 11; matrix products, arithmetic and copies ran while one was open for 13% -> 0% of each run, Pallas kernels for 0% -> 20%
where the time goes in v3:
time: 60.7 us; the launch traced here: 60.5 us
  starting transfers between devices  22.3 us (37%)
  waiting for transfers between devices  19.8 us (33%)
  Pallas kernels  17.1 us (28%)
  between operations  0.7 us (1%)
  other arithmetic  0.65 us (1%)
    ppermute x16, starting transfers between devices, send(): return lax.ppermute(array, AXES, self.pairs(move))  22.3 us
    ppermute x16, waiting for transfers between devices, send(): return lax.ppermute(array, AXES, self.pairs(move))  19.8 us
    pallas_call x1, Pallas kernels, by_permutes(): pl.pallas_call(functools.partial(grad_kernel, plan), out_shape=shape((tok...  4.99 us
    pallas_call x1, Pallas kernels, by_permutes(): pl.pallas_call(functools.partial(term_kernel, plan), out_shape=(pltpu.VME...  4.11 us
    pallas_call x1, Pallas kernels, by_permutes(): pl.pallas_call(functools.partial(mine_kernel, plan), out_shape=(pltpu.VME...  3.18 us
    pallas_call x1, Pallas kernels, by_permutes(): pl.pallas_call(functools.partial(load_kernel, plan), out_shape=(pltpu.VME...  2.56 us
  transfers between devices with their start and end apart: 16, of which 11 were waited for; matrix products, arithmetic and copies ran while one was open for 0% of the time, Pallas kernels for 20%

profile of v3, /device:TPU:0, one launch (start us, length us, event | category | flops | bytes accessed | tf_op | source)
XLA Modules:
  0.0 60.5 jit_solution(10535476229414021929)
XLA Ops:
  0.6 0.5 collective-permute-start
  1.1 0.1 pad_add_fusion.where
  1.2 3.2 %mine.1 = (bf16[512,2048]{1,0:T(8,128)(2,1)S(1)}, bf16[384,512]{1,0:T(8,128)(2,1)S(1)}, bf16[384,512]{1,0:T(8,128)(2,1)S(1)}, bf16[192,256]{1,0:T(8,128)(2,1)S(1)}) custom-call(s32[4]{0:T(128)S(1)} %pad_add_fusion.where, bf16[512,2048]{1,0:T(8,128)(2,1)} %acts_ref.3, f32[1,2048]{1,0:T(1,128)} %bitcast.7, bf16[512,768]{1,0:T(8,128)(2,1)} %grads_ref.3, ...), custom_call_target="tpu_custom_call" | custom-call | tf_op jit(solution)/shard_map/mine/pallas_call | solution.py:343
  4.4 0.2 collective-permute-start.1
  4.6 1.6 %collective-permute-done.1.theirs = bf16[384,512]{1,0:T(8,128)(2,1)S(1)} collective-permute-done((bf16[384,512]{1,0:T(8,128)(2,1)S(1)}, bf16[384,512]{1,0:T(8,128)(2,1)S(1)}, u32[]{:S(2)}, u32[]{:S(2)}) %collective-permute-start.1) | collective-permute-done | bytes 393248 | tf_op jit(solution)/shard_map/ppermute | solution.py:46
  6.2 0.0 collective-permute-done.acts
  6.2 4.1 %term.1 = (bf16[8,192,256]{2,1,0:T(8,128)(2,1)S(1)}, f32[4,192,256]{2,1,0:T(8,128)S(1)}, f32[4,192,256]{2,1,0:T(8,128)S(1)}) custom-call(s32[4]{0:T(128)S(1)} %pad_add_fusion.where, bf16[512,2048]{1,0:T(8,128)(2,1)S(1)} %collective-permute-done.acts, f32[1,2048]{1,0:T(1,128)} %bitcast.8, bf16[512,2048]{1,0:T(8,128)(2,1)S(1)} %get-tuple-element.32.scaled, ...), custom_call_target="tpu_custom_call" | custom-call | tf_op jit(solution)/shard_map/term/pallas_call | solution.py:366
  10.3 2.8 %collective-permute-start.2 = (bf16[8,192,256]{2,1,0:T(8,128)(2,1)S(1)}, bf16[8,192,256]{2,1,0:T(8,128)(2,1)S(1)}, u32[]{:S(2)}, u32[]{:S(2)}) collective-permute-start(bf16[8,192,256]{2,1,0:T(8,128)(2,1)S(1)} %get-tuple-element.35), channel_id=1, source_target_pairs={{0,16},{2,18},{4,20},{6,22},{1,17},{3,19},{5,21},{7,23},{16,0},{18... | collective-permute-start | bytes 2359304 | tf_op jit(solution)/shard_map/ppermute | solution.py:46
  13.1 2.6 %collective-permute-start.4 = (bf16[192,256]{1,0:T(8,128)(2,1)S(1)}, bf16[192,256]{1,0:T(8,128)(2,1)S(1)}, u32[]{:S(2)}, u32[]{:S(2)}) collective-permute-start(bf16[192,256]{1,0:T(8,128)(2,1)S(1)} %get-tuple-element.44.refs_0_), channel_id=1, source_target_pairs={{0,4},{2,6},{4,0},{6,2},{1,5},{3,7},{5,1},{7,3},{16,20},{18,22},{2... | collective-permute-start | bytes 294920 | tf_op jit(solution)/shard_map/ppermute | solution.py:46
  15.7 1.6 %collective-permute-start.3 = (bf16[192,256]{1,0:T(8,128)(2,1)S(1)}, bf16[192,256]{1,0:T(8,128)(2,1)S(1)}, u32[]{:S(2)}, u32[]{:S(2)}) collective-permute-start(bf16[192,256]{1,0:T(8,128)(2,1)S(1)} %get-tuple-element.44.refs_0_), channel_id=1, source_target_pairs={{0,2},{2,0},{4,6},{6,4},{1,3},{3,1},{5,7},{7,5},{16,18},{18,16},{2... | collective-permute-start | bytes 294920 | tf_op jit(solution)/shard_map/ppermute | solution.py:46
  17.3 2.6 %load.1 = (bf16[2,4,512,256]{3,2,1,0:T(8,128)(2,1)S(1)}, bf16[512,768]{1,0:T(8,128)(2,1)S(1)}, f32[512,128]{1,0:T(8,128)S(1)}) custom-call(s32[4]{0:T(128)S(1)} %pad_add_fusion.where, bf16[512,2048]{1,0:T(8,128)(2,1)} %acts_ref.3, bf16[512,768]{1,0:T(8,128)(2,1)} %grads_ref.3), custom_call_target="tpu_custom_call" | custom-call | tf_op jit(solution)/shard_map/load/pallas_call | solution.py:387
  19.9 1.1 %collective-permute-done.4.refs_2_ = bf16[192,256]{1,0:T(8,128)(2,1)S(1)} collective-permute-done((bf16[192,256]{1,0:T(8,128)(2,1)S(1)}, bf16[192,256]{1,0:T(8,128)(2,1)S(1)}, u32[]{:S(2)}, u32[]{:S(2)}) %collective-permute-start.4) | collective-permute-done | bytes 98336 | tf_op jit(solution)/shard_map/ppermute | solution.py:46
  21.0 0.2 collective-permute-done.3.refs_1_
  21.2 1.9 %collective-permute-done.2.got_ref = bf16[8,192,256]{2,1,0:T(8,128)(2,1)S(1)} collective-permute-done((bf16[8,192,256]{2,1,0:T(8,128)(2,1)S(1)}, bf16[8,192,256]{2,1,0:T(8,128)(2,1)S(1)}, u32[]{:S(2)}, u32[]{:S(2)}) %collective-permute-start.2) | collective-permute-done | bytes 786464 | tf_op jit(solution)/shard_map/ppermute | solution.py:46
  23.1 0.0 copy-start
  23.1 0.6 %half.1.sent_ref = bf16[7,192,256]{2,1,0:T(8,128)(2,1)S(1)} custom-call(s32[4]{0:T(128)S(1)} %pad_add_fusion.where, f32[4,192,256]{2,1,0:T(8,128)S(1)} %get-tuple-element.42.kept, bf16[8,192,256]{2,1,0:T(8,128)(2,1)S(1)} %collective-permute-done.2.got_ref, bf16[192,256]{1,0:T(8,128)(2,1)S(1)} %get-tuple-element.44.refs_0_, ...), custom_call_target="tpu_custom_call" | custom-call | tf_op jit(solution)/shard_map/half/pallas_call | solution.py:406
  23.7 2.0 %collective-permute-start.6 = (bf16[7,192,256]{2,1,0:T(8,128)(2,1)S(1)}, bf16[7,192,256]{2,1,0:T(8,128)(2,1)S(1)}, u32[]{:S(2)}, u32[]{:S(2)}) collective-permute-start(bf16[7,192,256]{2,1,0:T(8,128)(2,1)S(1)} %half.1.sent_ref), channel_id=1, source_target_pairs={{0,1},{2,3},{4,5},{6,7},{1,0},{3,2},{5,4},{7,6},{16,17},{18,19},{2... | collective-permute-start | bytes 2064392 | tf_op jit(solution)/shard_map/ppermute | solution.py:46
  25.8 3.6 %collective-permute-start.5 = (bf16[192,256]{1,0:T(8,128)(2,1)S(1)}, bf16[192,256]{1,0:T(8,128)(2,1)S(1)}, u32[]{:S(2)}, u32[]{:S(2)}) collective-permute-start(bf16[192,256]{1,0:T(8,128)(2,1)S(1)} %get-tuple-element.44.refs_0_), channel_id=1, source_target_pairs={{0,6},{2,4},{4,2},{6,0},{1,7},{3,5},{5,3},{7,1},{16,22},{18,20},{2... | collective-permute-start | bytes 294920 | tf_op jit(solution)/shard_map/ppermute | solution.py:46
  29.4 2.9 %collective-permute-done.5.late_ref = bf16[192,256]{1,0:T(8,128)(2,1)S(1)} collective-permute-done((bf16[192,256]{1,0:T(8,128)(2,1)S(1)}, bf16[192,256]{1,0:T(8,128)(2,1)S(1)}, u32[]{:S(2)}, u32[]{:S(2)}) %collective-permute-start.5) | collective-permute-done | bytes 98336 | tf_op jit(solution)/shard_map/ppermute | solution.py:46
  32.3 0.9 %collective-permute-start.7 = (bf16[192,256]{1,0:T(8,128)(2,1)S(1)}, bf16[192,256]{1,0:T(8,128)(2,1)S(1)}, u32[]{:S(2)}, u32[]{:S(2)}) collective-permute-start(bf16[192,256]{1,0:T(8,128)(2,1)S(1)} %collective-permute-done.5.late_ref), channel_id=1, source_target_pairs={{0,1},{2,3},{4,5},{6,7},{1,0},{3,2},{5,4},{7,6},{16,17},{18,19},{2... | collective-permute-start | bytes 294920 | tf_op jit(solution)/shard_map/ppermute | solution.py:46
  33.2 3.7 %collective-permute-done.7.late_got_ref = bf16[192,256]{1,0:T(8,128)(2,1)S(1)} collective-permute-done((bf16[192,256]{1,0:T(8,128)(2,1)S(1)}, bf16[192,256]{1,0:T(8,128)(2,1)S(1)}, u32[]{:S(2)}, u32[]{:S(2)}) %collective-permute-start.7) | collective-permute-done | bytes 98336 | tf_op jit(solution)/shard_map/ppermute | solution.py:46
  36.9 0.0 collective-permute-done.6.got_ref.again_ref
  36.9 0.1 pack.1.own.mine_sent
  37.0 1.6 %collective-permute-start.8 = (bf16[8,192,256]{2,1,0:T(8,128)(2,1)S(1)}, bf16[8,192,256]{2,1,0:T(8,128)(2,1)S(1)}, u32[]{:S(2)}, u32[]{:S(2)}) collective-permute-start(bf16[8,192,256]{2,1,0:T(8,128)(2,1)S(1)} %pack.1.own.mine_sent), channel_id=1, source_target_pairs={{0,16},{2,18},{4,20},{6,22},{1,17},{3,19},{5,21},{7,23},{16,0},{18... | collective-permute-start | bytes 2359304 | tf_op jit(solution)/shard_map/ppermute | solution.py:46
  38.6 0.0 copy-done
  38.6 0.8 %plane.1 = (f32[192,256]{1,0:T(8,128)S(1)}, f32[1,256]{1,0:T(1,128)S(1)}, bf16[208,256]{1,0:T(8,128)(2,1)S(1)}, bf16[208,256]{1,0:T(8,128)(2,1)S(1)}, bf16[208,256]{1,0:T(8,128)(2,1)S(1)}) custom-call(s32[4]{0:T(128)S(1)} %pad_add_fusion.where, f32[4,192,256]{2,1,0:T(8,128)S(1)} %get-tuple-element.47.held, ...), custom_call_target="tpu_custom_call" | custom-call | tf_op jit(solution)/shard_map/plane/pallas_call | solution.py:429
  39.4 1.0 %collective-permute-start.9 = (bf16[208,256]{1,0:T(8,128)(2,1)S(1)}, bf16[208,256]{1,0:T(8,128)(2,1)S(1)}, u32[]{:S(2)}, u32[]{:S(2)}) collective-permute-start(bf16[208,256]{1,0:T(8,128)(2,1)S(1)} %get-tuple-element.48), channel_id=1, source_target_pairs={{0,2},{2,0},{4,6},{6,4},{1,3},{3,1},{5,7},{7,5},{16,18},{18,16},{2... | collective-permute-start | bytes 319496 | tf_op jit(solution)/shard_map/ppermute | solution.py:46
  40.4 3.1 %collective-permute-start.10 = (bf16[208,256]{1,0:T(8,128)(2,1)S(1)}, bf16[208,256]{1,0:T(8,128)(2,1)S(1)}, u32[]{:S(2)}, u32[]{:S(2)}) collective-permute-start(bf16[208,256]{1,0:T(8,128)(2,1)S(1)} %get-tuple-element.49), channel_id=1, source_target_pairs={{0,4},{2,6},{4,0},{6,2},{1,5},{3,7},{5,1},{7,3},{16,20},{18,22},{2... | collective-permute-start | bytes 319496 | tf_op jit(solution)/shard_map/ppermute | solution.py:46
  43.5 0.3 collective-permute-start.11
  43.8 0.3 collective-permute-done.9.refs_0_
  44.2 4.7 %collective-permute-done.10.refs_1_ = bf16[208,256]{1,0:T(8,128)(2,1)S(1)} collective-permute-done((bf16[208,256]{1,0:T(8,128)(2,1)S(1)}, bf16[208,256]{1,0:T(8,128)(2,1)S(1)}, u32[]{:S(2)}, u32[]{:S(2)}) %collective-permute-start.10) | collective-permute-done | bytes 106528 | tf_op jit(solution)/shard_map/ppermute | solution.py:46
  48.9 1.2 %collective-permute-done.11.refs_2_ = bf16[208,256]{1,0:T(8,128)(2,1)S(1)} collective-permute-done((bf16[208,256]{1,0:T(8,128)(2,1)S(1)}, bf16[208,256]{1,0:T(8,128)(2,1)S(1)}, u32[]{:S(2)}, u32[]{:S(2)}) %collective-permute-start.11) | collective-permute-done | bytes 106528 | tf_op jit(solution)/shard_map/ppermute | solution.py:46
  50.1 0.0 collective-permute-done.8.mine_got
  50.1 0.0 collective-permute-start.13
  50.1 0.5 collective-permute-start.12
  50.6 0.7 %last.1 = (f32[192,256]{1,0:T(8,128)}, f32[1,256]{1,0:T(1,128)S(1)}) custom-call(f32[192,256]{1,0:T(8,128)S(1)} %get-tuple-element.52.sums_ref, f32[1,256]{1,0:T(1,128)S(1)} %get-tuple-element.53.gains_ref, bf16[208,256]{1,0:T(8,128)(2,1)S(1)} %collective-permute-done.9.refs_0_, bf16[208,256]{1,0:T(8,128)(2,1)S(1)} %collective-permute-done.10.refs_1_, ...), custom_call_target="tpu_custom_call" | custom-call | tf_op jit(solution)/shard_map/last/pallas_call | solution.py:442
  51.4 1.0 %collective-permute-done.13.peer_got = bf16[8,192,256]{2,1,0:T(8,128)(2,1)S(1)} collective-permute-done((bf16[8,192,256]{2,1,0:T(8,128)(2,1)S(1)}, bf16[8,192,256]{2,1,0:T(8,128)(2,1)S(1)}, u32[]{:S(2)}, u32[]{:S(2)}) %collective-permute-start.13) | collective-permute-done | bytes 786464 | tf_op jit(solution)/shard_map/ppermute | solution.py:46
  52.4 0.1 collective-permute-start.14
  52.5 1.0 %collective-permute-done.14 = f32[1,256]{1,0:T(1,128)S(1)} collective-permute-done((f32[1,256]{1,0:T(1,128)S(1)}, f32[1,256]{1,0:T(1,128)S(1)}, u32[]{:S(2)}, u32[]{:S(2)}) %collective-permute-start.14) | collective-permute-done | bytes 1056 | tf_op jit(solution)/shard_map/ppermute | solution.py:46
  53.5 1.3 %collective-permute-start.15 = (f32[1,256]{1,0:T(1,128)S(1)}, f32[1,256]{1,0:T(1,128)S(1)}, u32[]{:S(2)}, u32[]{:S(2)}) collective-permute-start(f32[1,256]{1,0:T(1,128)S(1)} %add.17), channel_id=1, source_target_pairs={{0,16},{2,18},{4,20},{6,22},{1,17},{3,19},{5,21},{7,23},{16,0},{18... | collective-permute-start | bytes 3080 | tf_op jit(solution)/shard_map/ppermute | solution.py:46
  54.9 0.0 collective-permute-done.12.peer_sent
  54.9 5.0 %grad.1 = bf16[512,2048]{1,0:T(8,128)(2,1)} custom-call(s32[4]{0:T(128)S(1)} %pad_add_fusion.where, bf16[2,4,512,256]{3,2,1,0:T(8,128)(2,1)S(1)} %get-tuple-element.39.acts, f32[1,2048]{1,0:T(1,128)S(1)} %bitcast.10, bf16[512,768]{1,0:T(8,128)(2,1)S(1)} %get-tuple-element.40.grads, f32[512,128]{1,0:T(8,128)S(1)} %get-tuple-element.41.inverse, ...), custom_call_target="tpu_custom_call" | custom-call | tf_op jit(solution)/shard_map/grad/pallas_call | solution.py:455
  59.9 0.0 collective-permute-done.15
  59.9 0.6 add_multiply_fusion
  (1 shorter events, 0.0 us)
Async XLA Ops:
  0.6 5.6 %collective-permute-start = (bf16[512,2048]{1,0:T(8,128)(2,1)}, bf16[512,2048]{1,0:T(8,128)(2,1)S(1)}, u32[]{:S(2)}, u32[]{:S(2)}) collective-permute-start(bf16[512,2048]{1,0:T(8,128)(2,1)} %acts_ref.3), channel_id=1, source_target_pairs={{0,8},{2,10},{4,12},{6,14},{1,9},{3,11},{5,13},{7,15},{16,24},{18,... | collective-permute-start | bytes 6291464 | tf_op jit(solution)/shard_map/ppermute | solution.py:46
  4.4 1.8 %collective-permute-start.1 = (bf16[384,512]{1,0:T(8,128)(2,1)S(1)}, bf16[384,512]{1,0:T(8,128)(2,1)S(1)}, u32[]{:S(2)}, u32[]{:S(2)}) collective-permute-start(bf16[384,512]{1,0:T(8,128)(2,1)S(1)} %get-tuple-element.34), channel_id=1, source_target_pairs={{0,8},{2,10},{4,12},{6,14},{1,9},{3,11},{5,13},{7,15},{16,24},{18,... | collective-permute-start | bytes 1179656 | tf_op jit(solution)/shard_map/ppermute | solution.py:46
  10.3 12.8 %collective-permute-start.2 = (bf16[8,192,256]{2,1,0:T(8,128)(2,1)S(1)}, bf16[8,192,256]{2,1,0:T(8,128)(2,1)S(1)}, u32[]{:S(2)}, u32[]{:S(2)}) collective-permute-start(bf16[8,192,256]{2,1,0:T(8,128)(2,1)S(1)} %get-tuple-element.35), channel_id=1, source_target_pairs={{0,16},{2,18},{4,20},{6,22},{1,17},{3,19},{5,21},{7,23},{16,0},{18... | collective-permute-start | bytes 2359304 | tf_op jit(solution)/shard_map/ppermute | solution.py:46
  13.1 7.9 %collective-permute-start.4 = (bf16[192,256]{1,0:T(8,128)(2,1)S(1)}, bf16[192,256]{1,0:T(8,128)(2,1)S(1)}, u32[]{:S(2)}, u32[]{:S(2)}) collective-permute-start(bf16[192,256]{1,0:T(8,128)(2,1)S(1)} %get-tuple-element.44.refs_0_), channel_id=1, source_target_pairs={{0,4},{2,6},{4,0},{6,2},{1,5},{3,7},{5,1},{7,3},{16,20},{18,22},{2... | collective-permute-start | bytes 294920 | tf_op jit(solution)/shard_map/ppermute | solution.py:46
  15.7 5.5 %collective-permute-start.3 = (bf16[192,256]{1,0:T(8,128)(2,1)S(1)}, bf16[192,256]{1,0:T(8,128)(2,1)S(1)}, u32[]{:S(2)}, u32[]{:S(2)}) collective-permute-start(bf16[192,256]{1,0:T(8,128)(2,1)S(1)} %get-tuple-element.44.refs_0_), channel_id=1, source_target_pairs={{0,2},{2,0},{4,6},{6,4},{1,3},{3,1},{5,7},{7,5},{16,18},{18,16},{2... | collective-permute-start | bytes 294920 | tf_op jit(solution)/shard_map/ppermute | solution.py:46
  23.1 15.5 %copy-start = (f32[2048]{0:T(1024)S(1)}, f32[2048]{0:T(1024)}, u32[]{:S(2)}) copy-start(f32[2048]{0:T(1024)} %param.5) | copy-start | bytes 24580
  23.7 13.2 %collective-permute-start.6 = (bf16[7,192,256]{2,1,0:T(8,128)(2,1)S(1)}, bf16[7,192,256]{2,1,0:T(8,128)(2,1)S(1)}, u32[]{:S(2)}, u32[]{:S(2)}) collective-permute-start(bf16[7,192,256]{2,1,0:T(8,128)(2,1)S(1)} %half.1.sent_ref), channel_id=1, source_target_pairs={{0,1},{2,3},{4,5},{6,7},{1,0},{3,2},{5,4},{7,6},{16,17},{18,19},{2... | collective-permute-start | bytes 2064392 | tf_op jit(solution)/shard_map/ppermute | solution.py:46
  25.8 6.5 %collective-permute-start.5 = (bf16[192,256]{1,0:T(8,128)(2,1)S(1)}, bf16[192,256]{1,0:T(8,128)(2,1)S(1)}, u32[]{:S(2)}, u32[]{:S(2)}) collective-permute-start(bf16[192,256]{1,0:T(8,128)(2,1)S(1)} %get-tuple-element.44.refs_0_), channel_id=1, source_target_pairs={{0,6},{2,4},{4,2},{6,0},{1,7},{3,5},{5,3},{7,1},{16,22},{18,20},{2... | collective-permute-start | bytes 294920 | tf_op jit(solution)/shard_map/ppermute | solution.py:46
  32.3 4.6 %collective-permute-start.7 = (bf16[192,256]{1,0:T(8,128)(2,1)S(1)}, bf16[192,256]{1,0:T(8,128)(2,1)S(1)}, u32[]{:S(2)}, u32[]{:S(2)}) collective-permute-start(bf16[192,256]{1,0:T(8,128)(2,1)S(1)} %collective-permute-done.5.late_ref), channel_id=1, source_target_pairs={{0,1},{2,3},{4,5},{6,7},{1,0},{3,2},{5,4},{7,6},{16,17},{18,19},{2... | collective-permute-start | bytes 294920 | tf_op jit(solution)/shard_map/ppermute | solution.py:46
  37.0 13.1 %collective-permute-start.8 = (bf16[8,192,256]{2,1,0:T(8,128)(2,1)S(1)}, bf16[8,192,256]{2,1,0:T(8,128)(2,1)S(1)}, u32[]{:S(2)}, u32[]{:S(2)}) collective-permute-start(bf16[8,192,256]{2,1,0:T(8,128)(2,1)S(1)} %pack.1.own.mine_sent), channel_id=1, source_target_pairs={{0,16},{2,18},{4,20},{6,22},{1,17},{3,19},{5,21},{7,23},{16,0},{18... | collective-permute-start | bytes 2359304 | tf_op jit(solution)/shard_map/ppermute | solution.py:46
  39.4 4.8 %collective-permute-start.9 = (bf16[208,256]{1,0:T(8,128)(2,1)S(1)}, bf16[208,256]{1,0:T(8,128)(2,1)S(1)}, u32[]{:S(2)}, u32[]{:S(2)}) collective-permute-start(bf16[208,256]{1,0:T(8,128)(2,1)S(1)} %get-tuple-element.48), channel_id=1, source_target_pairs={{0,2},{2,0},{4,6},{6,4},{1,3},{3,1},{5,7},{7,5},{16,18},{18,16},{2... | collective-permute-start | bytes 319496 | tf_op jit(solution)/shard_map/ppermute | solution.py:46
  40.4 8.5 %collective-permute-start.10 = (bf16[208,256]{1,0:T(8,128)(2,1)S(1)}, bf16[208,256]{1,0:T(8,128)(2,1)S(1)}, u32[]{:S(2)}, u32[]{:S(2)}) collective-permute-start(bf16[208,256]{1,0:T(8,128)(2,1)S(1)} %get-tuple-element.49), channel_id=1, source_target_pairs={{0,4},{2,6},{4,0},{6,2},{1,5},{3,7},{5,1},{7,3},{16,20},{18,22},{2... | collective-permute-start | bytes 319496 | tf_op jit(solution)/shard_map/ppermute | solution.py:46
  43.5 6.6 %collective-permute-start.11 = (bf16[208,256]{1,0:T(8,128)(2,1)S(1)}, bf16[208,256]{1,0:T(8,128)(2,1)S(1)}, u32[]{:S(2)}, u32[]{:S(2)}) collective-permute-start(bf16[208,256]{1,0:T(8,128)(2,1)S(1)} %get-tuple-element.50), channel_id=1, source_target_pairs={{0,6},{2,4},{4,2},{6,0},{1,7},{3,5},{5,3},{7,1},{16,22},{18,20},{2... | collective-permute-start | bytes 319496 | tf_op jit(solution)/shard_map/ppermute | solution.py:46
  50.1 2.3 %collective-permute-start.13 = (bf16[8,192,256]{2,1,0:T(8,128)(2,1)S(1)}, bf16[8,192,256]{2,1,0:T(8,128)(2,1)S(1)}, u32[]{:S(2)}, u32[]{:S(2)}) collective-permute-start(bf16[8,192,256]{2,1,0:T(8,128)(2,1)S(1)} %collective-permute-done.8.mine_got), channel_id=1, source_target_pairs={{0,8},{2,10},{4,12},{6,14},{1,9},{3,11},{5,13},{7,15},{16,24},{18,... | collective-permute-start | bytes 2359304 | tf_op jit(solution)/shard_map/ppermute | solution.py:46
  50.1 4.8 %collective-permute-start.12 = (bf16[8,192,256]{2,1,0:T(8,128)(2,1)S(1)}, bf16[8,192,256]{2,1,0:T(8,128)(2,1)S(1)}, u32[]{:S(2)}, u32[]{:S(2)}) collective-permute-start(bf16[8,192,256]{2,1,0:T(8,128)(2,1)S(1)} %pack.1.own.mine_sent), channel_id=1, source_target_pairs={{0,8},{2,10},{4,12},{6,14},{1,9},{3,11},{5,13},{7,15},{16,24},{18,... | collective-permute-start | bytes 2359304 | tf_op jit(solution)/shard_map/ppermute | solution.py:46
  52.4 1.1 %collective-permute-start.14 = (f32[1,256]{1,0:T(1,128)S(1)}, f32[1,256]{1,0:T(1,128)S(1)}, u32[]{:S(2)}, u32[]{:S(2)}) collective-permute-start(f32[1,256]{1,0:T(1,128)S(1)} %get-tuple-element.60), channel_id=1, source_target_pairs={{0,8},{2,10},{4,12},{6,14},{1,9},{3,11},{5,13},{7,15},{16,24},{18,... | collective-permute-start | bytes 3080 | tf_op jit(solution)/shard_map/ppermute | solution.py:46
  53.5 6.3 %collective-permute-start.15 = (f32[1,256]{1,0:T(1,128)S(1)}, f32[1,256]{1,0:T(1,128)S(1)}, u32[]{:S(2)}, u32[]{:S(2)}) collective-permute-start(f32[1,256]{1,0:T(1,128)S(1)} %add.17), channel_id=1, source_target_pairs={{0,16},{2,18},{4,20},{6,22},{1,17},{3,19},{5,21},{7,23},{16,0},{18... | collective-permute-start | bytes 3080 | tf_op jit(solution)/shard_map/ppermute | solution.py:46

commit v4 on v3

--- a/solution.py
+++ b/solution.py
@@ -14,6 +14,7 @@
 MIB = 1024 * 1024
 TILE = 16
 CHUNKS = 4
+EARLY = 1
 
 
 def params(limit):
@@ -149,21 +150,16 @@
             out_ref[to_z] = totals[pl.ds(slot_of(plan, where, first, second, to_z), 1)][0]
 
 
-def half_kernel(plan, where, kept, got_ref, *refs):
-    pieces, sent_ref = refs[:-1], refs[-1]
+def half_kernel(plan, where, kept, got_ref, sent_ref):
     _, second = first_and_second(where)
-    for step, piece in enumerate(pieces):
-        sent_ref[plan.depth + step] = piece[...]
     for to_z in range(plan.depth):
         block = kept[to_z] + got_ref[pl.ds((1 - second) * plan.depth + to_z, 1)][0].astype(F32)
         sent_ref[to_z] = block.astype(BF16)
 
 
-def pack_kernel(plan, sent_ref, late_ref, got_ref, late_got_ref, out_ref):
-    depth = plan.depth
-    for part, (early, late) in enumerate(((sent_ref, late_ref), (got_ref, late_got_ref))):
-        out_ref[part * depth : (part + 1) * depth - 1] = early[depth:]
-        out_ref[(part + 1) * depth - 1] = late[...]
+def pack_kernel(plan, *refs):
+    for number, ref in enumerate(refs[:-1]):
+        refs[-1][number] = ref[...]
 
 
 def plane_kernel(plan, where, held, got_ref, own, again_ref, gain_ref, sums_ref, gains_ref, *sent_refs):
@@ -234,7 +230,8 @@
 
 def place_weight(plan, where, pieces, from_core, second, weight):
     depth = plan.depth
-    rows = pieces.shape[1]
+    blocks = [array.at[number] for array in pieces for number in range(array.shape[0])]
+    rows = blocks[0].shape[0]
     for part in range(2):
         if second:
             flip = from_core if part == 0 else 1
@@ -245,21 +242,21 @@
         grp = (where[1] ^ far_y) * 2 + from_core
         here = pl.ds(pl.multiple_of(grp * rows, rows), rows)
         for step in range(depth):
-            weight[pl.ds(flip * depth + step, 1), here] = pieces[part * depth + step][None]
+            weight[pl.ds(flip * depth + step, 1), here] = blocks[part * depth + step][...][None]
 
 
 def grad_kernel(
-    plan, where, acts, gain_ref, grads, inverse, mine_sent, mine_got, peer_sent, peer_got,
+    plan, where, acts, gain_ref, grads, inverse, mine_sent, mine_got, peer_first, peer_rest, peer_got,
     out_ref, weight, grad_scaled, mean_ref, out, ends,
 ):
     core = where[0]
     depth = plan.depth
     tokens, cols = acts.shape[2:]
     model = cols * plan.subs
-    place_weight(plan, where, mine_sent, core, False, weight)
-    place_weight(plan, where, peer_sent, 1 - core, False, weight)
-    place_weight(plan, where, mine_got, core, True, weight)
-    place_weight(plan, where, peer_got, 1 - core, True, weight)
+    place_weight(plan, where, [mine_sent], core, False, weight)
+    place_weight(plan, where, [peer_first, peer_rest], 1 - core, False, weight)
+    place_weight(plan, where, [mine_got], core, True, weight)
+    place_weight(plan, where, [peer_got], 1 - core, True, weight)
     blocks = [(flip, step) for flip in range(2) for step in range(depth)]
     for flip, step in blocks:
         number = flip * depth + step
@@ -399,33 +396,34 @@
         name="load",
     )(where, acts_hbm, grads_hbm)
 
-    pieces = [piece] + [plan.send(piece, to_z(step)) for step in range(1, depth - 1)]
-    got, pieces, acts, grads = lax.optimization_barrier((got, pieces, acts, grads))
-
-    both = (2 * depth, rows, cols)
+    planes = [plan.send(piece, to_z(step)) for step in range(1, depth)]
+    got, planes[:-1], acts, grads, inverse = lax.optimization_barrier(
+        (got, planes[:-1], acts, grads, inverse)
+    )
+
     sent = pl.pallas_call(
         functools.partial(half_kernel, plan),
-        out_shape=pltpu.VMEM((2 * depth - 1, rows, cols), BF16),
-        in_specs=[SMEM] + [VMEM] * (1 + depth),
+        out_shape=pltpu.VMEM((depth, rows, cols), BF16),
+        in_specs=[SMEM, VMEM, VMEM],
         out_specs=VMEM,
         compiler_params=params(2),
         cost_estimate=cost(0, 2 * MIB),
         name="half",
-    )(where, kept, got, *pieces)
+    )(where, kept, got)
     again = plan.send(sent, x_then)
-    late = plan.send(pieces[0], to_z(depth - 1))
-    late_again = plan.send(late, x_then)
-    mine_sent = pl.pallas_call(
+
+    own = pl.pallas_call(
         functools.partial(pack_kernel, plan),
-        out_shape=pltpu.VMEM(both, BF16),
-        in_specs=[VMEM] * 4,
+        out_shape=pltpu.VMEM((depth, rows, cols), BF16),
+        in_specs=[VMEM] * depth,
         out_specs=VMEM,
         compiler_params=params(1),
-        cost_estimate=cost(0, 2 * MIB),
+        cost_estimate=cost(0, MIB),
         name="pack",
-    )(sent, late, again, late_again)
-    mine_got = plan.send(mine_sent, y_then)
-    peer_sent = plan.send(mine_sent, to_core)
+    )(piece, *planes)
+    own, _ = lax.optimization_barrier((own, sent))
+    over = plan.send(own, x_then)
+    mine_sent = jnp.concatenate([own, over])
     sums, gains, *sents = pl.pallas_call(
         functools.partial(plane_kernel, plan),
         out_shape=[pltpu.VMEM((rows, cols), F32), pltpu.VMEM((1, cols), F32)]
@@ -435,10 +433,9 @@
         compiler_params=params(3),
         cost_estimate=cost(0, 2 * MIB),
         name="plane",
-    )(where, held, got, mine_sent, again, gain)
+    )(where, held, got, own, again, gain)
     gots = [plan.send(array, to_z(step + 1)) for step, array in enumerate(sents)]
-    mine_got, gots = lax.optimization_barrier((mine_got, gots))
-    peer_got = plan.send(mine_got, to_core)
+    mine_got = plan.send(mine_sent, y_then)
     weight_grads, gains = pl.pallas_call(
         functools.partial(last_kernel, plan),
         out_shape=(shape((rows, cols), F32), pltpu.VMEM((1, cols), F32)),
@@ -448,14 +445,18 @@
         cost_estimate=cost(0, MIB),
         name="last",
     )(sums, gains, *gots)
-    gains, peer_got = lax.optimization_barrier((gains, peer_got))
     gains = gains + plan.send(gains, to_core)
-    gains = gains + plan.send(gains, to_y)
+    peer_first = plan.send(mine_sent[:EARLY], to_core)
+    rest, gains = lax.optimization_barrier((mine_sent[EARLY:], gains))
+    peer_rest = plan.send(rest, to_core)
+    peer_gains = plan.send(gains, to_y)
+    mine_got, peer_rest, peer_gains = lax.optimization_barrier((mine_got, peer_rest, peer_gains))
+    peer_got = plan.send(mine_got, to_core)
 
     input_grads = pl.pallas_call(
         functools.partial(grad_kernel, plan),
         out_shape=shape((tokens, model), BF16),
-        in_specs=[SMEM] + [VMEM] * 8,
+        in_specs=[SMEM] + [VMEM] * 9,
         out_specs=HBM,
         scratch_shapes=[
             pltpu.VMEM((2 * depth, key_width, cols), BF16),
@@ -467,8 +468,8 @@
         compiler_params=params(12),
         cost_estimate=cost(2 * tokens * model * key_width, 8 * MIB),
         name="grad",
-    )(where, acts, gain, grads, inverse, mine_sent, mine_got, peer_sent, peer_got)
-    return input_grads, weight_grads.T, gains.reshape(cols) / plan.groups
+    )(where, acts, gain, grads, inverse, mine_sent, mine_got, peer_first, peer_rest, peer_got)
+    return input_grads, weight_grads.T, (gains + peer_gains).reshape(cols) / plan.groups
 
 
 def by_collectives(activations, norm_gain, key_weight, key_grads):

time: 60.7 us -> 57.6 us (0.949)
  starting transfers between devices: 22.3 us -> 18.9 us
    ppermute x16 -> x17, starting transfers between devices: 22.3 us -> 18.9 us  [send(): return lax.ppermute(array, AXES, self.pairs(move))]
    ppermute x16 -> x17, waiting for transfers between devices: 19.8 us -> 20.1 us  [send(): return lax.ppermute(array, AXES, self.pairs(move))]
  transfers between devices with their start and end apart: 16 -> 17, of which waited for: 11 -> 8; matrix products, arithmetic and copies ran while one was open for 0% -> 1% of each run, Pallas kernels for 20% -> 14%
where the time goes in v4:
time: 57.6 us; the launch traced here: 57.4 us
  waiting for transfers between devices  20.1 us (35%)
  starting transfers between devices  18.9 us (33%)
  Pallas kernels  17 us (30%)
  between operations  0.72 us (1%)
  other arithmetic  0.64 us (1%)
    ppermute x17, waiting for transfers between devices, send(): return lax.ppermute(array, AXES, self.pairs(move))  20.1 us
    ppermute x17, starting transfers between devices, send(): return lax.ppermute(array, AXES, self.pairs(move))  18.9 us
    pallas_call x1, Pallas kernels, by_permutes(): pl.pallas_call(functools.partial(grad_kernel, plan), out_shape=shape((tok...  5.01 us
    pallas_call x1, Pallas kernels, by_permutes(): pl.pallas_call(functools.partial(term_kernel, plan), out_shape=(pltpu.VME...  4.11 us
    pallas_call x1, Pallas kernels, by_permutes(): pl.pallas_call(functools.partial(mine_kernel, plan), out_shape=(pltpu.VME...  3.18 us
    pallas_call x1, Pallas kernels, by_permutes(): pl.pallas_call(functools.partial(load_kernel, plan), out_shape=(pltpu.VME...  2.56 us
  transfers between devices with their start and end apart: 17, of which 8 were waited for; matrix products, arithmetic and copies ran while one was open for 1% of the time, Pallas kernels for 14%

profile of v4, /device:TPU:0, one launch (start us, length us, event | category | flops | bytes accessed | tf_op | source)
XLA Modules:
  0.0 57.4 jit_solution(10883324368934604025)
XLA Ops:
  0.6 0.5 collective-permute-start
  1.1 0.1 pad_add_fusion.where
  1.2 3.2 %mine.1 = (bf16[512,2048]{1,0:T(8,128)(2,1)S(1)}, bf16[384,512]{1,0:T(8,128)(2,1)S(1)}, bf16[384,512]{1,0:T(8,128)(2,1)S(1)}, bf16[192,256]{1,0:T(8,128)(2,1)S(1)}) custom-call(s32[4]{0:T(128)S(1)} %pad_add_fusion.where, bf16[512,2048]{1,0:T(8,128)(2,1)} %acts_ref.3, f32[1,2048]{1,0:T(1,128)} %bitcast.7, bf16[512,768]{1,0:T(8,128)(2,1)} %grads_ref.3, ...), custom_call_target="tpu_custom_call" | custom-call | tf_op jit(solution)/shard_map/mine/pallas_call | solution.py:340
  4.4 0.2 collective-permute-start.1
  4.6 1.6 %collective-permute-done.1.theirs = bf16[384,512]{1,0:T(8,128)(2,1)S(1)} collective-permute-done((bf16[384,512]{1,0:T(8,128)(2,1)S(1)}, bf16[384,512]{1,0:T(8,128)(2,1)S(1)}, u32[]{:S(2)}, u32[]{:S(2)}) %collective-permute-start.1) | collective-permute-done | bytes 393248 | tf_op jit(solution)/shard_map/ppermute | solution.py:47
  6.2 0.0 collective-permute-done.acts
  6.2 4.1 %term.1 = (bf16[8,192,256]{2,1,0:T(8,128)(2,1)S(1)}, f32[4,192,256]{2,1,0:T(8,128)S(1)}, f32[4,192,256]{2,1,0:T(8,128)S(1)}) custom-call(s32[4]{0:T(128)S(1)} %pad_add_fusion.where, bf16[512,2048]{1,0:T(8,128)(2,1)S(1)} %collective-permute-done.acts, f32[1,2048]{1,0:T(1,128)} %bitcast.8, bf16[512,2048]{1,0:T(8,128)(2,1)S(1)} %get-tuple-element.32.scaled, ...), custom_call_target="tpu_custom_call" | custom-call | tf_op jit(solution)/shard_map/term/pallas_call | solution.py:363
  10.3 2.8 %collective-permute-start.2 = (bf16[8,192,256]{2,1,0:T(8,128)(2,1)S(1)}, bf16[8,192,256]{2,1,0:T(8,128)(2,1)S(1)}, u32[]{:S(2)}, u32[]{:S(2)}) collective-permute-start(bf16[8,192,256]{2,1,0:T(8,128)(2,1)S(1)} %get-tuple-element.35), channel_id=1, source_target_pairs={{0,16},{2,18},{4,20},{6,22},{1,17},{3,19},{5,21},{7,23},{16,0},{18... | collective-permute-start | bytes 2359304 | tf_op jit(solution)/shard_map/ppermute | solution.py:47
  13.1 2.6 %collective-permute-start.4 = (bf16[192,256]{1,0:T(8,128)(2,1)S(1)}, bf16[192,256]{1,0:T(8,128)(2,1)S(1)}, u32[]{:S(2)}, u32[]{:S(2)}) collective-permute-start(bf16[192,256]{1,0:T(8,128)(2,1)S(1)} %get-tuple-element.36.refs_0_), channel_id=1, source_target_pairs={{0,4},{2,6},{4,0},{6,2},{1,5},{3,7},{5,1},{7,3},{16,20},{18,22},{2... | collective-permute-start | bytes 294920 | tf_op jit(solution)/shard_map/ppermute | solution.py:47
  15.7 1.6 %collective-permute-start.3 = (bf16[192,256]{1,0:T(8,128)(2,1)S(1)}, bf16[192,256]{1,0:T(8,128)(2,1)S(1)}, u32[]{:S(2)}, u32[]{:S(2)}) collective-permute-start(bf16[192,256]{1,0:T(8,128)(2,1)S(1)} %get-tuple-element.36.refs_0_), channel_id=1, source_target_pairs={{0,2},{2,0},{4,6},{6,4},{1,3},{3,1},{5,7},{7,5},{16,18},{18,16},{2... | collective-permute-start | bytes 294920 | tf_op jit(solution)/shard_map/ppermute | solution.py:47
  17.3 0.2 collective-permute-start.5
  17.5 2.6 %load.1 = (bf16[2,4,512,256]{3,2,1,0:T(8,128)(2,1)S(1)}, bf16[512,768]{1,0:T(8,128)(2,1)S(1)}, f32[512,128]{1,0:T(8,128)S(1)}) custom-call(s32[4]{0:T(128)S(1)} %pad_add_fusion.where, bf16[512,2048]{1,0:T(8,128)(2,1)} %acts_ref.3, bf16[512,768]{1,0:T(8,128)(2,1)} %grads_ref.3), custom_call_target="tpu_custom_call" | custom-call | tf_op jit(solution)/shard_map/load/pallas_call | solution.py:384
  20.1 0.0 copy-start
  20.1 2.2 %collective-permute-done.4.refs_2_ = bf16[192,256]{1,0:T(8,128)(2,1)S(1)} collective-permute-done((bf16[192,256]{1,0:T(8,128)(2,1)S(1)}, bf16[192,256]{1,0:T(8,128)(2,1)S(1)}, u32[]{:S(2)}, u32[]{:S(2)}) %collective-permute-start.4) | collective-permute-done | bytes 98336 | tf_op jit(solution)/shard_map/ppermute | solution.py:47
  22.3 0.0 collective-permute-done.3.refs_1_
  22.3 0.8 %collective-permute-done.2.got_ref = bf16[8,192,256]{2,1,0:T(8,128)(2,1)S(1)} collective-permute-done((bf16[8,192,256]{2,1,0:T(8,128)(2,1)S(1)}, bf16[8,192,256]{2,1,0:T(8,128)(2,1)S(1)}, u32[]{:S(2)}, u32[]{:S(2)}) %collective-permute-start.2) | collective-permute-done | bytes 786464 | tf_op jit(solution)/shard_map/ppermute | solution.py:47
  23.1 0.6 %half.1 = bf16[4,192,256]{2,1,0:T(8,128)(2,1)S(1)} custom-call(s32[4]{0:T(128)S(1)} %pad_add_fusion.where, f32[4,192,256]{2,1,0:T(8,128)S(1)} %get-tuple-element.45.kept, bf16[8,192,256]{2,1,0:T(8,128)(2,1)S(1)} %collective-permute-done.2.got_ref), custom_call_target="tpu_custom_call" | custom-call | tf_op jit(solution)/shard_map/half/pallas_call | solution.py:404
  23.7 2.0 %collective-permute-start.8 = (bf16[4,192,256]{2,1,0:T(8,128)(2,1)S(1)}, bf16[4,192,256]{2,1,0:T(8,128)(2,1)S(1)}, u32[]{:S(2)}, u32[]{:S(2)}) collective-permute-start(bf16[4,192,256]{2,1,0:T(8,128)(2,1)S(1)} %half.1), channel_id=1, source_target_pairs={{0,1},{2,3},{4,5},{6,7},{1,0},{3,2},{5,4},{7,6},{16,17},{18,19},{2... | collective-permute-start | bytes 1179656 | tf_op jit(solution)/shard_map/ppermute | solution.py:47
  25.8 0.0 collective-permute-done.5.refs_3_
  25.8 0.1 collective-permute-start.6
  25.9 5.6 %collective-permute-done.8.again_ref = bf16[4,192,256]{2,1,0:T(8,128)(2,1)S(1)} collective-permute-done((bf16[4,192,256]{2,1,0:T(8,128)(2,1)S(1)}, bf16[4,192,256]{2,1,0:T(8,128)(2,1)S(1)}, u32[]{:S(2)}, u32[]{:S(2)}) %collective-permute-start.8) | collective-permute-done | bytes 393248 | tf_op jit(solution)/shard_map/ppermute | solution.py:47
  31.6 0.0 copy-done
  31.6 0.8 %plane.1 = (f32[192,256]{1,0:T(8,128)S(1)}, f32[1,256]{1,0:T(1,128)S(1)}, bf16[208,256]{1,0:T(8,128)(2,1)S(1)}, bf16[208,256]{1,0:T(8,128)(2,1)S(1)}, bf16[208,256]{1,0:T(8,128)(2,1)S(1)}) custom-call(s32[4]{0:T(128)S(1)} %pad_add_fusion.where, f32[4,192,256]{2,1,0:T(8,128)S(1)} %get-tuple-element.48.held, ...), custom_call_target="tpu_custom_call" | custom-call | tf_op jit(solution)/shard_map/plane/pallas_call | solution.py:427
  32.3 2.1 %collective-permute-start.9 = (bf16[208,256]{1,0:T(8,128)(2,1)S(1)}, bf16[208,256]{1,0:T(8,128)(2,1)S(1)}, u32[]{:S(2)}, u32[]{:S(2)}) collective-permute-start(bf16[208,256]{1,0:T(8,128)(2,1)S(1)} %get-tuple-element.51), channel_id=1, source_target_pairs={{0,2},{2,0},{4,6},{6,4},{1,3},{3,1},{5,7},{7,5},{16,18},{18,16},{2... | collective-permute-start | bytes 319496 | tf_op jit(solution)/shard_map/ppermute | solution.py:47
  34.5 2.6 %collective-permute-start.10 = (bf16[208,256]{1,0:T(8,128)(2,1)S(1)}, bf16[208,256]{1,0:T(8,128)(2,1)S(1)}, u32[]{:S(2)}, u32[]{:S(2)}) collective-permute-start(bf16[208,256]{1,0:T(8,128)(2,1)S(1)} %get-tuple-element.52), channel_id=1, source_target_pairs={{0,4},{2,6},{4,0},{6,2},{1,5},{3,7},{5,1},{7,3},{16,20},{18,22},{2... | collective-permute-start | bytes 319496 | tf_op jit(solution)/shard_map/ppermute | solution.py:47
  37.1 0.0 collective-permute-start.11
  37.1 0.0 collective-permute-done.6
  37.1 1.8 %collective-permute-start.7 = (bf16[8,192,256]{2,1,0:T(8,128)(2,1)S(1)}, bf16[8,192,256]{2,1,0:T(8,128)(2,1)S(1)}, u32[]{:S(2)}, u32[]{:S(2)}) collective-permute-start(bf16[8,192,256]{2,1,0:T(8,128)(2,1)S(1)} %constant_dynamic-update-slice_fusion.mine_sent), channel_id=1, source_target_pairs={{0,16},{2,18},{4,20},{6,22},{1,17},{3,19},{5,21},{7,23},{16,0},{18... | collective-permute-start | bytes 2359304 | tf_op jit(solution)/shard_map/ppermute | solution.py:47
  38.9 0.0 collective-permute-done.9.refs_0_
  38.9 5.4 %collective-permute-done.10.refs_1_ = bf16[208,256]{1,0:T(8,128)(2,1)S(1)} collective-permute-done((bf16[208,256]{1,0:T(8,128)(2,1)S(1)}, bf16[208,256]{1,0:T(8,128)(2,1)S(1)}, u32[]{:S(2)}, u32[]{:S(2)}) %collective-permute-start.10) | collective-permute-done | bytes 106528 | tf_op jit(solution)/shard_map/ppermute | solution.py:47
  44.3 0.0 collective-permute-done.11.refs_2_
  44.3 0.7 %last.1 = (f32[192,256]{1,0:T(8,128)}, f32[1,256]{1,0:T(1,128)S(1)}) custom-call(f32[192,256]{1,0:T(8,128)S(1)} %get-tuple-element.49.sums_ref, f32[1,256]{1,0:T(1,128)S(1)} %get-tuple-element.50.gains_ref, bf16[208,256]{1,0:T(8,128)(2,1)S(1)} %collective-permute-done.9.refs_0_, bf16[208,256]{1,0:T(8,128)(2,1)S(1)} %collective-permute-done.10.refs_1_, ...), custom_call_target="tpu_custom_call" | custom-call | tf_op jit(solution)/shard_map/last/pallas_call | solution.py:439
  45.1 0.0 collective-permute-start.12
  45.1 1.1 %collective-permute-done.12 = f32[1,256]{1,0:T(1,128)S(1)} collective-permute-done((f32[1,256]{1,0:T(1,128)S(1)}, f32[1,256]{1,0:T(1,128)S(1)}, u32[]{:S(2)}, u32[]{:S(2)}) %collective-permute-start.12) | collective-permute-done | bytes 1056 | tf_op jit(solution)/shard_map/ppermute | solution.py:47
  46.2 0.2 collective-permute-start.13
  46.4 1.5 %collective-permute-start.14 = (f32[1,256]{1,0:T(1,128)S(1)}, f32[1,256]{1,0:T(1,128)S(1)}, u32[]{:S(2)}, u32[]{:S(2)}) collective-permute-start(f32[1,256]{1,0:T(1,128)S(1)} %add.17), channel_id=1, source_target_pairs={{0,16},{2,18},{4,20},{6,22},{1,17},{3,19},{5,21},{7,23},{16,0},{18... | collective-permute-start | bytes 3080 | tf_op jit(solution)/shard_map/ppermute | solution.py:47
  47.9 2.0 %collective-permute-done.14 = f32[1,256]{1,0:T(1,128)S(1)} collective-permute-done((f32[1,256]{1,0:T(1,128)S(1)}, f32[1,256]{1,0:T(1,128)S(1)}, u32[]{:S(2)}, u32[]{:S(2)}) %collective-permute-start.14) | collective-permute-done | bytes 1056 | tf_op jit(solution)/shard_map/ppermute | solution.py:47
  50.0 0.0 collective-permute-done.7.mine_got
  50.0 0.0 collective-permute-done.13.peer_rest
  50.0 0.0 collective-permute-start.16
  50.0 0.6 collective-permute-start.15
  50.6 0.6 add_multiply_fusion
  51.1 1.3 %collective-permute-done.15.peer_first = bf16[1,192,256]{2,1,0:T(8,128)(2,1)S(1)} collective-permute-done((bf16[1,192,256]{2,1,0:T(8,128)(2,1)S(1)}, bf16[1,192,256]{2,1,0:T(8,128)(2,1)S(1)}, u32[]{:S(2)}, u32[]{:S(2)}) %collective-permute-start.15) | collective-permute-done | bytes 98336 | tf_op jit(solution)/shard_map/ppermute | solution.py:47
  52.4 0.0 collective-permute-done.16.peer_got
  52.4 5.0 %grad.1 = bf16[512,2048]{1,0:T(8,128)(2,1)} custom-call(s32[4]{0:T(128)S(1)} %pad_add_fusion.where, bf16[2,4,512,256]{3,2,1,0:T(8,128)(2,1)S(1)} %get-tuple-element.40.acts, f32[1,2048]{1,0:T(1,128)S(1)} %bitcast.10, bf16[512,768]{1,0:T(8,128)(2,1)S(1)} %get-tuple-element.41.grads, f32[512,128]{1,0:T(8,128)S(1)} %get-tuple-element.42.inverse, ...), custom_call_target="tpu_custom_call" | custom-call | tf_op jit(solution)/shard_map/grad/pallas_call | solution.py:456
  (6 shorter events, 0.1 us)
Async XLA Ops:
  0.6 5.6 %collective-permute-start = (bf16[512,2048]{1,0:T(8,128)(2,1)}, bf16[512,2048]{1,0:T(8,128)(2,1)S(1)}, u32[]{:S(2)}, u32[]{:S(2)}) collective-permute-start(bf16[512,2048]{1,0:T(8,128)(2,1)} %acts_ref.3), channel_id=1, source_target_pairs={{0,8},{2,10},{4,12},{6,14},{1,9},{3,11},{5,13},{7,15},{16,24},{18,... | collective-permute-start | bytes 6291464 | tf_op jit(solution)/shard_map/ppermute | solution.py:47
  4.4 1.8 %collective-permute-start.1 = (bf16[384,512]{1,0:T(8,128)(2,1)S(1)}, bf16[384,512]{1,0:T(8,128)(2,1)S(1)}, u32[]{:S(2)}, u32[]{:S(2)}) collective-permute-start(bf16[384,512]{1,0:T(8,128)(2,1)S(1)} %get-tuple-element.34), channel_id=1, source_target_pairs={{0,8},{2,10},{4,12},{6,14},{1,9},{3,11},{5,13},{7,15},{16,24},{18,... | collective-permute-start | bytes 1179656 | tf_op jit(solution)/shard_map/ppermute | solution.py:47
  10.3 12.8 %collective-permute-start.2 = (bf16[8,192,256]{2,1,0:T(8,128)(2,1)S(1)}, bf16[8,192,256]{2,1,0:T(8,128)(2,1)S(1)}, u32[]{:S(2)}, u32[]{:S(2)}) collective-permute-start(bf16[8,192,256]{2,1,0:T(8,128)(2,1)S(1)} %get-tuple-element.35), channel_id=1, source_target_pairs={{0,16},{2,18},{4,20},{6,22},{1,17},{3,19},{5,21},{7,23},{16,0},{18... | collective-permute-start | bytes 2359304 | tf_op jit(solution)/shard_map/ppermute | solution.py:47
  13.1 9.2 %collective-permute-start.4 = (bf16[192,256]{1,0:T(8,128)(2,1)S(1)}, bf16[192,256]{1,0:T(8,128)(2,1)S(1)}, u32[]{:S(2)}, u32[]{:S(2)}) collective-permute-start(bf16[192,256]{1,0:T(8,128)(2,1)S(1)} %get-tuple-element.36.refs_0_), channel_id=1, source_target_pairs={{0,4},{2,6},{4,0},{6,2},{1,5},{3,7},{5,1},{7,3},{16,20},{18,22},{2... | collective-permute-start | bytes 294920 | tf_op jit(solution)/shard_map/ppermute | solution.py:47
  15.7 6.6 %collective-permute-start.3 = (bf16[192,256]{1,0:T(8,128)(2,1)S(1)}, bf16[192,256]{1,0:T(8,128)(2,1)S(1)}, u32[]{:S(2)}, u32[]{:S(2)}) collective-permute-start(bf16[192,256]{1,0:T(8,128)(2,1)S(1)} %get-tuple-element.36.refs_0_), channel_id=1, source_target_pairs={{0,2},{2,0},{4,6},{6,4},{1,3},{3,1},{5,7},{7,5},{16,18},{18,16},{2... | collective-permute-start | bytes 294920 | tf_op jit(solution)/shard_map/ppermute | solution.py:47
  17.3 8.5 %collective-permute-start.5 = (bf16[192,256]{1,0:T(8,128)(2,1)S(1)}, bf16[192,256]{1,0:T(8,128)(2,1)S(1)}, u32[]{:S(2)}, u32[]{:S(2)}) collective-permute-start(bf16[192,256]{1,0:T(8,128)(2,1)S(1)} %get-tuple-element.36.refs_0_), channel_id=1, source_target_pairs={{0,6},{2,4},{4,2},{6,0},{1,7},{3,5},{5,3},{7,1},{16,22},{18,20},{2... | collective-permute-start | bytes 294920 | tf_op jit(solution)/shard_map/ppermute | solution.py:47
  20.1 11.5 %copy-start = (f32[2048]{0:T(1024)S(1)}, f32[2048]{0:T(1024)}, u32[]{:S(2)}) copy-start(f32[2048]{0:T(1024)} %param.5) | copy-start | bytes 24580
  23.7 7.8 %collective-permute-start.8 = (bf16[4,192,256]{2,1,0:T(8,128)(2,1)S(1)}, bf16[4,192,256]{2,1,0:T(8,128)(2,1)S(1)}, u32[]{:S(2)}, u32[]{:S(2)}) collective-permute-start(bf16[4,192,256]{2,1,0:T(8,128)(2,1)S(1)} %half.1), channel_id=1, source_target_pairs={{0,1},{2,3},{4,5},{6,7},{1,0},{3,2},{5,4},{7,6},{16,17},{18,19},{2... | collective-permute-start | bytes 1179656 | tf_op jit(solution)/shard_map/ppermute | solution.py:47
  25.8 11.3 %collective-permute-start.6 = (bf16[4,192,256]{2,1,0:T(8,128)(2,1)S(1)}, bf16[4,192,256]{2,1,0:T(8,128)(2,1)S(1)}, u32[]{:S(2)}, u32[]{:S(2)}) collective-permute-start(bf16[4,192,256]{2,1,0:T(8,128)(2,1)S(1)} %pack.1.own), channel_id=1, source_target_pairs={{0,1},{2,3},{4,5},{6,7},{1,0},{3,2},{5,4},{7,6},{16,17},{18,19},{2... | collective-permute-start | bytes 1179656 | tf_op jit(solution)/shard_map/ppermute | solution.py:47
  32.3 6.6 %collective-permute-start.9 = (bf16[208,256]{1,0:T(8,128)(2,1)S(1)}, bf16[208,256]{1,0:T(8,128)(2,1)S(1)}, u32[]{:S(2)}, u32[]{:S(2)}) collective-permute-start(bf16[208,256]{1,0:T(8,128)(2,1)S(1)} %get-tuple-element.51), channel_id=1, source_target_pairs={{0,2},{2,0},{4,6},{6,4},{1,3},{3,1},{5,7},{7,5},{16,18},{18,16},{2... | collective-permute-start | bytes 319496 | tf_op jit(solution)/shard_map/ppermute | solution.py:47
  34.5 9.9 %collective-permute-start.10 = (bf16[208,256]{1,0:T(8,128)(2,1)S(1)}, bf16[208,256]{1,0:T(8,128)(2,1)S(1)}, u32[]{:S(2)}, u32[]{:S(2)}) collective-permute-start(bf16[208,256]{1,0:T(8,128)(2,1)S(1)} %get-tuple-element.52), channel_id=1, source_target_pairs={{0,4},{2,6},{4,0},{6,2},{1,5},{3,7},{5,1},{7,3},{16,20},{18,22},{2... | collective-permute-start | bytes 319496 | tf_op jit(solution)/shard_map/ppermute | solution.py:47
  37.1 7.3 %collective-permute-start.11 = (bf16[208,256]{1,0:T(8,128)(2,1)S(1)}, bf16[208,256]{1,0:T(8,128)(2,1)S(1)}, u32[]{:S(2)}, u32[]{:S(2)}) collective-permute-start(bf16[208,256]{1,0:T(8,128)(2,1)S(1)} %get-tuple-element.53), channel_id=1, source_target_pairs={{0,6},{2,4},{4,2},{6,0},{1,7},{3,5},{5,3},{7,1},{16,22},{18,20},{2... | collective-permute-start | bytes 319496 | tf_op jit(solution)/shard_map/ppermute | solution.py:47
  37.1 12.9 %collective-permute-start.7 = (bf16[8,192,256]{2,1,0:T(8,128)(2,1)S(1)}, bf16[8,192,256]{2,1,0:T(8,128)(2,1)S(1)}, u32[]{:S(2)}, u32[]{:S(2)}) collective-permute-start(bf16[8,192,256]{2,1,0:T(8,128)(2,1)S(1)} %constant_dynamic-update-slice_fusion.mine_sent), channel_id=1, source_target_pairs={{0,16},{2,18},{4,20},{6,22},{1,17},{3,19},{5,21},{7,23},{16,0},{18... | collective-permute-start | bytes 2359304 | tf_op jit(solution)/shard_map/ppermute | solution.py:47
  45.1 1.1 %collective-permute-start.12 = (f32[1,256]{1,0:T(1,128)S(1)}, f32[1,256]{1,0:T(1,128)S(1)}, u32[]{:S(2)}, u32[]{:S(2)}) collective-permute-start(f32[1,256]{1,0:T(1,128)S(1)} %get-tuple-element.54), channel_id=1, source_target_pairs={{0,8},{2,10},{4,12},{6,14},{1,9},{3,11},{5,13},{7,15},{16,24},{18,... | collective-permute-start | bytes 3080 | tf_op jit(solution)/shard_map/ppermute | solution.py:47
  46.2 3.8 %collective-permute-start.13 = (bf16[7,192,256]{2,1,0:T(8,128)(2,1)S(1)}, bf16[7,192,256]{2,1,0:T(8,128)(2,1)S(1)}, u32[]{:S(2)}, u32[]{:S(2)}) collective-permute-start(bf16[7,192,256]{2,1,0:T(8,128)(2,1)S(1)} %slice.8), channel_id=1, source_target_pairs={{0,8},{2,10},{4,12},{6,14},{1,9},{3,11},{5,13},{7,15},{16,24},{18,... | collective-permute-start | bytes 2064392 | tf_op jit(solution)/shard_map/ppermute | solution.py:47
  46.4 3.6 %collective-permute-start.14 = (f32[1,256]{1,0:T(1,128)S(1)}, f32[1,256]{1,0:T(1,128)S(1)}, u32[]{:S(2)}, u32[]{:S(2)}) collective-permute-start(f32[1,256]{1,0:T(1,128)S(1)} %add.17), channel_id=1, source_target_pairs={{0,16},{2,18},{4,20},{6,22},{1,17},{3,19},{5,21},{7,23},{16,0},{18... | collective-permute-start | bytes 3080 | tf_op jit(solution)/shard_map/ppermute | solution.py:47
  50.0 2.4 %collective-permute-start.16 = (bf16[8,192,256]{2,1,0:T(8,128)(2,1)S(1)}, bf16[8,192,256]{2,1,0:T(8,128)(2,1)S(1)}, u32[]{:S(2)}, u32[]{:S(2)}) collective-permute-start(bf16[8,192,256]{2,1,0:T(8,128)(2,1)S(1)} %collective-permute-done.7.mine_got), channel_id=1, source_target_pairs={{0,8},{2,10},{4,12},{6,14},{1,9},{3,11},{5,13},{7,15},{16,24},{18,... | collective-permute-start | bytes 2359304 | tf_op jit(solution)/shard_map/ppermute | solution.py:47
  50.0 2.4 %collective-permute-start.15 = (bf16[1,192,256]{2,1,0:T(8,128)(2,1)S(1)}, bf16[1,192,256]{2,1,0:T(8,128)(2,1)S(1)}, u32[]{:S(2)}, u32[]{:S(2)}) collective-permute-start(bf16[1,192,256]{2,1,0:T(8,128)(2,1)S(1)} %slice.7), channel_id=1, source_target_pairs={{0,8},{2,10},{4,12},{6,14},{1,9},{3,11},{5,13},{7,15},{16,24},{18,... | collective-permute-start | bytes 294920 | tf_op jit(solution)/shard_map/ppermute | solution.py:47

commit v5 on v4

--- a/solution.py
+++ b/solution.py
@@ -120,16 +120,17 @@
             piece[...] = weight[:, number * rows : (number + 1) * rows].T
 
 
+def peer_kernel(plan, acts, gain_ref, scaled, gain, end):
+    fetch(gain_ref, gain, end).wait()
+    scale_rows(acts, gain, scaled, 0, acts.shape[0])
+
+
 def term_kernel(
-    plan, where, acts, gain_ref, scaled, mine, theirs,
-    sent_ref, kept_ref, held_ref, gain, peer_scaled, totals, end,
+    plan, where, scaled, peer_scaled, mine, theirs, sent_ref, kept_ref, held_ref, totals,
 ):
     width, depth = plan.width, plan.depth
-    tokens, model = acts.shape
     rows = mine.shape[0] // width
-    cols = model // plan.subs
-    fetch(gain_ref, gain, end).wait()
-    scale_rows(acts, gain, peer_scaled, 0, tokens)
+    cols = scaled.shape[1] // plan.subs
 
     for to_x in range(width):
         for to_z in range(depth):
@@ -246,53 +247,68 @@
 
 
 def grad_kernel(
-    plan, where, acts, gain_ref, grads, inverse, mine_sent, mine_got, peer_first, peer_rest, peer_got,
+    plan, where, acts, gain_ref, grads, inverse,
+    own, over, own_got, over_got, peer_own, peer_first, peer_over, peer_own_first, peer_own_rest, peer_over_got,
     out_ref, weight, grad_scaled, mean_ref, out, ends,
 ):
     core = where[0]
     depth = plan.depth
     tokens, cols = acts.shape[2:]
     model = cols * plan.subs
-    place_weight(plan, where, [mine_sent], core, False, weight)
-    place_weight(plan, where, [peer_first, peer_rest], 1 - core, False, weight)
-    place_weight(plan, where, [mine_got], core, True, weight)
-    place_weight(plan, where, [peer_got], 1 - core, True, weight)
+    place_weight(plan, where, [own, over], core, False, weight)
+    place_weight(plan, where, [peer_own, peer_first, peer_over], 1 - core, False, weight)
+    place_weight(plan, where, [own_got, over_got], core, True, weight)
+    place_weight(plan, where, [peer_own_first, peer_own_rest, peer_over_got], 1 - core, True, weight)
     blocks = [(flip, step) for flip in range(2) for step in range(depth)]
-    for flip, step in blocks:
-        number = flip * depth + step
+
+    def multiply(number):
         grad_scaled[number] = jnp.dot(grads[...], weight[number], preferred_element_type=F32)
+
+    def add_mean(number):
+        flip, step = blocks[number]
         gain = gain_ref[:, columns(plan, where, flip, step, cols)]
         for start in range(0, tokens, TILE):
             part = slice(start, start + TILE)
-            scale = inverse[part, :]
             mean = None
             for lane in range(0, cols, 128):
                 lanes = slice(lane, lane + 128)
-                normed = acts[flip, step, part, lanes].astype(F32) * scale
-                product = gain[:, lanes] * grad_scaled[number, part, lanes] * normed
+                product = gain[:, lanes] * grad_scaled[number, part, lanes]
+                product = product * acts[flip, step, part, lanes].astype(F32)
                 mean = product if mean is None else mean + product
             if number == 0:
                 mean_ref[part, :] = mean
             else:
                 mean_ref[part, :] += mean
+
+    multiply(0)
+    for number in range(1, len(blocks)):
+        multiply(number)
+        add_mean(number - 1)
+    add_mean(len(blocks) - 1)
     mean = jnp.sum(mean_ref[...], axis=1, keepdims=True) / model
-    mean_ref[...] = jnp.broadcast_to(mean, mean_ref.shape)
+    scale = inverse[...]
+    mean_ref[...] = mean * scale * scale * scale
 
     stores = []
-    for flip, step in blocks:
-        number = flip * depth + step
-        here = columns(plan, where, flip, step, cols)
-        gain = gain_ref[:, here]
-        for start in range(0, tokens, TILE):
-            part = slice(start, start + TILE)
-            scale = inverse[part, :]
-            mean = mean_ref[part, :]
-            for lane in range(0, cols, 128):
-                lanes = slice(lane, lane + 128)
-                normed = acts[flip, step, part, lanes].astype(F32) * scale
-                gained = gain[:, lanes] * grad_scaled[number, part, lanes]
-                out[number, part, lanes] = (scale * (gained - normed * mean)).astype(BF16)
-        stores.append(fetch(out.at[number], out_ref.at[:, here], ends.at[number]))
+    big = tokens // CHUNKS
+    for base in range(0, tokens, big):
+        for flip, step in blocks:
+            number = flip * depth + step
+            here = columns(plan, where, flip, step, cols)
+            gain = gain_ref[:, here]
+            for start in range(base, base + big, TILE):
+                part = slice(start, start + TILE)
+                scale = inverse[part, :]
+                mean = mean_ref[part, :]
+                tiles = []
+                for lane in range(0, cols, 128):
+                    lanes = slice(lane, lane + 128)
+                    inputs = acts[flip, step, part, lanes].astype(F32)
+                    gained = gain[:, lanes] * grad_scaled[number, part, lanes]
+                    tiles.append((scale * gained - inputs * mean).astype(BF16))
+                out[part, here] = jnp.concatenate(tiles, axis=1)
+        rows_here = pl.ds(base, big)
+        stores.append(fetch(out.at[rows_here], out_ref.at[rows_here], ends.at[base // big]))
     for store in stores:
         store.wait()
 
@@ -360,6 +376,17 @@
         name="mine",
     )(where, acts_hbm, gain_hbm, grads_hbm, in_hbm(key_weight))
     theirs = plan.send(other, to_core)
+    peer_scaled = pl.pallas_call(
+        functools.partial(peer_kernel, plan),
+        out_shape=pltpu.VMEM((tokens, model), BF16),
+        in_specs=[VMEM, HBM],
+        out_specs=VMEM,
+        scratch_shapes=[pltpu.VMEM((1, model), F32), pltpu.SemaphoreType.DMA(())],
+        compiler_params=params(2),
+        cost_estimate=cost(0, 2 * MIB),
+        name="peer",
+    )(peer_acts, gain_hbm)
+    theirs, _ = lax.optimization_barrier((theirs, peer_scaled))
     sent, kept, held = pl.pallas_call(
         functools.partial(term_kernel, plan),
         out_shape=(
@@ -367,18 +394,13 @@
             pltpu.VMEM((depth, rows, cols), F32),
             pltpu.VMEM((depth, rows, cols), F32),
         ),
-        in_specs=[SMEM, VMEM, HBM, VMEM, VMEM, VMEM],
+        in_specs=[SMEM] + [VMEM] * 4,
         out_specs=[VMEM] * 3,
-        scratch_shapes=[
-            pltpu.VMEM((1, model), F32),
-            pltpu.VMEM((tokens, model), BF16),
-            pltpu.VMEM((2 * width * depth, rows, cols), F32),
-            pltpu.SemaphoreType.DMA(()),
-        ],
-        compiler_params=params(8),
+        scratch_shapes=[pltpu.VMEM((2 * width * depth, rows, cols), F32)],
+        compiler_params=params(6),
         cost_estimate=cost(4 * tokens * model * width * rows, 20 * MIB),
         name="term",
-    )(where, peer_acts, gain_hbm, scaled, mine, theirs)
+    )(where, scaled, peer_scaled, mine, theirs)
     got = plan.send(sent, y_then)
 
     acts, grads, inverse = pl.pallas_call(
@@ -397,8 +419,8 @@
     )(where, acts_hbm, grads_hbm)
 
     planes = [plan.send(piece, to_z(step)) for step in range(1, depth)]
-    got, planes[:-1], acts, grads, inverse = lax.optimization_barrier(
-        (got, planes[:-1], acts, grads, inverse)
+    got, planes[1], acts, grads, inverse = lax.optimization_barrier(
+        (got, planes[1], acts, grads, inverse)
     )
 
     sent = pl.pallas_call(
@@ -410,6 +432,7 @@
         cost_estimate=cost(0, 2 * MIB),
         name="half",
     )(where, kept, got)
+    sent, planes = lax.optimization_barrier((sent, planes))
     again = plan.send(sent, x_then)
 
     own = pl.pallas_call(
@@ -423,7 +446,6 @@
     )(piece, *planes)
     own, _ = lax.optimization_barrier((own, sent))
     over = plan.send(own, x_then)
-    mine_sent = jnp.concatenate([own, over])
     sums, gains, *sents = pl.pallas_call(
         functools.partial(plane_kernel, plan),
         out_shape=[pltpu.VMEM((rows, cols), F32), pltpu.VMEM((1, cols), F32)]
@@ -435,7 +457,9 @@
         name="plane",
     )(where, held, got, own, again, gain)
     gots = [plan.send(array, to_z(step + 1)) for step, array in enumerate(sents)]
-    mine_got = plan.send(mine_sent, y_then)
+    first, _ = lax.optimization_barrier((own, again))
+    own_got = plan.send(first, y_then)
+    over_got = plan.send(over, y_then)
     weight_grads, gains = pl.pallas_call(
         functools.partial(last_kernel, plan),
         out_shape=(shape((rows, cols), F32), pltpu.VMEM((1, cols), F32)),
@@ -445,30 +469,39 @@
         cost_estimate=cost(0, MIB),
         name="last",
     )(sums, gains, *gots)
+    peer_own = plan.send(own, to_core)
+    peer_first = plan.send(over[: 2 * EARLY], to_core)
+    rest, gains = lax.optimization_barrier((over[2 * EARLY :], gains))
+    peer_over = plan.send(rest, to_core)
     gains = gains + plan.send(gains, to_core)
-    peer_first = plan.send(mine_sent[:EARLY], to_core)
-    rest, gains = lax.optimization_barrier((mine_sent[EARLY:], gains))
-    peer_rest = plan.send(rest, to_core)
+    peer_own_first = plan.send(own_got[: depth - 1], to_core)
+    over_got, peer_over, peer_own_first, gains = lax.optimization_barrier(
+        (over_got, peer_over, peer_own_first, gains)
+    )
+    peer_over_got = plan.send(over_got, to_core)
+    peer_own_rest = plan.send(own_got[depth - 1 :], to_core)
     peer_gains = plan.send(gains, to_y)
-    mine_got, peer_rest, peer_gains = lax.optimization_barrier((mine_got, peer_rest, peer_gains))
-    peer_got = plan.send(mine_got, to_core)
 
     input_grads = pl.pallas_call(
         functools.partial(grad_kernel, plan),
         out_shape=shape((tokens, model), BF16),
-        in_specs=[SMEM] + [VMEM] * 9,
+        in_specs=[SMEM] + [VMEM] * 14,
         out_specs=HBM,
         scratch_shapes=[
             pltpu.VMEM((2 * depth, key_width, cols), BF16),
             pltpu.VMEM((2 * depth, tokens, cols), F32),
             pltpu.VMEM((tokens, 128), F32),
-            pltpu.VMEM((2 * depth, tokens, cols), BF16),
-            pltpu.SemaphoreType.DMA((2 * depth,)),
+            pltpu.VMEM((tokens, model), BF16),
+            pltpu.SemaphoreType.DMA((CHUNKS,)),
         ],
         compiler_params=params(12),
         cost_estimate=cost(2 * tokens * model * key_width, 8 * MIB),
         name="grad",
-    )(where, acts, gain, grads, inverse, mine_sent, mine_got, peer_first, peer_rest, peer_got)
+    )(
+        where, acts, gain, grads, inverse,
+        own, over, own_got, over_got, peer_own, peer_first, peer_over, peer_own_first, peer_own_rest, peer_over_got,
+    )
+    peer_gains, input_grads = lax.optimization_barrier((peer_gains, input_grads))
     return input_grads, weight_grads.T, (gains + peer_gains).reshape(cols) / plan.groups
 
 

time: 57.6 us -> 53.9 us (0.936)
  waiting for transfers between devices: 20.1 us -> 14.8 us
  starting transfers between devices: 18.9 us -> 20.9 us
    ppermute x17 -> x21, waiting for transfers between devices: 20.1 us -> 14.8 us  [send(): return lax.ppermute(array, AXES, self.pairs(move))]
    ppermute x17 -> x21, starting transfers between devices: 18.9 us -> 20.9 us  [send(): return lax.ppermute(array, AXES, self.pairs(move))]
    pallas_call x1, Pallas kernels: 4.11 us -> 2.51 us  [by_permutes(): pl.pallas_call(functools.partial(term_kernel, plan), out_shape=(pltpu.VME...]
    pallas_call x0 -> x1, Pallas kernels: none -> 1.58 us  [by_permutes(): pl.pallas_call(functools.partial(peer_kernel, plan), out_shape=pltpu.VMEM...]
  transfers between devices with their start and end apart: 17 -> 21, of which waited for: 8 -> 11; matrix products, arithmetic and copies ran while one was open for 1% -> 0% of each run, Pallas kernels for 14% -> 26%
where the time goes in v5:
time: 53.9 us; the launch traced here: 53.7 us
  starting transfers between devices  20.9 us (39%)
  Pallas kernels  16.6 us (31%)
  waiting for transfers between devices  14.8 us (27%)
  between operations  0.76 us (1%)
  other arithmetic  0.65 us (1%)
    ppermute x21, starting transfers between devices, send(): return lax.ppermute(array, AXES, self.pairs(move))  20.9 us
    ppermute x21, waiting for transfers between devices, send(): return lax.ppermute(array, AXES, self.pairs(move))  14.8 us
    pallas_call x1, Pallas kernels, by_permutes(): pl.pallas_call(functools.partial(grad_kernel, plan), out_shape=shape((tok...  4.56 us
    pallas_call x1, Pallas kernels, by_permutes(): pl.pallas_call(functools.partial(mine_kernel, plan), out_shape=(pltpu.VME...  3.18 us
    pallas_call x1, Pallas kernels, by_permutes(): pl.pallas_call(functools.partial(load_kernel, plan), out_shape=(pltpu.VME...  2.56 us
    pallas_call x1, Pallas kernels, by_permutes(): pl.pallas_call(functools.partial(term_kernel, plan), out_shape=(pltpu.VME...  2.51 us
    pallas_call x1, Pallas kernels, by_permutes(): pl.pallas_call(functools.partial(peer_kernel, plan), out_shape=pltpu.VMEM...  1.58 us
  transfers between devices with their start and end apart: 21, of which 11 were waited for; matrix products, arithmetic and copies ran while one was open for 0% of the time, Pallas kernels for 26%

profile of v5, /device:TPU:0, one launch (start us, length us, event | category | flops | bytes accessed | tf_op | source)
XLA Modules:
  0.0 53.7 jit_solution(11162874841010831580)
XLA Ops:
  0.6 0.5 collective-permute-start
  1.1 0.1 pad_add_fusion.where
  1.2 3.2 %mine.1 = (bf16[512,2048]{1,0:T(8,128)(2,1)S(1)}, bf16[384,512]{1,0:T(8,128)(2,1)S(1)}, bf16[384,512]{1,0:T(8,128)(2,1)S(1)}, bf16[192,256]{1,0:T(8,128)(2,1)S(1)}) custom-call(s32[4]{0:T(128)S(1)} %pad_add_fusion.where, bf16[512,2048]{1,0:T(8,128)(2,1)} %acts_ref.3, f32[1,2048]{1,0:T(1,128)} %bitcast.7, bf16[512,768]{1,0:T(8,128)(2,1)} %grads_ref.3, ...), custom_call_target="tpu_custom_call" | custom-call | tf_op jit(solution)/shard_map/mine/pallas_call | solution.py:356
  4.4 0.2 collective-permute-start.1
  4.6 0.5 collective-permute-done.acts
  5.1 1.6 %peer.1.peer_scaled = bf16[512,2048]{1,0:T(8,128)(2,1)S(1)} custom-call(bf16[512,2048]{1,0:T(8,128)(2,1)S(1)} %collective-permute-done.acts, f32[1,2048]{1,0:T(1,128)} %bitcast.8), custom_call_target="tpu_custom_call" | custom-call | tf_op jit(solution)/shard_map/peer/pallas_call | solution.py:379
  6.7 0.0 collective-permute-done.1.theirs
  6.7 2.5 %term.1 = (bf16[8,192,256]{2,1,0:T(8,128)(2,1)S(1)}, f32[4,192,256]{2,1,0:T(8,128)S(1)}, f32[4,192,256]{2,1,0:T(8,128)S(1)}) custom-call(s32[4]{0:T(128)S(1)} %pad_add_fusion.where, bf16[512,2048]{1,0:T(8,128)(2,1)S(1)} %get-tuple-element.41.scaled, bf16[512,2048]{1,0:T(8,128)(2,1)S(1)} %peer.1.peer_scaled, bf16[384,512]{1,0:T(8,128)(2,1)S(1)} %get-tuple-element.42.mine, ...), custom_call_target="tpu_custom_call" | custom-call | tf_op jit(solution)/shard_map/term/pallas_call | solution.py:390
  9.3 3.0 %collective-permute-start.2 = (bf16[8,192,256]{2,1,0:T(8,128)(2,1)S(1)}, bf16[8,192,256]{2,1,0:T(8,128)(2,1)S(1)}, u32[]{:S(2)}, u32[]{:S(2)}) collective-permute-start(bf16[8,192,256]{2,1,0:T(8,128)(2,1)S(1)} %get-tuple-element.46), channel_id=1, source_target_pairs={{0,16},{2,18},{4,20},{6,22},{1,17},{3,19},{5,21},{7,23},{16,0},{18... | collective-permute-start | bytes 2359304 | tf_op jit(solution)/shard_map/ppermute | solution.py:47
  12.2 2.6 %collective-permute-start.3 = (bf16[192,256]{1,0:T(8,128)(2,1)S(1)}, bf16[192,256]{1,0:T(8,128)(2,1)S(1)}, u32[]{:S(2)}, u32[]{:S(2)}) collective-permute-start(bf16[192,256]{1,0:T(8,128)(2,1)S(1)} %get-tuple-element.40.refs_0_), channel_id=1, source_target_pairs={{0,4},{2,6},{4,0},{6,2},{1,5},{3,7},{5,1},{7,3},{16,20},{18,22},{2... | collective-permute-start | bytes 294920 | tf_op jit(solution)/shard_map/ppermute | solution.py:47
  14.8 1.6 %collective-permute-start.4 = (bf16[192,256]{1,0:T(8,128)(2,1)S(1)}, bf16[192,256]{1,0:T(8,128)(2,1)S(1)}, u32[]{:S(2)}, u32[]{:S(2)}) collective-permute-start(bf16[192,256]{1,0:T(8,128)(2,1)S(1)} %get-tuple-element.40.refs_0_), channel_id=1, source_target_pairs={{0,2},{2,0},{4,6},{6,4},{1,3},{3,1},{5,7},{7,5},{16,18},{18,16},{2... | collective-permute-start | bytes 294920 | tf_op jit(solution)/shard_map/ppermute | solution.py:47
  16.4 0.2 collective-permute-start.5
  16.6 2.6 %load.1 = (bf16[2,4,512,256]{3,2,1,0:T(8,128)(2,1)S(1)}, bf16[512,768]{1,0:T(8,128)(2,1)S(1)}, f32[512,128]{1,0:T(8,128)S(1)}) custom-call(s32[4]{0:T(128)S(1)} %pad_add_fusion.where, bf16[512,2048]{1,0:T(8,128)(2,1)} %acts_ref.3, bf16[512,768]{1,0:T(8,128)(2,1)} %grads_ref.3), custom_call_target="tpu_custom_call" | custom-call | tf_op jit(solution)/shard_map/load/pallas_call | solution.py:406
  19.2 0.0 copy-start
  19.2 1.7 %collective-permute-done.3.refs_2_ = bf16[192,256]{1,0:T(8,128)(2,1)S(1)} collective-permute-done((bf16[192,256]{1,0:T(8,128)(2,1)S(1)}, bf16[192,256]{1,0:T(8,128)(2,1)S(1)}, u32[]{:S(2)}, u32[]{:S(2)}) %collective-permute-start.3) | collective-permute-done | bytes 98336 | tf_op jit(solution)/shard_map/ppermute | solution.py:47
  20.9 1.2 %collective-permute-done.2.got_ref = bf16[8,192,256]{2,1,0:T(8,128)(2,1)S(1)} collective-permute-done((bf16[8,192,256]{2,1,0:T(8,128)(2,1)S(1)}, bf16[8,192,256]{2,1,0:T(8,128)(2,1)S(1)}, u32[]{:S(2)}, u32[]{:S(2)}) %collective-permute-start.2) | collective-permute-done | bytes 786464 | tf_op jit(solution)/shard_map/ppermute | solution.py:47
  22.2 0.6 %half.1 = bf16[4,192,256]{2,1,0:T(8,128)(2,1)S(1)} custom-call(s32[4]{0:T(128)S(1)} %pad_add_fusion.where, f32[4,192,256]{2,1,0:T(8,128)S(1)} %get-tuple-element.45.kept, bf16[8,192,256]{2,1,0:T(8,128)(2,1)S(1)} %collective-permute-done.2.got_ref), custom_call_target="tpu_custom_call" | custom-call | tf_op jit(solution)/shard_map/half/pallas_call | solution.py:426
  22.8 0.1 collective-permute-done.5.refs_3_
  22.9 2.0 %collective-permute-start.8 = (bf16[4,192,256]{2,1,0:T(8,128)(2,1)S(1)}, bf16[4,192,256]{2,1,0:T(8,128)(2,1)S(1)}, u32[]{:S(2)}, u32[]{:S(2)}) collective-permute-start(bf16[4,192,256]{2,1,0:T(8,128)(2,1)S(1)} %half.1), channel_id=1, source_target_pairs={{0,1},{2,3},{4,5},{6,7},{1,0},{3,2},{5,4},{7,6},{16,17},{18,19},{2... | collective-permute-start | bytes 1179656 | tf_op jit(solution)/shard_map/ppermute | solution.py:47
  24.9 0.1 collective-permute-start.6
  25.0 5.7 %collective-permute-done.8.again_ref = bf16[4,192,256]{2,1,0:T(8,128)(2,1)S(1)} collective-permute-done((bf16[4,192,256]{2,1,0:T(8,128)(2,1)S(1)}, bf16[4,192,256]{2,1,0:T(8,128)(2,1)S(1)}, u32[]{:S(2)}, u32[]{:S(2)}) %collective-permute-start.8) | collective-permute-done | bytes 393248 | tf_op jit(solution)/shard_map/ppermute | solution.py:47
  30.7 2.0 %collective-permute-start.13 = (bf16[4,192,256]{2,1,0:T(8,128)(2,1)S(1)}, bf16[4,192,256]{2,1,0:T(8,128)(2,1)S(1)}, u32[]{:S(2)}, u32[]{:S(2)}) collective-permute-start(bf16[4,192,256]{2,1,0:T(8,128)(2,1)S(1)} %pack.1.own), channel_id=1, source_target_pairs={{0,16},{2,18},{4,20},{6,22},{1,17},{3,19},{5,21},{7,23},{16,0},{18... | collective-permute-start | bytes 1179656 | tf_op jit(solution)/shard_map/ppermute | solution.py:47
  32.7 0.8 %plane.1 = (f32[192,256]{1,0:T(8,128)S(1)}, f32[1,256]{1,0:T(1,128)S(1)}, bf16[208,256]{1,0:T(8,128)(2,1)S(1)}, bf16[208,256]{1,0:T(8,128)(2,1)S(1)}, bf16[208,256]{1,0:T(8,128)(2,1)S(1)}) custom-call(s32[4]{0:T(128)S(1)} %pad_add_fusion.where, f32[4,192,256]{2,1,0:T(8,128)S(1)} %get-tuple-element.57.held, ...), custom_call_target="tpu_custom_call" | custom-call | tf_op jit(solution)/shard_map/plane/pallas_call | solution.py:449
  33.5 3.2 %collective-permute-start.10 = (bf16[208,256]{1,0:T(8,128)(2,1)S(1)}, bf16[208,256]{1,0:T(8,128)(2,1)S(1)}, u32[]{:S(2)}, u32[]{:S(2)}) collective-permute-start(bf16[208,256]{1,0:T(8,128)(2,1)S(1)} %get-tuple-element.61), channel_id=1, source_target_pairs={{0,4},{2,6},{4,0},{6,2},{1,5},{3,7},{5,1},{7,3},{16,20},{18,22},{2... | collective-permute-start | bytes 319496 | tf_op jit(solution)/shard_map/ppermute | solution.py:47
  36.7 0.8 %collective-permute-start.11 = (bf16[208,256]{1,0:T(8,128)(2,1)S(1)}, bf16[208,256]{1,0:T(8,128)(2,1)S(1)}, u32[]{:S(2)}, u32[]{:S(2)}) collective-permute-start(bf16[208,256]{1,0:T(8,128)(2,1)S(1)} %get-tuple-element.62), channel_id=1, source_target_pairs={{0,6},{2,4},{4,2},{6,0},{1,7},{3,5},{5,3},{7,1},{16,22},{18,20},{2... | collective-permute-start | bytes 319496 | tf_op jit(solution)/shard_map/ppermute | solution.py:47
  37.5 0.2 collective-permute-start.9
  37.7 0.0 collective-permute-done.6.over
  37.7 2.0 %collective-permute-start.7 = (bf16[4,192,256]{2,1,0:T(8,128)(2,1)S(1)}, bf16[4,192,256]{2,1,0:T(8,128)(2,1)S(1)}, u32[]{:S(2)}, u32[]{:S(2)}) collective-permute-start(bf16[4,192,256]{2,1,0:T(8,128)(2,1)S(1)} %collective-permute-done.6.over), channel_id=1, source_target_pairs={{0,16},{2,18},{4,20},{6,22},{1,17},{3,19},{5,21},{7,23},{16,0},{18... | collective-permute-start | bytes 1179656 | tf_op jit(solution)/shard_map/ppermute | solution.py:47
  39.8 0.0 collective-permute-done.13.own_got
  39.8 0.1 collective-permute-start.14
  39.9 2.3 %collective-permute-done.10.refs_1_ = bf16[208,256]{1,0:T(8,128)(2,1)S(1)} collective-permute-done((bf16[208,256]{1,0:T(8,128)(2,1)S(1)}, bf16[208,256]{1,0:T(8,128)(2,1)S(1)}, u32[]{:S(2)}, u32[]{:S(2)}) %collective-permute-start.10) | collective-permute-done | bytes 106528 | tf_op jit(solution)/shard_map/ppermute | solution.py:47
  42.2 1.2 %collective-permute-done.11.refs_2_ = bf16[208,256]{1,0:T(8,128)(2,1)S(1)} collective-permute-done((bf16[208,256]{1,0:T(8,128)(2,1)S(1)}, bf16[208,256]{1,0:T(8,128)(2,1)S(1)}, u32[]{:S(2)}, u32[]{:S(2)}) %collective-permute-start.11) | collective-permute-done | bytes 106528 | tf_op jit(solution)/shard_map/ppermute | solution.py:47
  43.4 0.8 %collective-permute-done.9.refs_0_ = bf16[208,256]{1,0:T(8,128)(2,1)S(1)} collective-permute-done((bf16[208,256]{1,0:T(8,128)(2,1)S(1)}, bf16[208,256]{1,0:T(8,128)(2,1)S(1)}, u32[]{:S(2)}, u32[]{:S(2)}) %collective-permute-start.9) | collective-permute-done | bytes 106528 | tf_op jit(solution)/shard_map/ppermute | solution.py:47
  44.1 0.7 %last.1 = (f32[192,256]{1,0:T(8,128)}, f32[1,256]{1,0:T(1,128)S(1)}) custom-call(f32[192,256]{1,0:T(8,128)S(1)} %get-tuple-element.58.sums_ref, f32[1,256]{1,0:T(1,128)S(1)} %get-tuple-element.59.gains_ref, bf16[208,256]{1,0:T(8,128)(2,1)S(1)} %collective-permute-done.9.refs_0_, bf16[208,256]{1,0:T(8,128)(2,1)S(1)} %collective-permute-done.10.refs_1_, ...), custom_call_target="tpu_custom_call" | custom-call | tf_op jit(solution)/shard_map/last/pallas_call | solution.py:463
  44.9 0.0 collective-permute-start.12
  44.9 0.5 collective-permute-start.15
  45.4 0.9 %collective-permute-done.15 = f32[1,256]{1,0:T(1,128)S(1)} collective-permute-done((f32[1,256]{1,0:T(1,128)S(1)}, f32[1,256]{1,0:T(1,128)S(1)}, u32[]{:S(2)}, u32[]{:S(2)}) %collective-permute-start.15) | collective-permute-done | bytes 1056 | tf_op jit(solution)/shard_map/ppermute | solution.py:47
  46.3 0.0 collective-permute-done.12.peer_over
  46.3 0.0 collective-permute-done.7.over_got
  46.3 0.0 collective-permute-done.14.peer_own_first
  46.3 0.3 collective-permute-start.20
  46.6 0.3 collective-permute-start.18
  46.9 0.3 collective-permute-start.19
  47.2 1.0 %collective-permute-start.16 = (f32[1,256]{1,0:T(1,128)S(1)}, f32[1,256]{1,0:T(1,128)S(1)}, u32[]{:S(2)}, u32[]{:S(2)}) collective-permute-start(f32[1,256]{1,0:T(1,128)S(1)} %add.17), channel_id=1, source_target_pairs={{0,16},{2,18},{4,20},{6,22},{1,17},{3,19},{5,21},{7,23},{16,0},{18... | collective-permute-start | bytes 3080 | tf_op jit(solution)/shard_map/ppermute | solution.py:47
  48.2 0.2 collective-permute-done.18.peer_first
  48.4 0.1 collective-permute-done.19.peer_own_rest
  48.5 4.6 %grad.1 = bf16[512,2048]{1,0:T(8,128)(2,1)} custom-call(s32[4]{0:T(128)S(1)} %pad_add_fusion.where, bf16[2,4,512,256]{3,2,1,0:T(8,128)(2,1)S(1)} %get-tuple-element.68.acts, f32[1,2048]{1,0:T(1,128)S(1)} %bitcast.10, bf16[512,768]{1,0:T(8,128)(2,1)S(1)} %get-tuple-element.69.grads, f32[512,128]{1,0:T(8,128)S(1)} %get-tuple-element.70.inverse, ...), custom_call_target="tpu_custom_call" | custom-call | tf_op jit(solution)/shard_map/grad/pallas_call | solution.py:485
  53.1 0.6 %add_multiply_fusion = f32[1,256]{1,0:T(1,128)} fusion(f32[1,256]{1,0:T(1,128)S(1)} %add.17, f32[1,256]{1,0:T(1,128)S(1)} %collective-permute-done.16), kind=kLoop, calls=%fused_computation | loop fusion | flops 512 | bytes 3072 | tf_op jit(solution)/shard_map/div | solution.py:505
  (11 shorter events, 0.1 us)
Async XLA Ops:
  0.6 4.5 %collective-permute-start = (bf16[512,2048]{1,0:T(8,128)(2,1)}, bf16[512,2048]{1,0:T(8,128)(2,1)S(1)}, u32[]{:S(2)}, u32[]{:S(2)}) collective-permute-start(bf16[512,2048]{1,0:T(8,128)(2,1)} %acts_ref.3), channel_id=1, source_target_pairs={{0,8},{2,10},{4,12},{6,14},{1,9},{3,11},{5,13},{7,15},{16,24},{18,... | collective-permute-start | bytes 6291464 | tf_op jit(solution)/shard_map/ppermute | solution.py:47
  4.4 2.3 %collective-permute-start.1 = (bf16[384,512]{1,0:T(8,128)(2,1)S(1)}, bf16[384,512]{1,0:T(8,128)(2,1)S(1)}, u32[]{:S(2)}, u32[]{:S(2)}) collective-permute-start(bf16[384,512]{1,0:T(8,128)(2,1)S(1)} %get-tuple-element.43), channel_id=1, source_target_pairs={{0,8},{2,10},{4,12},{6,14},{1,9},{3,11},{5,13},{7,15},{16,24},{18,... | collective-permute-start | bytes 1179656 | tf_op jit(solution)/shard_map/ppermute | solution.py:47
  9.3 12.9 %collective-permute-start.2 = (bf16[8,192,256]{2,1,0:T(8,128)(2,1)S(1)}, bf16[8,192,256]{2,1,0:T(8,128)(2,1)S(1)}, u32[]{:S(2)}, u32[]{:S(2)}) collective-permute-start(bf16[8,192,256]{2,1,0:T(8,128)(2,1)S(1)} %get-tuple-element.46), channel_id=1, source_target_pairs={{0,16},{2,18},{4,20},{6,22},{1,17},{3,19},{5,21},{7,23},{16,0},{18... | collective-permute-start | bytes 2359304 | tf_op jit(solution)/shard_map/ppermute | solution.py:47
  12.2 8.7 %collective-permute-start.3 = (bf16[192,256]{1,0:T(8,128)(2,1)S(1)}, bf16[192,256]{1,0:T(8,128)(2,1)S(1)}, u32[]{:S(2)}, u32[]{:S(2)}) collective-permute-start(bf16[192,256]{1,0:T(8,128)(2,1)S(1)} %get-tuple-element.40.refs_0_), channel_id=1, source_target_pairs={{0,4},{2,6},{4,0},{6,2},{1,5},{3,7},{5,1},{7,3},{16,20},{18,22},{2... | collective-permute-start | bytes 294920 | tf_op jit(solution)/shard_map/ppermute | solution.py:47
  14.8 8.0 %collective-permute-start.4 = (bf16[192,256]{1,0:T(8,128)(2,1)S(1)}, bf16[192,256]{1,0:T(8,128)(2,1)S(1)}, u32[]{:S(2)}, u32[]{:S(2)}) collective-permute-start(bf16[192,256]{1,0:T(8,128)(2,1)S(1)} %get-tuple-element.40.refs_0_), channel_id=1, source_target_pairs={{0,2},{2,0},{4,6},{6,4},{1,3},{3,1},{5,7},{7,5},{16,18},{18,16},{2... | collective-permute-start | bytes 294920 | tf_op jit(solution)/shard_map/ppermute | solution.py:47
  16.4 6.5 %collective-permute-start.5 = (bf16[192,256]{1,0:T(8,128)(2,1)S(1)}, bf16[192,256]{1,0:T(8,128)(2,1)S(1)}, u32[]{:S(2)}, u32[]{:S(2)}) collective-permute-start(bf16[192,256]{1,0:T(8,128)(2,1)S(1)} %get-tuple-element.40.refs_0_), channel_id=1, source_target_pairs={{0,6},{2,4},{4,2},{6,0},{1,7},{3,5},{5,3},{7,1},{16,22},{18,20},{2... | collective-permute-start | bytes 294920 | tf_op jit(solution)/shard_map/ppermute | solution.py:47
  19.2 13.5 %copy-start = (f32[2048]{0:T(1024)S(1)}, f32[2048]{0:T(1024)}, u32[]{:S(2)}) copy-start(f32[2048]{0:T(1024)} %param.5) | copy-start | bytes 24580
  22.9 7.8 %collective-permute-start.8 = (bf16[4,192,256]{2,1,0:T(8,128)(2,1)S(1)}, bf16[4,192,256]{2,1,0:T(8,128)(2,1)S(1)}, u32[]{:S(2)}, u32[]{:S(2)}) collective-permute-start(bf16[4,192,256]{2,1,0:T(8,128)(2,1)S(1)} %half.1), channel_id=1, source_target_pairs={{0,1},{2,3},{4,5},{6,7},{1,0},{3,2},{5,4},{7,6},{16,17},{18,19},{2... | collective-permute-start | bytes 1179656 | tf_op jit(solution)/shard_map/ppermute | solution.py:47
  24.9 12.8 %collective-permute-start.6 = (bf16[4,192,256]{2,1,0:T(8,128)(2,1)S(1)}, bf16[4,192,256]{2,1,0:T(8,128)(2,1)S(1)}, u32[]{:S(2)}, u32[]{:S(2)}) collective-permute-start(bf16[4,192,256]{2,1,0:T(8,128)(2,1)S(1)} %pack.1.own), channel_id=1, source_target_pairs={{0,1},{2,3},{4,5},{6,7},{1,0},{3,2},{5,4},{7,6},{16,17},{18,19},{2... | collective-permute-start | bytes 1179656 | tf_op jit(solution)/shard_map/ppermute | solution.py:47
  30.7 9.1 %collective-permute-start.13 = (bf16[4,192,256]{2,1,0:T(8,128)(2,1)S(1)}, bf16[4,192,256]{2,1,0:T(8,128)(2,1)S(1)}, u32[]{:S(2)}, u32[]{:S(2)}) collective-permute-start(bf16[4,192,256]{2,1,0:T(8,128)(2,1)S(1)} %pack.1.own), channel_id=1, source_target_pairs={{0,16},{2,18},{4,20},{6,22},{1,17},{3,19},{5,21},{7,23},{16,0},{18... | collective-permute-start | bytes 1179656 | tf_op jit(solution)/shard_map/ppermute | solution.py:47
  33.5 8.7 %collective-permute-start.10 = (bf16[208,256]{1,0:T(8,128)(2,1)S(1)}, bf16[208,256]{1,0:T(8,128)(2,1)S(1)}, u32[]{:S(2)}, u32[]{:S(2)}) collective-permute-start(bf16[208,256]{1,0:T(8,128)(2,1)S(1)} %get-tuple-element.61), channel_id=1, source_target_pairs={{0,4},{2,6},{4,0},{6,2},{1,5},{3,7},{5,1},{7,3},{16,20},{18,22},{2... | collective-permute-start | bytes 319496 | tf_op jit(solution)/shard_map/ppermute | solution.py:47
  36.7 6.7 %collective-permute-start.11 = (bf16[208,256]{1,0:T(8,128)(2,1)S(1)}, bf16[208,256]{1,0:T(8,128)(2,1)S(1)}, u32[]{:S(2)}, u32[]{:S(2)}) collective-permute-start(bf16[208,256]{1,0:T(8,128)(2,1)S(1)} %get-tuple-element.62), channel_id=1, source_target_pairs={{0,6},{2,4},{4,2},{6,0},{1,7},{3,5},{5,3},{7,1},{16,22},{18,20},{2... | collective-permute-start | bytes 319496 | tf_op jit(solution)/shard_map/ppermute | solution.py:47
  37.5 6.6 %collective-permute-start.9 = (bf16[208,256]{1,0:T(8,128)(2,1)S(1)}, bf16[208,256]{1,0:T(8,128)(2,1)S(1)}, u32[]{:S(2)}, u32[]{:S(2)}) collective-permute-start(bf16[208,256]{1,0:T(8,128)(2,1)S(1)} %get-tuple-element.60), channel_id=1, source_target_pairs={{0,2},{2,0},{4,6},{6,4},{1,3},{3,1},{5,7},{7,5},{16,18},{18,16},{2... | collective-permute-start | bytes 319496 | tf_op jit(solution)/shard_map/ppermute | solution.py:47
  37.7 8.6 %collective-permute-start.7 = (bf16[4,192,256]{2,1,0:T(8,128)(2,1)S(1)}, bf16[4,192,256]{2,1,0:T(8,128)(2,1)S(1)}, u32[]{:S(2)}, u32[]{:S(2)}) collective-permute-start(bf16[4,192,256]{2,1,0:T(8,128)(2,1)S(1)} %collective-permute-done.6.over), channel_id=1, source_target_pairs={{0,16},{2,18},{4,20},{6,22},{1,17},{3,19},{5,21},{7,23},{16,0},{18... | collective-permute-start | bytes 1179656 | tf_op jit(solution)/shard_map/ppermute | solution.py:47
  39.8 6.5 %collective-permute-start.14 = (bf16[3,192,256]{2,1,0:T(8,128)(2,1)S(1)}, bf16[3,192,256]{2,1,0:T(8,128)(2,1)S(1)}, u32[]{:S(2)}, u32[]{:S(2)}) collective-permute-start(bf16[3,192,256]{2,1,0:T(8,128)(2,1)S(1)} %slice.17), channel_id=1, source_target_pairs={{0,8},{2,10},{4,12},{6,14},{1,9},{3,11},{5,13},{7,15},{16,24},{18,... | collective-permute-start | bytes 884744 | tf_op jit(solution)/shard_map/ppermute | solution.py:47
  44.9 1.4 %collective-permute-start.12 = (bf16[2,192,256]{2,1,0:T(8,128)(2,1)S(1)}, bf16[2,192,256]{2,1,0:T(8,128)(2,1)S(1)}, u32[]{:S(2)}, u32[]{:S(2)}) collective-permute-start(bf16[2,192,256]{2,1,0:T(8,128)(2,1)S(1)} %get-tuple-element.64), channel_id=1, source_target_pairs={{0,8},{2,10},{4,12},{6,14},{1,9},{3,11},{5,13},{7,15},{16,24},{18,... | collective-permute-start | bytes 589832 | tf_op jit(solution)/shard_map/ppermute | solution.py:47
  44.9 1.4 %collective-permute-start.15 = (f32[1,256]{1,0:T(1,128)S(1)}, f32[1,256]{1,0:T(1,128)S(1)}, u32[]{:S(2)}, u32[]{:S(2)}) collective-permute-start(f32[1,256]{1,0:T(1,128)S(1)} %get-tuple-element.66), channel_id=1, source_target_pairs={{0,8},{2,10},{4,12},{6,14},{1,9},{3,11},{5,13},{7,15},{16,24},{18,... | collective-permute-start | bytes 3080 | tf_op jit(solution)/shard_map/ppermute | solution.py:47
  45.4 2.8 %collective-permute-start.17 = (bf16[4,192,256]{2,1,0:T(8,128)(2,1)S(1)}, bf16[4,192,256]{2,1,0:T(8,128)(2,1)S(1)}, u32[]{:S(2)}, u32[]{:S(2)}) collective-permute-start(bf16[4,192,256]{2,1,0:T(8,128)(2,1)S(1)} %pack.1.own), channel_id=1, source_target_pairs={{0,8},{2,10},{4,12},{6,14},{1,9},{3,11},{5,13},{7,15},{16,24},{18,... | collective-permute-start | bytes 1179656 | tf_op jit(solution)/shard_map/ppermute | solution.py:47
  46.3 2.2 %collective-permute-start.20 = (bf16[4,192,256]{2,1,0:T(8,128)(2,1)S(1)}, bf16[4,192,256]{2,1,0:T(8,128)(2,1)S(1)}, u32[]{:S(2)}, u32[]{:S(2)}) collective-permute-start(bf16[4,192,256]{2,1,0:T(8,128)(2,1)S(1)} %collective-permute-done.7.over_got), channel_id=1, source_target_pairs={{0,8},{2,10},{4,12},{6,14},{1,9},{3,11},{5,13},{7,15},{16,24},{18,... | collective-permute-start | bytes 1179656 | tf_op jit(solution)/shard_map/ppermute | solution.py:47
  46.6 1.8 %collective-permute-start.18 = (bf16[2,192,256]{2,1,0:T(8,128)(2,1)S(1)}, bf16[2,192,256]{2,1,0:T(8,128)(2,1)S(1)}, u32[]{:S(2)}, u32[]{:S(2)}) collective-permute-start(bf16[2,192,256]{2,1,0:T(8,128)(2,1)S(1)} %get-tuple-element.77), channel_id=1, source_target_pairs={{0,8},{2,10},{4,12},{6,14},{1,9},{3,11},{5,13},{7,15},{16,24},{18,... | collective-permute-start | bytes 589832 | tf_op jit(solution)/shard_map/ppermute | solution.py:47
  46.9 1.6 %collective-permute-start.19 = (bf16[1,192,256]{2,1,0:T(8,128)(2,1)S(1)}, bf16[1,192,256]{2,1,0:T(8,128)(2,1)S(1)}, u32[]{:S(2)}, u32[]{:S(2)}) collective-permute-start(bf16[1,192,256]{2,1,0:T(8,128)(2,1)S(1)} %slice.19), channel_id=1, source_target_pairs={{0,8},{2,10},{4,12},{6,14},{1,9},{3,11},{5,13},{7,15},{16,24},{18,... | collective-permute-start | bytes 294920 | tf_op jit(solution)/shard_map/ppermute | solution.py:47
  47.2 5.9 %collective-permute-start.16 = (f32[1,256]{1,0:T(1,128)S(1)}, f32[1,256]{1,0:T(1,128)S(1)}, u32[]{:S(2)}, u32[]{:S(2)}) collective-permute-start(f32[1,256]{1,0:T(1,128)S(1)} %add.17), channel_id=1, source_target_pairs={{0,16},{2,18},{4,20},{6,22},{1,17},{3,19},{5,21},{7,23},{16,0},{18... | collective-permute-start | bytes 3080 | tf_op jit(solution)/shard_map/ppermute | solution.py:47

commit v6 on v5

--- a/solution.py
+++ b/solution.py
@@ -87,7 +87,7 @@
 
 def mine_kernel(
     plan, where, acts_ref, gain_ref, grads_ref, weight_ref,
-    scaled, mine, other, piece, acts, grads, gain, weight, sems, ends,
+    scaled, mine, other, piece, gain, acts, grads, weight, sems, ends,
 ):
     core = where[0]
     tokens = acts.shape[0]
@@ -120,8 +120,7 @@
             piece[...] = weight[:, number * rows : (number + 1) * rows].T
 
 
-def peer_kernel(plan, acts, gain_ref, scaled, gain, end):
-    fetch(gain_ref, gain, end).wait()
+def peer_kernel(plan, acts, gain, scaled):
     scale_rows(acts, gain, scaled, 0, acts.shape[0])
 
 
@@ -353,20 +352,20 @@
 
     peer_acts = plan.send(activations, to_core)
     half_shape = (width * rows, tokens)
-    scaled, mine, other, piece = pl.pallas_call(
+    scaled, mine, other, piece, near_gain = pl.pallas_call(
         functools.partial(mine_kernel, plan),
         out_shape=(
             pltpu.VMEM((tokens, model), BF16),
             pltpu.VMEM(half_shape, BF16),
             pltpu.VMEM(half_shape, BF16),
             pltpu.VMEM((rows, cols), BF16),
+            pltpu.VMEM((1, model), F32),
         ),
         in_specs=[SMEM, HBM, HBM, HBM, HBM],
-        out_specs=[VMEM] * 4,
+        out_specs=[VMEM] * 5,
         scratch_shapes=[
             pltpu.VMEM((tokens, model), BF16),
             pltpu.VMEM((tokens, key_width), BF16),
-            pltpu.VMEM((1, model), F32),
             pltpu.VMEM((cols, key_width), BF16),
             pltpu.SemaphoreType.DMA((CHUNKS,)),
             pltpu.SemaphoreType.DMA((3,)),
@@ -379,13 +378,12 @@
     peer_scaled = pl.pallas_call(
         functools.partial(peer_kernel, plan),
         out_shape=pltpu.VMEM((tokens, model), BF16),
-        in_specs=[VMEM, HBM],
+        in_specs=[VMEM, VMEM],
         out_specs=VMEM,
-        scratch_shapes=[pltpu.VMEM((1, model), F32), pltpu.SemaphoreType.DMA(())],
         compiler_params=params(2),
         cost_estimate=cost(0, 2 * MIB),
         name="peer",
-    )(peer_acts, gain_hbm)
+    )(peer_acts, near_gain)
     theirs, _ = lax.optimization_barrier((theirs, peer_scaled))
     sent, kept, held = pl.pallas_call(
         functools.partial(term_kernel, plan),

time: 53.9 us -> 53.2 us (0.987)
  starting transfers between devices: 20.9 us -> 20 us
  waiting for transfers between devices: 14.8 us -> 15.7 us
  Pallas kernels: 16.6 us -> 15.9 us
    ppermute x21, waiting for transfers between devices: 14.8 us -> 15.7 us  [send(): return lax.ppermute(array, AXES, self.pairs(move))]
    ppermute x21, starting transfers between devices: 20.9 us -> 20 us  [send(): return lax.ppermute(array, AXES, self.pairs(move))]
    pallas_call x1, Pallas kernels: 1.58 us -> 0.89 us  [by_permutes(): pl.pallas_call(functools.partial(peer_kernel, plan), out_shape=pltpu.VMEM...]
  transfers between devices with their start and end apart: 21 -> 21, of which waited for: 11 -> 12; matrix products, arithmetic and copies ran while one was open for 0% -> 0% of each run, Pallas kernels for 26% -> 25%
where the time goes in v6:
time: 53.2 us; the launch traced here: 53 us
  starting transfers between devices  20 us (38%)
  Pallas kernels  15.9 us (30%)
  waiting for transfers between devices  15.7 us (30%)
  between operations  0.76 us (1%)
  other arithmetic  0.65 us (1%)
    ppermute x21, starting transfers between devices, send(): return lax.ppermute(array, AXES, self.pairs(move))  20 us
    ppermute x21, waiting for transfers between devices, send(): return lax.ppermute(array, AXES, self.pairs(move))  15.7 us
    pallas_call x1, Pallas kernels, by_permutes(): pl.pallas_call(functools.partial(grad_kernel, plan), out_shape=shape((tok...  4.56 us
    pallas_call x1, Pallas kernels, by_permutes(): pl.pallas_call(functools.partial(mine_kernel, plan), out_shape=(pltpu.VME...  3.19 us
    pallas_call x1, Pallas kernels, by_permutes(): pl.pallas_call(functools.partial(load_kernel, plan), out_shape=(pltpu.VME...  2.56 us
    pallas_call x1, Pallas kernels, by_permutes(): pl.pallas_call(functools.partial(term_kernel, plan), out_shape=(pltpu.VME...  2.5 us
  transfers between devices with their start and end apart: 21, of which 12 were waited for; matrix products, arithmetic and copies ran while one was open for 0% of the time, Pallas kernels for 25%

profile of v6, /device:TPU:0, one launch (start us, length us, event | category | flops | bytes accessed | tf_op | source)
XLA Modules:
  0.0 53.0 jit_solution(11649999327699000923)
XLA Ops:
  0.6 0.5 collective-permute-start
  1.1 0.1 pad_add_fusion.where
  1.2 3.2 %mine.1 = (bf16[512,2048]{1,0:T(8,128)(2,1)S(1)}, bf16[384,512]{1,0:T(8,128)(2,1)S(1)}, bf16[384,512]{1,0:T(8,128)(2,1)S(1)}, bf16[192,256]{1,0:T(8,128)(2,1)S(1)}, f32[1,2048]{1,0:T(1,128)S(1)}) custom-call(s32[4]{0:T(128)S(1)} %pad_add_fusion.where, bf16[512,2048]{1,0:T(8,128)(2,1)} %acts_ref.3, f32[1,2048]{1,0:T(1,128)} %bitcast.7, ...), custom_call_target="tpu_custom_call" | custom-call | tf_op jit(solution)/shard_map/mine/pallas_call | solution.py:355
  4.4 0.2 collective-permute-start.1
  4.6 0.5 collective-permute-done.acts
  5.1 0.9 %peer.1.peer_scaled = bf16[512,2048]{1,0:T(8,128)(2,1)S(1)} custom-call(bf16[512,2048]{1,0:T(8,128)(2,1)S(1)} %collective-permute-done.acts, f32[1,2048]{1,0:T(1,128)S(1)} %get-tuple-element.43.gain), custom_call_target="tpu_custom_call" | custom-call | tf_op jit(solution)/shard_map/peer/pallas_call | solution.py:378
  6.0 0.2 collective-permute-done.1.theirs
  6.2 2.5 %term.1 = (bf16[8,192,256]{2,1,0:T(8,128)(2,1)S(1)}, f32[4,192,256]{2,1,0:T(8,128)S(1)}, f32[4,192,256]{2,1,0:T(8,128)S(1)}) custom-call(s32[4]{0:T(128)S(1)} %pad_add_fusion.where, bf16[512,2048]{1,0:T(8,128)(2,1)S(1)} %get-tuple-element.42.scaled, bf16[512,2048]{1,0:T(8,128)(2,1)S(1)} %peer.1.peer_scaled, bf16[384,512]{1,0:T(8,128)(2,1)S(1)} %get-tuple-element.44.mine, ...), custom_call_target="tpu_custom_call" | custom-call | tf_op jit(solution)/shard_map/term/pallas_call | solution.py:388
  8.7 2.8 %collective-permute-start.2 = (bf16[8,192,256]{2,1,0:T(8,128)(2,1)S(1)}, bf16[8,192,256]{2,1,0:T(8,128)(2,1)S(1)}, u32[]{:S(2)}, u32[]{:S(2)}) collective-permute-start(bf16[8,192,256]{2,1,0:T(8,128)(2,1)S(1)} %get-tuple-element.48), channel_id=1, source_target_pairs={{0,16},{2,18},{4,20},{6,22},{1,17},{3,19},{5,21},{7,23},{16,0},{18... | collective-permute-start | bytes 2359304 | tf_op jit(solution)/shard_map/ppermute | solution.py:47
  11.5 2.6 %collective-permute-start.3 = (bf16[192,256]{1,0:T(8,128)(2,1)S(1)}, bf16[192,256]{1,0:T(8,128)(2,1)S(1)}, u32[]{:S(2)}, u32[]{:S(2)}) collective-permute-start(bf16[192,256]{1,0:T(8,128)(2,1)S(1)} %get-tuple-element.41.refs_0_), channel_id=1, source_target_pairs={{0,4},{2,6},{4,0},{6,2},{1,5},{3,7},{5,1},{7,3},{16,20},{18,22},{2... | collective-permute-start | bytes 294920 | tf_op jit(solution)/shard_map/ppermute | solution.py:47
  14.1 1.6 %collective-permute-start.4 = (bf16[192,256]{1,0:T(8,128)(2,1)S(1)}, bf16[192,256]{1,0:T(8,128)(2,1)S(1)}, u32[]{:S(2)}, u32[]{:S(2)}) collective-permute-start(bf16[192,256]{1,0:T(8,128)(2,1)S(1)} %get-tuple-element.41.refs_0_), channel_id=1, source_target_pairs={{0,2},{2,0},{4,6},{6,4},{1,3},{3,1},{5,7},{7,5},{16,18},{18,16},{2... | collective-permute-start | bytes 294920 | tf_op jit(solution)/shard_map/ppermute | solution.py:47
  15.7 0.2 collective-permute-start.5
  15.9 2.6 %load.1 = (bf16[2,4,512,256]{3,2,1,0:T(8,128)(2,1)S(1)}, bf16[512,768]{1,0:T(8,128)(2,1)S(1)}, f32[512,128]{1,0:T(8,128)S(1)}) custom-call(s32[4]{0:T(128)S(1)} %pad_add_fusion.where, bf16[512,2048]{1,0:T(8,128)(2,1)} %acts_ref.3, bf16[512,768]{1,0:T(8,128)(2,1)} %grads_ref.3), custom_call_target="tpu_custom_call" | custom-call | tf_op jit(solution)/shard_map/load/pallas_call | solution.py:404
  18.5 0.0 copy-start
  18.5 2.2 %collective-permute-done.3.refs_2_ = bf16[192,256]{1,0:T(8,128)(2,1)S(1)} collective-permute-done((bf16[192,256]{1,0:T(8,128)(2,1)S(1)}, bf16[192,256]{1,0:T(8,128)(2,1)S(1)}, u32[]{:S(2)}, u32[]{:S(2)}) %collective-permute-start.3) | collective-permute-done | bytes 98336 | tf_op jit(solution)/shard_map/ppermute | solution.py:47
  20.7 0.8 %collective-permute-done.2.got_ref = bf16[8,192,256]{2,1,0:T(8,128)(2,1)S(1)} collective-permute-done((bf16[8,192,256]{2,1,0:T(8,128)(2,1)S(1)}, bf16[8,192,256]{2,1,0:T(8,128)(2,1)S(1)}, u32[]{:S(2)}, u32[]{:S(2)}) %collective-permute-start.2) | collective-permute-done | bytes 786464 | tf_op jit(solution)/shard_map/ppermute | solution.py:47
  21.5 0.6 %half.1 = bf16[4,192,256]{2,1,0:T(8,128)(2,1)S(1)} custom-call(s32[4]{0:T(128)S(1)} %pad_add_fusion.where, f32[4,192,256]{2,1,0:T(8,128)S(1)} %get-tuple-element.47.kept, bf16[8,192,256]{2,1,0:T(8,128)(2,1)S(1)} %collective-permute-done.2.got_ref), custom_call_target="tpu_custom_call" | custom-call | tf_op jit(solution)/shard_map/half/pallas_call | solution.py:424
  22.1 0.0 collective-permute-done.4.refs_1_
  22.1 0.4 collective-permute-done.5.refs_3_
  22.6 1.6 %collective-permute-start.8 = (bf16[4,192,256]{2,1,0:T(8,128)(2,1)S(1)}, bf16[4,192,256]{2,1,0:T(8,128)(2,1)S(1)}, u32[]{:S(2)}, u32[]{:S(2)}) collective-permute-start(bf16[4,192,256]{2,1,0:T(8,128)(2,1)S(1)} %half.1), channel_id=1, source_target_pairs={{0,1},{2,3},{4,5},{6,7},{1,0},{3,2},{5,4},{7,6},{16,17},{18,19},{2... | collective-permute-start | bytes 1179656 | tf_op jit(solution)/shard_map/ppermute | solution.py:47
  24.2 0.5 collective-permute-start.6
  24.7 5.7 %collective-permute-done.8.again_ref = bf16[4,192,256]{2,1,0:T(8,128)(2,1)S(1)} collective-permute-done((bf16[4,192,256]{2,1,0:T(8,128)(2,1)S(1)}, bf16[4,192,256]{2,1,0:T(8,128)(2,1)S(1)}, u32[]{:S(2)}, u32[]{:S(2)}) %collective-permute-start.8) | collective-permute-done | bytes 393248 | tf_op jit(solution)/shard_map/ppermute | solution.py:47
  30.3 1.7 %collective-permute-start.13 = (bf16[4,192,256]{2,1,0:T(8,128)(2,1)S(1)}, bf16[4,192,256]{2,1,0:T(8,128)(2,1)S(1)}, u32[]{:S(2)}, u32[]{:S(2)}) collective-permute-start(bf16[4,192,256]{2,1,0:T(8,128)(2,1)S(1)} %pack.1.own), channel_id=1, source_target_pairs={{0,16},{2,18},{4,20},{6,22},{1,17},{3,19},{5,21},{7,23},{16,0},{18... | collective-permute-start | bytes 1179656 | tf_op jit(solution)/shard_map/ppermute | solution.py:47
  32.0 0.8 %plane.1 = (f32[192,256]{1,0:T(8,128)S(1)}, f32[1,256]{1,0:T(1,128)S(1)}, bf16[208,256]{1,0:T(8,128)(2,1)S(1)}, bf16[208,256]{1,0:T(8,128)(2,1)S(1)}, bf16[208,256]{1,0:T(8,128)(2,1)S(1)}) custom-call(s32[4]{0:T(128)S(1)} %pad_add_fusion.where, f32[4,192,256]{2,1,0:T(8,128)S(1)} %get-tuple-element.59.held, ...), custom_call_target="tpu_custom_call" | custom-call | tf_op jit(solution)/shard_map/plane/pallas_call | solution.py:447
  32.8 3.3 %collective-permute-start.10 = (bf16[208,256]{1,0:T(8,128)(2,1)S(1)}, bf16[208,256]{1,0:T(8,128)(2,1)S(1)}, u32[]{:S(2)}, u32[]{:S(2)}) collective-permute-start(bf16[208,256]{1,0:T(8,128)(2,1)S(1)} %get-tuple-element.63), channel_id=1, source_target_pairs={{0,4},{2,6},{4,0},{6,2},{1,5},{3,7},{5,1},{7,3},{16,20},{18,22},{2... | collective-permute-start | bytes 319496 | tf_op jit(solution)/shard_map/ppermute | solution.py:47
  36.1 0.7 %collective-permute-start.11 = (bf16[208,256]{1,0:T(8,128)(2,1)S(1)}, bf16[208,256]{1,0:T(8,128)(2,1)S(1)}, u32[]{:S(2)}, u32[]{:S(2)}) collective-permute-start(bf16[208,256]{1,0:T(8,128)(2,1)S(1)} %get-tuple-element.64), channel_id=1, source_target_pairs={{0,6},{2,4},{4,2},{6,0},{1,7},{3,5},{5,3},{7,1},{16,22},{18,20},{2... | collective-permute-start | bytes 319496 | tf_op jit(solution)/shard_map/ppermute | solution.py:47
  36.8 0.2 collective-permute-start.9
  37.0 0.3 collective-permute-done.6.over
  37.3 1.6 %collective-permute-start.7 = (bf16[4,192,256]{2,1,0:T(8,128)(2,1)S(1)}, bf16[4,192,256]{2,1,0:T(8,128)(2,1)S(1)}, u32[]{:S(2)}, u32[]{:S(2)}) collective-permute-start(bf16[4,192,256]{2,1,0:T(8,128)(2,1)S(1)} %collective-permute-done.6.over), channel_id=1, source_target_pairs={{0,16},{2,18},{4,20},{6,22},{1,17},{3,19},{5,21},{7,23},{16,0},{18... | collective-permute-start | bytes 1179656 | tf_op jit(solution)/shard_map/ppermute | solution.py:47
  38.9 0.0 collective-permute-done.13.own_got
  39.0 0.1 collective-permute-start.14
  39.1 3.8 %collective-permute-done.10.refs_1_ = bf16[208,256]{1,0:T(8,128)(2,1)S(1)} collective-permute-done((bf16[208,256]{1,0:T(8,128)(2,1)S(1)}, bf16[208,256]{1,0:T(8,128)(2,1)S(1)}, u32[]{:S(2)}, u32[]{:S(2)}) %collective-permute-start.10) | collective-permute-done | bytes 106528 | tf_op jit(solution)/shard_map/ppermute | solution.py:47
  42.9 0.0 collective-permute-done.11.refs_2_
  42.9 0.6 %collective-permute-done.9.refs_0_ = bf16[208,256]{1,0:T(8,128)(2,1)S(1)} collective-permute-done((bf16[208,256]{1,0:T(8,128)(2,1)S(1)}, bf16[208,256]{1,0:T(8,128)(2,1)S(1)}, u32[]{:S(2)}, u32[]{:S(2)}) %collective-permute-start.9) | collective-permute-done | bytes 106528 | tf_op jit(solution)/shard_map/ppermute | solution.py:47
  43.5 0.7 %last.1 = (f32[192,256]{1,0:T(8,128)}, f32[1,256]{1,0:T(1,128)S(1)}) custom-call(f32[192,256]{1,0:T(8,128)S(1)} %get-tuple-element.60.sums_ref, f32[1,256]{1,0:T(1,128)S(1)} %get-tuple-element.61.gains_ref, bf16[208,256]{1,0:T(8,128)(2,1)S(1)} %collective-permute-done.9.refs_0_, bf16[208,256]{1,0:T(8,128)(2,1)S(1)} %collective-permute-done.10.refs_1_, ...), custom_call_target="tpu_custom_call" | custom-call | tf_op jit(solution)/shard_map/last/pallas_call | solution.py:461
  44.2 0.0 collective-permute-start.12
  44.2 0.5 collective-permute-start.15
  44.7 0.0 collective-permute-start.17
  44.7 0.9 %collective-permute-done.15 = f32[1,256]{1,0:T(1,128)S(1)} collective-permute-done((f32[1,256]{1,0:T(1,128)S(1)}, f32[1,256]{1,0:T(1,128)S(1)}, u32[]{:S(2)}, u32[]{:S(2)}) %collective-permute-start.15) | collective-permute-done | bytes 1056 | tf_op jit(solution)/shard_map/ppermute | solution.py:47
  45.6 0.0 collective-permute-done.14.peer_own_first
  45.7 0.3 collective-permute-start.20
  45.9 0.3 collective-permute-start.18
  46.2 0.3 collective-permute-start.19
  46.5 1.1 %collective-permute-start.16 = (f32[1,256]{1,0:T(1,128)S(1)}, f32[1,256]{1,0:T(1,128)S(1)}, u32[]{:S(2)}, u32[]{:S(2)}) collective-permute-start(f32[1,256]{1,0:T(1,128)S(1)} %add.17), channel_id=1, source_target_pairs={{0,16},{2,18},{4,20},{6,22},{1,17},{3,19},{5,21},{7,23},{16,0},{18... | collective-permute-start | bytes 3080 | tf_op jit(solution)/shard_map/ppermute | solution.py:47
  47.6 0.2 collective-permute-done.18.peer_first
  47.7 0.1 collective-permute-done.19.peer_own_rest
  47.9 4.6 %grad.1 = bf16[512,2048]{1,0:T(8,128)(2,1)} custom-call(s32[4]{0:T(128)S(1)} %pad_add_fusion.where, bf16[2,4,512,256]{3,2,1,0:T(8,128)(2,1)S(1)} %get-tuple-element.70.acts, f32[1,2048]{1,0:T(1,128)S(1)} %bitcast.9, bf16[512,768]{1,0:T(8,128)(2,1)S(1)} %get-tuple-element.71.grads, f32[512,128]{1,0:T(8,128)S(1)} %get-tuple-element.72.inverse, ...), custom_call_target="tpu_custom_call" | custom-call | tf_op jit(solution)/shard_map/grad/pallas_call | solution.py:483
  52.5 0.6 %add_multiply_fusion = f32[1,256]{1,0:T(1,128)} fusion(f32[1,256]{1,0:T(1,128)S(1)} %add.17, f32[1,256]{1,0:T(1,128)S(1)} %collective-permute-done.16), kind=kLoop, calls=%fused_computation | loop fusion | flops 512 | bytes 3072 | tf_op jit(solution)/shard_map/div | solution.py:503
  (11 shorter events, 0.1 us)
Async XLA Ops:
  0.6 4.5 %collective-permute-start = (bf16[512,2048]{1,0:T(8,128)(2,1)}, bf16[512,2048]{1,0:T(8,128)(2,1)S(1)}, u32[]{:S(2)}, u32[]{:S(2)}) collective-permute-start(bf16[512,2048]{1,0:T(8,128)(2,1)} %acts_ref.3), channel_id=1, source_target_pairs={{0,8},{2,10},{4,12},{6,14},{1,9},{3,11},{5,13},{7,15},{16,24},{18,... | collective-permute-start | bytes 6291464 | tf_op jit(solution)/shard_map/ppermute | solution.py:47
  4.4 1.8 %collective-permute-start.1 = (bf16[384,512]{1,0:T(8,128)(2,1)S(1)}, bf16[384,512]{1,0:T(8,128)(2,1)S(1)}, u32[]{:S(2)}, u32[]{:S(2)}) collective-permute-start(bf16[384,512]{1,0:T(8,128)(2,1)S(1)} %get-tuple-element.45), channel_id=1, source_target_pairs={{0,8},{2,10},{4,12},{6,14},{1,9},{3,11},{5,13},{7,15},{16,24},{18,... | collective-permute-start | bytes 1179656 | tf_op jit(solution)/shard_map/ppermute | solution.py:47
  8.7 12.8 %collective-permute-start.2 = (bf16[8,192,256]{2,1,0:T(8,128)(2,1)S(1)}, bf16[8,192,256]{2,1,0:T(8,128)(2,1)S(1)}, u32[]{:S(2)}, u32[]{:S(2)}) collective-permute-start(bf16[8,192,256]{2,1,0:T(8,128)(2,1)S(1)} %get-tuple-element.48), channel_id=1, source_target_pairs={{0,16},{2,18},{4,20},{6,22},{1,17},{3,19},{5,21},{7,23},{16,0},{18... | collective-permute-start | bytes 2359304 | tf_op jit(solution)/shard_map/ppermute | solution.py:47
  11.5 9.2 %collective-permute-start.3 = (bf16[192,256]{1,0:T(8,128)(2,1)S(1)}, bf16[192,256]{1,0:T(8,128)(2,1)S(1)}, u32[]{:S(2)}, u32[]{:S(2)}) collective-permute-start(bf16[192,256]{1,0:T(8,128)(2,1)S(1)} %get-tuple-element.41.refs_0_), channel_id=1, source_target_pairs={{0,4},{2,6},{4,0},{6,2},{1,5},{3,7},{5,1},{7,3},{16,20},{18,22},{2... | collective-permute-start | bytes 294920 | tf_op jit(solution)/shard_map/ppermute | solution.py:47
  14.1 8.0 %collective-permute-start.4 = (bf16[192,256]{1,0:T(8,128)(2,1)S(1)}, bf16[192,256]{1,0:T(8,128)(2,1)S(1)}, u32[]{:S(2)}, u32[]{:S(2)}) collective-permute-start(bf16[192,256]{1,0:T(8,128)(2,1)S(1)} %get-tuple-element.41.refs_0_), channel_id=1, source_target_pairs={{0,2},{2,0},{4,6},{6,4},{1,3},{3,1},{5,7},{7,5},{16,18},{18,16},{2... | collective-permute-start | bytes 294920 | tf_op jit(solution)/shard_map/ppermute | solution.py:47
  15.7 6.9 %collective-permute-start.5 = (bf16[192,256]{1,0:T(8,128)(2,1)S(1)}, bf16[192,256]{1,0:T(8,128)(2,1)S(1)}, u32[]{:S(2)}, u32[]{:S(2)}) collective-permute-start(bf16[192,256]{1,0:T(8,128)(2,1)S(1)} %get-tuple-element.41.refs_0_), channel_id=1, source_target_pairs={{0,6},{2,4},{4,2},{6,0},{1,7},{3,5},{5,3},{7,1},{16,22},{18,20},{2... | collective-permute-start | bytes 294920 | tf_op jit(solution)/shard_map/ppermute | solution.py:47
  18.5 13.5 %copy-start = (f32[2048]{0:T(1024)S(1)}, f32[2048]{0:T(1024)}, u32[]{:S(2)}) copy-start(f32[2048]{0:T(1024)} %param.5) | copy-start | bytes 24580
  22.6 7.8 %collective-permute-start.8 = (bf16[4,192,256]{2,1,0:T(8,128)(2,1)S(1)}, bf16[4,192,256]{2,1,0:T(8,128)(2,1)S(1)}, u32[]{:S(2)}, u32[]{:S(2)}) collective-permute-start(bf16[4,192,256]{2,1,0:T(8,128)(2,1)S(1)} %half.1), channel_id=1, source_target_pairs={{0,1},{2,3},{4,5},{6,7},{1,0},{3,2},{5,4},{7,6},{16,17},{18,19},{2... | collective-permute-start | bytes 1179656 | tf_op jit(solution)/shard_map/ppermute | solution.py:47
  24.2 13.1 %collective-permute-start.6 = (bf16[4,192,256]{2,1,0:T(8,128)(2,1)S(1)}, bf16[4,192,256]{2,1,0:T(8,128)(2,1)S(1)}, u32[]{:S(2)}, u32[]{:S(2)}) collective-permute-start(bf16[4,192,256]{2,1,0:T(8,128)(2,1)S(1)} %pack.1.own), channel_id=1, source_target_pairs={{0,1},{2,3},{4,5},{6,7},{1,0},{3,2},{5,4},{7,6},{16,17},{18,19},{2... | collective-permute-start | bytes 1179656 | tf_op jit(solution)/shard_map/ppermute | solution.py:47
  30.3 8.6 %collective-permute-start.13 = (bf16[4,192,256]{2,1,0:T(8,128)(2,1)S(1)}, bf16[4,192,256]{2,1,0:T(8,128)(2,1)S(1)}, u32[]{:S(2)}, u32[]{:S(2)}) collective-permute-start(bf16[4,192,256]{2,1,0:T(8,128)(2,1)S(1)} %pack.1.own), channel_id=1, source_target_pairs={{0,16},{2,18},{4,20},{6,22},{1,17},{3,19},{5,21},{7,23},{16,0},{18... | collective-permute-start | bytes 1179656 | tf_op jit(solution)/shard_map/ppermute | solution.py:47
  32.8 10.1 %collective-permute-start.10 = (bf16[208,256]{1,0:T(8,128)(2,1)S(1)}, bf16[208,256]{1,0:T(8,128)(2,1)S(1)}, u32[]{:S(2)}, u32[]{:S(2)}) collective-permute-start(bf16[208,256]{1,0:T(8,128)(2,1)S(1)} %get-tuple-element.63), channel_id=1, source_target_pairs={{0,4},{2,6},{4,0},{6,2},{1,5},{3,7},{5,1},{7,3},{16,20},{18,22},{2... | collective-permute-start | bytes 319496 | tf_op jit(solution)/shard_map/ppermute | solution.py:47
  36.1 6.8 %collective-permute-start.11 = (bf16[208,256]{1,0:T(8,128)(2,1)S(1)}, bf16[208,256]{1,0:T(8,128)(2,1)S(1)}, u32[]{:S(2)}, u32[]{:S(2)}) collective-permute-start(bf16[208,256]{1,0:T(8,128)(2,1)S(1)} %get-tuple-element.64), channel_id=1, source_target_pairs={{0,6},{2,4},{4,2},{6,0},{1,7},{3,5},{5,3},{7,1},{16,22},{18,20},{2... | collective-permute-start | bytes 319496 | tf_op jit(solution)/shard_map/ppermute | solution.py:47
  36.8 6.7 %collective-permute-start.9 = (bf16[208,256]{1,0:T(8,128)(2,1)S(1)}, bf16[208,256]{1,0:T(8,128)(2,1)S(1)}, u32[]{:S(2)}, u32[]{:S(2)}) collective-permute-start(bf16[208,256]{1,0:T(8,128)(2,1)S(1)} %get-tuple-element.62), channel_id=1, source_target_pairs={{0,2},{2,0},{4,6},{6,4},{1,3},{3,1},{5,7},{7,5},{16,18},{18,16},{2... | collective-permute-start | bytes 319496 | tf_op jit(solution)/shard_map/ppermute | solution.py:47
  37.3 8.3 %collective-permute-start.7 = (bf16[4,192,256]{2,1,0:T(8,128)(2,1)S(1)}, bf16[4,192,256]{2,1,0:T(8,128)(2,1)S(1)}, u32[]{:S(2)}, u32[]{:S(2)}) collective-permute-start(bf16[4,192,256]{2,1,0:T(8,128)(2,1)S(1)} %collective-permute-done.6.over), channel_id=1, source_target_pairs={{0,16},{2,18},{4,20},{6,22},{1,17},{3,19},{5,21},{7,23},{16,0},{18... | collective-permute-start | bytes 1179656 | tf_op jit(solution)/shard_map/ppermute | solution.py:47
  39.0 6.7 %collective-permute-start.14 = (bf16[3,192,256]{2,1,0:T(8,128)(2,1)S(1)}, bf16[3,192,256]{2,1,0:T(8,128)(2,1)S(1)}, u32[]{:S(2)}, u32[]{:S(2)}) collective-permute-start(bf16[3,192,256]{2,1,0:T(8,128)(2,1)S(1)} %slice.17), channel_id=1, source_target_pairs={{0,8},{2,10},{4,12},{6,14},{1,9},{3,11},{5,13},{7,15},{16,24},{18,... | collective-permute-start | bytes 884744 | tf_op jit(solution)/shard_map/ppermute | solution.py:47
  44.2 1.4 %collective-permute-start.12 = (bf16[2,192,256]{2,1,0:T(8,128)(2,1)S(1)}, bf16[2,192,256]{2,1,0:T(8,128)(2,1)S(1)}, u32[]{:S(2)}, u32[]{:S(2)}) collective-permute-start(bf16[2,192,256]{2,1,0:T(8,128)(2,1)S(1)} %get-tuple-element.66), channel_id=1, source_target_pairs={{0,8},{2,10},{4,12},{6,14},{1,9},{3,11},{5,13},{7,15},{16,24},{18,... | collective-permute-start | bytes 589832 | tf_op jit(solution)/shard_map/ppermute | solution.py:47
  44.2 1.4 %collective-permute-start.15 = (f32[1,256]{1,0:T(1,128)S(1)}, f32[1,256]{1,0:T(1,128)S(1)}, u32[]{:S(2)}, u32[]{:S(2)}) collective-permute-start(f32[1,256]{1,0:T(1,128)S(1)} %get-tuple-element.68), channel_id=1, source_target_pairs={{0,8},{2,10},{4,12},{6,14},{1,9},{3,11},{5,13},{7,15},{16,24},{18,... | collective-permute-start | bytes 3080 | tf_op jit(solution)/shard_map/ppermute | solution.py:47
  44.7 2.9 %collective-permute-start.17 = (bf16[4,192,256]{2,1,0:T(8,128)(2,1)S(1)}, bf16[4,192,256]{2,1,0:T(8,128)(2,1)S(1)}, u32[]{:S(2)}, u32[]{:S(2)}) collective-permute-start(bf16[4,192,256]{2,1,0:T(8,128)(2,1)S(1)} %pack.1.own), channel_id=1, source_target_pairs={{0,8},{2,10},{4,12},{6,14},{1,9},{3,11},{5,13},{7,15},{16,24},{18,... | collective-permute-start | bytes 1179656 | tf_op jit(solution)/shard_map/ppermute | solution.py:47
  45.7 2.2 %collective-permute-start.20 = (bf16[4,192,256]{2,1,0:T(8,128)(2,1)S(1)}, bf16[4,192,256]{2,1,0:T(8,128)(2,1)S(1)}, u32[]{:S(2)}, u32[]{:S(2)}) collective-permute-start(bf16[4,192,256]{2,1,0:T(8,128)(2,1)S(1)} %collective-permute-done.7.over_got), channel_id=1, source_target_pairs={{0,8},{2,10},{4,12},{6,14},{1,9},{3,11},{5,13},{7,15},{16,24},{18,... | collective-permute-start | bytes 1179656 | tf_op jit(solution)/shard_map/ppermute | solution.py:47
  45.9 1.8 %collective-permute-start.18 = (bf16[2,192,256]{2,1,0:T(8,128)(2,1)S(1)}, bf16[2,192,256]{2,1,0:T(8,128)(2,1)S(1)}, u32[]{:S(2)}, u32[]{:S(2)}) collective-permute-start(bf16[2,192,256]{2,1,0:T(8,128)(2,1)S(1)} %get-tuple-element.79), channel_id=1, source_target_pairs={{0,8},{2,10},{4,12},{6,14},{1,9},{3,11},{5,13},{7,15},{16,24},{18,... | collective-permute-start | bytes 589832 | tf_op jit(solution)/shard_map/ppermute | solution.py:47
  46.2 1.6 %collective-permute-start.19 = (bf16[1,192,256]{2,1,0:T(8,128)(2,1)S(1)}, bf16[1,192,256]{2,1,0:T(8,128)(2,1)S(1)}, u32[]{:S(2)}, u32[]{:S(2)}) collective-permute-start(bf16[1,192,256]{2,1,0:T(8,128)(2,1)S(1)} %slice.19), channel_id=1, source_target_pairs={{0,8},{2,10},{4,12},{6,14},{1,9},{3,11},{5,13},{7,15},{16,24},{18,... | collective-permute-start | bytes 294920 | tf_op jit(solution)/shard_map/ppermute | solution.py:47
  46.5 5.9 %collective-permute-start.16 = (f32[1,256]{1,0:T(1,128)S(1)}, f32[1,256]{1,0:T(1,128)S(1)}, u32[]{:S(2)}, u32[]{:S(2)}) collective-permute-start(f32[1,256]{1,0:T(1,128)S(1)} %add.17), channel_id=1, source_target_pairs={{0,16},{2,18},{4,20},{6,22},{1,17},{3,19},{5,21},{7,23},{16,0},{18... | collective-permute-start | bytes 3080 | tf_op jit(solution)/shard_map/ppermute | solution.py:47

commit v7 on v6

--- a/solution.py
+++ b/solution.py
@@ -245,8 +245,30 @@
             weight[pl.ds(flip * depth + step, 1), here] = blocks[part * depth + step][...][None]
 
 
+def early_kernel(plan, where, grads, own, over, own_got, peer_own, partial, late_grads, weight):
+    core, y = where[0], where[1]
+    depth, rows = own.shape[:2]
+
+    def place(grp, step, block):
+        weight[step, pl.ds(pl.multiple_of(grp * rows, rows), rows)] = block
+
+    missing = (1 - y) * 2 + 1 - core
+    for step in range(depth):
+        third = jnp.where(core == 0, own_got[step].astype(F32), over[step].astype(F32))
+        place(y * 2 + core, step, own[step])
+        place(y * 2 + 1 - core, step, peer_own[step])
+        place((1 - y) * 2 + core, step, third.astype(BF16))
+        place(missing, step, jnp.zeros(third.shape, BF16))
+        partial[step] = jnp.dot(grads[...], weight[step], preferred_element_type=F32)
+    for number in range(plan.groups):
+
+        @pl.when(missing == number)
+        def _():
+            late_grads[...] = grads[:, number * rows : (number + 1) * rows]
+
+
 def grad_kernel(
-    plan, where, acts, gain_ref, grads, inverse,
+    plan, where, acts, gain_ref, grads, inverse, partial, late_grads,
     own, over, own_got, over_got, peer_own, peer_first, peer_over, peer_own_first, peer_own_rest, peer_over_got,
     out_ref, weight, grad_scaled, mean_ref, out, ends,
 ):
@@ -261,7 +283,14 @@
     blocks = [(flip, step) for flip in range(2) for step in range(depth)]
 
     def multiply(number):
-        grad_scaled[number] = jnp.dot(grads[...], weight[number], preferred_element_type=F32)
+        if number < depth:
+            rows = late_grads.shape[1]
+            missing = (1 - where[1]) * 2 + 1 - core
+            block = weight[number, pl.ds(pl.multiple_of(missing * rows, rows), rows)]
+            late = jnp.dot(late_grads[...], block, preferred_element_type=F32)
+            grad_scaled[number] = partial[number] + late
+        else:
+            grad_scaled[number] = jnp.dot(grads[...], weight[number], preferred_element_type=F32)
 
     def add_mean(number):
         flip, step = blocks[number]
@@ -455,9 +484,21 @@
         name="plane",
     )(where, held, got, own, again, gain)
     gots = [plan.send(array, to_z(step + 1)) for step, array in enumerate(sents)]
-    first, _ = lax.optimization_barrier((own, again))
+    peer_own = plan.send(own, to_core)
+    first, _, peer_own = lax.optimization_barrier((own, again, peer_own))
     own_got = plan.send(first, y_then)
     over_got = plan.send(over, y_then)
+    partial, late_grads = pl.pallas_call(
+        functools.partial(early_kernel, plan),
+        out_shape=(pltpu.VMEM((depth, tokens, cols), F32), pltpu.VMEM((tokens, rows), BF16)),
+        in_specs=[SMEM] + [VMEM] * 5,
+        out_specs=[VMEM] * 2,
+        scratch_shapes=[pltpu.VMEM((depth, key_width, cols), BF16)],
+        compiler_params=params(5),
+        cost_estimate=cost(0, MIB),
+        name="early",
+    )(where, grads, own, over, own_got, peer_own)
+    gots, partial = lax.optimization_barrier((gots, partial))
     weight_grads, gains = pl.pallas_call(
         functools.partial(last_kernel, plan),
         out_shape=(shape((rows, cols), F32), pltpu.VMEM((1, cols), F32)),
@@ -467,7 +508,6 @@
         cost_estimate=cost(0, MIB),
         name="last",
     )(sums, gains, *gots)
-    peer_own = plan.send(own, to_core)
     peer_first = plan.send(over[: 2 * EARLY], to_core)
     rest, gains = lax.optimization_barrier((over[2 * EARLY :], gains))
     peer_over = plan.send(rest, to_core)
@@ -483,7 +523,7 @@
     input_grads = pl.pallas_call(
         functools.partial(grad_kernel, plan),
         out_shape=shape((tokens, model), BF16),
-        in_specs=[SMEM] + [VMEM] * 14,
+        in_specs=[SMEM] + [VMEM] * 16,
         out_specs=HBM,
         scratch_shapes=[
             pltpu.VMEM((2 * depth, key_width, cols), BF16),
@@ -496,7 +536,7 @@
         cost_estimate=cost(2 * tokens * model * key_width, 8 * MIB),
         name="grad",
     )(
-        where, acts, gain, grads, inverse,
+        where, acts, gain, grads, inverse, partial, late_grads,
         own, over, own_got, over_got, peer_own, peer_first, peer_over, peer_own_first, peer_own_rest, peer_over_got,
     )
     peer_gains, input_grads = lax.optimization_barrier((peer_gains, input_grads))

time: 53.2 us -> 53.4 us (level)
  waiting for transfers between devices: 15.7 us -> 13.8 us
  Pallas kernels: 15.9 us -> 17.2 us
  starting transfers between devices: 20 us -> 20.7 us
    ppermute x21, waiting for transfers between devices: 15.7 us -> 13.8 us  [send(): return lax.ppermute(array, AXES, self.pairs(move))]
    pallas_call x0 -> x1, Pallas kernels: none -> 1.8 us  [by_permutes(): pl.pallas_call(functools.partial(early_kernel, plan), out_shape=(pltpu.VM...]
    ppermute x21, starting transfers between devices: 20 us -> 20.7 us  [send(): return lax.ppermute(array, AXES, self.pairs(move))]
  transfers between devices with their start and end apart: 21 -> 21, of which waited for: 12 -> 10; matrix products, arithmetic and copies ran while one was open for 0% -> 0% of each run, Pallas kernels for 25% -> 28%
where the time goes in v7:
time: 53.4 us; the launch traced here: 53.2 us
  starting transfers between devices  20.7 us (39%)
  Pallas kernels  17.2 us (32%)
  waiting for transfers between devices  13.8 us (26%)
  between operations  0.76 us (1%)
  other arithmetic  0.65 us (1%)
    ppermute x21, starting transfers between devices, send(): return lax.ppermute(array, AXES, self.pairs(move))  20.7 us
    ppermute x21, waiting for transfers between devices, send(): return lax.ppermute(array, AXES, self.pairs(move))  13.8 us
    pallas_call x1, Pallas kernels, by_permutes(): pl.pallas_call(functools.partial(grad_kernel, plan), out_shape=shape((tok...  4.06 us
    pallas_call x1, Pallas kernels, by_permutes(): pl.pallas_call(functools.partial(mine_kernel, plan), out_shape=(pltpu.VME...  3.19 us
    pallas_call x1, Pallas kernels, by_permutes(): pl.pallas_call(functools.partial(load_kernel, plan), out_shape=(pltpu.VME...  2.57 us
    pallas_call x1, Pallas kernels, by_permutes(): pl.pallas_call(functools.partial(term_kernel, plan), out_shape=(pltpu.VME...  2.5 us
    pallas_call x1, Pallas kernels, by_permutes(): pl.pallas_call(functools.partial(early_kernel, plan), out_shape=(pltpu.VM...  1.8 us
  transfers between devices with their start and end apart: 21, of which 10 were waited for; matrix products, arithmetic and copies ran while one was open for 0% of the time, Pallas kernels for 28%

profile of v7, /device:TPU:0, one launch (start us, length us, event | category | flops | bytes accessed | tf_op | source)
XLA Modules:
  0.0 53.2 jit_solution(16476463338118152933)
XLA Ops:
  0.6 0.5 collective-permute-start
  1.1 0.1 pad_add_fusion.where
  1.2 3.2 %mine.1 = (bf16[512,2048]{1,0:T(8,128)(2,1)S(1)}, bf16[384,512]{1,0:T(8,128)(2,1)S(1)}, bf16[384,512]{1,0:T(8,128)(2,1)S(1)}, bf16[192,256]{1,0:T(8,128)(2,1)S(1)}, f32[1,2048]{1,0:T(1,128)S(1)}) custom-call(s32[4]{0:T(128)S(1)} %pad_add_fusion.where, bf16[512,2048]{1,0:T(8,128)(2,1)} %acts_ref.3, f32[1,2048]{1,0:T(1,128)} %bitcast.7, ...), custom_call_target="tpu_custom_call" | custom-call | tf_op jit(solution)/shard_map/mine/pallas_call | solution.py:384
  4.4 0.2 collective-permute-start.1
  4.6 0.5 collective-permute-done.acts
  5.1 0.9 %peer.1.peer_scaled = bf16[512,2048]{1,0:T(8,128)(2,1)S(1)} custom-call(bf16[512,2048]{1,0:T(8,128)(2,1)S(1)} %collective-permute-done.acts, f32[1,2048]{1,0:T(1,128)S(1)} %get-tuple-element.50.gain), custom_call_target="tpu_custom_call" | custom-call | tf_op jit(solution)/shard_map/peer/pallas_call | solution.py:407
  6.0 0.2 collective-permute-done.1.theirs
  6.2 2.5 %term.1 = (bf16[8,192,256]{2,1,0:T(8,128)(2,1)S(1)}, f32[4,192,256]{2,1,0:T(8,128)S(1)}, f32[4,192,256]{2,1,0:T(8,128)S(1)}) custom-call(s32[4]{0:T(128)S(1)} %pad_add_fusion.where, bf16[512,2048]{1,0:T(8,128)(2,1)S(1)} %get-tuple-element.49.scaled, bf16[512,2048]{1,0:T(8,128)(2,1)S(1)} %peer.1.peer_scaled, bf16[384,512]{1,0:T(8,128)(2,1)S(1)} %get-tuple-element.51.mine, ...), custom_call_target="tpu_custom_call" | custom-call | tf_op jit(solution)/shard_map/term/pallas_call | solution.py:417
  8.7 2.8 %collective-permute-start.2 = (bf16[8,192,256]{2,1,0:T(8,128)(2,1)S(1)}, bf16[8,192,256]{2,1,0:T(8,128)(2,1)S(1)}, u32[]{:S(2)}, u32[]{:S(2)}) collective-permute-start(bf16[8,192,256]{2,1,0:T(8,128)(2,1)S(1)} %get-tuple-element.55), channel_id=1, source_target_pairs={{0,16},{2,18},{4,20},{6,22},{1,17},{3,19},{5,21},{7,23},{16,0},{18... | collective-permute-start | bytes 2359304 | tf_op jit(solution)/shard_map/ppermute | solution.py:47
  11.5 2.6 %collective-permute-start.3 = (bf16[192,256]{1,0:T(8,128)(2,1)S(1)}, bf16[192,256]{1,0:T(8,128)(2,1)S(1)}, u32[]{:S(2)}, u32[]{:S(2)}) collective-permute-start(bf16[192,256]{1,0:T(8,128)(2,1)S(1)} %get-tuple-element.48.refs_0_), channel_id=1, source_target_pairs={{0,4},{2,6},{4,0},{6,2},{1,5},{3,7},{5,1},{7,3},{16,20},{18,22},{2... | collective-permute-start | bytes 294920 | tf_op jit(solution)/shard_map/ppermute | solution.py:47
  14.1 1.6 %collective-permute-start.4 = (bf16[192,256]{1,0:T(8,128)(2,1)S(1)}, bf16[192,256]{1,0:T(8,128)(2,1)S(1)}, u32[]{:S(2)}, u32[]{:S(2)}) collective-permute-start(bf16[192,256]{1,0:T(8,128)(2,1)S(1)} %get-tuple-element.48.refs_0_), channel_id=1, source_target_pairs={{0,2},{2,0},{4,6},{6,4},{1,3},{3,1},{5,7},{7,5},{16,18},{18,16},{2... | collective-permute-start | bytes 294920 | tf_op jit(solution)/shard_map/ppermute | solution.py:47
  15.7 0.2 collective-permute-start.5
  15.9 2.6 %load.1 = (bf16[2,4,512,256]{3,2,1,0:T(8,128)(2,1)S(1)}, bf16[512,768]{1,0:T(8,128)(2,1)S(1)}, f32[512,128]{1,0:T(8,128)S(1)}) custom-call(s32[4]{0:T(128)S(1)} %pad_add_fusion.where, bf16[512,2048]{1,0:T(8,128)(2,1)} %acts_ref.3, bf16[512,768]{1,0:T(8,128)(2,1)} %grads_ref.3), custom_call_target="tpu_custom_call" | custom-call | tf_op jit(solution)/shard_map/load/pallas_call | solution.py:433
  18.5 0.0 copy-start
  18.5 2.2 %collective-permute-done.3.refs_2_ = bf16[192,256]{1,0:T(8,128)(2,1)S(1)} collective-permute-done((bf16[192,256]{1,0:T(8,128)(2,1)S(1)}, bf16[192,256]{1,0:T(8,128)(2,1)S(1)}, u32[]{:S(2)}, u32[]{:S(2)}) %collective-permute-start.3) | collective-permute-done | bytes 98336 | tf_op jit(solution)/shard_map/ppermute | solution.py:47
  20.7 0.8 %collective-permute-done.2.got_ref = bf16[8,192,256]{2,1,0:T(8,128)(2,1)S(1)} collective-permute-done((bf16[8,192,256]{2,1,0:T(8,128)(2,1)S(1)}, bf16[8,192,256]{2,1,0:T(8,128)(2,1)S(1)}, u32[]{:S(2)}, u32[]{:S(2)}) %collective-permute-start.2) | collective-permute-done | bytes 786464 | tf_op jit(solution)/shard_map/ppermute | solution.py:47
  21.5 0.6 %half.1 = bf16[4,192,256]{2,1,0:T(8,128)(2,1)S(1)} custom-call(s32[4]{0:T(128)S(1)} %pad_add_fusion.where, f32[4,192,256]{2,1,0:T(8,128)S(1)} %get-tuple-element.54.kept, bf16[8,192,256]{2,1,0:T(8,128)(2,1)S(1)} %collective-permute-done.2.got_ref), custom_call_target="tpu_custom_call" | custom-call | tf_op jit(solution)/shard_map/half/pallas_call | solution.py:453
  22.1 0.0 collective-permute-done.4.refs_1_
  22.1 0.4 collective-permute-done.5.refs_3_
  22.6 0.1 collective-permute-start.12
  22.7 1.7 %collective-permute-start.8 = (bf16[4,192,256]{2,1,0:T(8,128)(2,1)S(1)}, bf16[4,192,256]{2,1,0:T(8,128)(2,1)S(1)}, u32[]{:S(2)}, u32[]{:S(2)}) collective-permute-start(bf16[4,192,256]{2,1,0:T(8,128)(2,1)S(1)} %half.1), channel_id=1, source_target_pairs={{0,1},{2,3},{4,5},{6,7},{1,0},{3,2},{5,4},{7,6},{16,17},{18,19},{2... | collective-permute-start | bytes 1179656 | tf_op jit(solution)/shard_map/ppermute | solution.py:47
  24.3 0.4 collective-permute-start.6
  24.8 0.0 collective-permute-done.12.peer_own
  24.8 5.7 %collective-permute-done.8.again_ref = bf16[4,192,256]{2,1,0:T(8,128)(2,1)S(1)} collective-permute-done((bf16[4,192,256]{2,1,0:T(8,128)(2,1)S(1)}, bf16[4,192,256]{2,1,0:T(8,128)(2,1)S(1)}, u32[]{:S(2)}, u32[]{:S(2)}) %collective-permute-start.8) | collective-permute-done | bytes 393248 | tf_op jit(solution)/shard_map/ppermute | solution.py:47
  30.5 1.6 %collective-permute-start.13 = (bf16[4,192,256]{2,1,0:T(8,128)(2,1)S(1)}, bf16[4,192,256]{2,1,0:T(8,128)(2,1)S(1)}, u32[]{:S(2)}, u32[]{:S(2)}) collective-permute-start(bf16[4,192,256]{2,1,0:T(8,128)(2,1)S(1)} %pack.1.own), channel_id=1, source_target_pairs={{0,16},{2,18},{4,20},{6,22},{1,17},{3,19},{5,21},{7,23},{16,0},{18... | collective-permute-start | bytes 1179656 | tf_op jit(solution)/shard_map/ppermute | solution.py:47
  32.1 0.8 %plane.1 = (f32[192,256]{1,0:T(8,128)S(1)}, f32[1,256]{1,0:T(1,128)S(1)}, bf16[208,256]{1,0:T(8,128)(2,1)S(1)}, bf16[208,256]{1,0:T(8,128)(2,1)S(1)}, bf16[208,256]{1,0:T(8,128)(2,1)S(1)}) custom-call(s32[4]{0:T(128)S(1)} %pad_add_fusion.where, f32[4,192,256]{2,1,0:T(8,128)S(1)} %get-tuple-element.66.held, ...), custom_call_target="tpu_custom_call" | custom-call | tf_op jit(solution)/shard_map/plane/pallas_call | solution.py:476
  32.9 3.4 %collective-permute-start.10 = (bf16[208,256]{1,0:T(8,128)(2,1)S(1)}, bf16[208,256]{1,0:T(8,128)(2,1)S(1)}, u32[]{:S(2)}, u32[]{:S(2)}) collective-permute-start(bf16[208,256]{1,0:T(8,128)(2,1)S(1)} %get-tuple-element.70), channel_id=1, source_target_pairs={{0,4},{2,6},{4,0},{6,2},{1,5},{3,7},{5,1},{7,3},{16,20},{18,22},{2... | collective-permute-start | bytes 319496 | tf_op jit(solution)/shard_map/ppermute | solution.py:47
  36.3 0.6 %collective-permute-start.11 = (bf16[208,256]{1,0:T(8,128)(2,1)S(1)}, bf16[208,256]{1,0:T(8,128)(2,1)S(1)}, u32[]{:S(2)}, u32[]{:S(2)}) collective-permute-start(bf16[208,256]{1,0:T(8,128)(2,1)S(1)} %get-tuple-element.71), channel_id=1, source_target_pairs={{0,6},{2,4},{4,2},{6,0},{1,7},{3,5},{5,3},{7,1},{16,22},{18,20},{2... | collective-permute-start | bytes 319496 | tf_op jit(solution)/shard_map/ppermute | solution.py:47
  36.9 0.2 collective-permute-start.9
  37.2 0.0 collective-permute-done.6.over
  37.2 1.2 %collective-permute-start.7 = (bf16[4,192,256]{2,1,0:T(8,128)(2,1)S(1)}, bf16[4,192,256]{2,1,0:T(8,128)(2,1)S(1)}, u32[]{:S(2)}, u32[]{:S(2)}) collective-permute-start(bf16[4,192,256]{2,1,0:T(8,128)(2,1)S(1)} %collective-permute-done.6.over), channel_id=1, source_target_pairs={{0,16},{2,18},{4,20},{6,22},{1,17},{3,19},{5,21},{7,23},{16,0},{18... | collective-permute-start | bytes 1179656 | tf_op jit(solution)/shard_map/ppermute | solution.py:47
  38.3 0.1 collective-permute-done.13.own_got
  38.4 0.7 %collective-permute-start.15 = (bf16[3,192,256]{2,1,0:T(8,128)(2,1)S(1)}, bf16[3,192,256]{2,1,0:T(8,128)(2,1)S(1)}, u32[]{:S(2)}, u32[]{:S(2)}) collective-permute-start(bf16[3,192,256]{2,1,0:T(8,128)(2,1)S(1)} %slice.17), channel_id=1, source_target_pairs={{0,8},{2,10},{4,12},{6,14},{1,9},{3,11},{5,13},{7,15},{16,24},{18,... | collective-permute-start | bytes 884744 | tf_op jit(solution)/shard_map/ppermute | solution.py:47
  39.2 1.8 %early.1 = (f32[4,512,256]{2,1,0:T(8,128)S(1)}, bf16[512,192]{1,0:T(8,128)(2,1)S(1)}) custom-call(s32[4]{0:T(128)S(1)} %pad_add_fusion.where, bf16[512,768]{1,0:T(8,128)(2,1)S(1)} %get-tuple-element.72.grads, bf16[4,192,256]{2,1,0:T(8,128)(2,1)S(1)} %pack.1.own, bf16[4,192,256]{2,1,0:T(8,128)(2,1)S(1)} %collective-permute-done.6.over, ...), custom_call_target="tpu_custom_call" | custom-call | tf_op jit(solution)/shard_map/early/pallas_call | solution.py:491
  41.0 2.6 %collective-permute-done.10.refs_1_ = bf16[208,256]{1,0:T(8,128)(2,1)S(1)} collective-permute-done((bf16[208,256]{1,0:T(8,128)(2,1)S(1)}, bf16[208,256]{1,0:T(8,128)(2,1)S(1)}, u32[]{:S(2)}, u32[]{:S(2)}) %collective-permute-start.10) | collective-permute-done | bytes 106528 | tf_op jit(solution)/shard_map/ppermute | solution.py:47
  43.6 0.0 collective-permute-done.11.refs_2_
  43.6 0.3 collective-permute-done.9.refs_0_
  43.9 0.7 %last.1 = (f32[192,256]{1,0:T(8,128)}, f32[1,256]{1,0:T(1,128)S(1)}) custom-call(f32[192,256]{1,0:T(8,128)S(1)} %get-tuple-element.67.sums_ref, f32[1,256]{1,0:T(1,128)S(1)} %get-tuple-element.68.gains_ref, bf16[208,256]{1,0:T(8,128)(2,1)S(1)} %collective-permute-done.9.refs_0_, bf16[208,256]{1,0:T(8,128)(2,1)S(1)} %collective-permute-done.10.refs_1_, ...), custom_call_target="tpu_custom_call" | custom-call | tf_op jit(solution)/shard_map/last/pallas_call | solution.py:502
  44.7 0.5 collective-permute-start.16
  45.2 0.9 %collective-permute-done.16 = f32[1,256]{1,0:T(1,128)S(1)} collective-permute-done((f32[1,256]{1,0:T(1,128)S(1)}, f32[1,256]{1,0:T(1,128)S(1)}, u32[]{:S(2)}, u32[]{:S(2)}) %collective-permute-start.16) | collective-permute-done | bytes 1056 | tf_op jit(solution)/shard_map/ppermute | solution.py:47
  46.1 0.0 collective-permute-done.14.peer_over
  46.1 0.3 collective-permute-start.20
  46.4 0.3 collective-permute-start.18
  46.7 0.3 collective-permute-start.19
  47.0 1.6 %collective-permute-start.17 = (f32[1,256]{1,0:T(1,128)S(1)}, f32[1,256]{1,0:T(1,128)S(1)}, u32[]{:S(2)}, u32[]{:S(2)}) collective-permute-start(f32[1,256]{1,0:T(1,128)S(1)} %add.17), channel_id=1, source_target_pairs={{0,16},{2,18},{4,20},{6,22},{1,17},{3,19},{5,21},{7,23},{16,0},{18... | collective-permute-start | bytes 3080 | tf_op jit(solution)/shard_map/ppermute | solution.py:47
  48.6 4.1 %grad.1 = bf16[512,2048]{1,0:T(8,128)(2,1)} custom-call(s32[4]{0:T(128)S(1)} %pad_add_fusion.where, bf16[2,4,512,256]{3,2,1,0:T(8,128)(2,1)S(1)} %get-tuple-element.83.acts, f32[1,2048]{1,0:T(1,128)S(1)} %bitcast.9, bf16[512,768]{1,0:T(8,128)(2,1)S(1)} %get-tuple-element.72.grads, f32[512,128]{1,0:T(8,128)S(1)} %get-tuple-element.84.inverse, ...), custom_call_target="tpu_custom_call" | custom-call | tf_op jit(solution)/shard_map/grad/pallas_call | solution.py:523
  52.6 0.0 collective-permute-done.17
  52.6 0.6 %add_multiply_fusion = f32[1,256]{1,0:T(1,128)} fusion(f32[1,256]{1,0:T(1,128)S(1)} %add.17, f32[1,256]{1,0:T(1,128)S(1)} %collective-permute-done.17), kind=kLoop, calls=%fused_computation | loop fusion | flops 512 | bytes 3072 | tf_op jit(solution)/shard_map/div | solution.py:543
  (12 shorter events, 0.1 us)
Async XLA Ops:
  0.6 4.5 %collective-permute-start = (bf16[512,2048]{1,0:T(8,128)(2,1)}, bf16[512,2048]{1,0:T(8,128)(2,1)S(1)}, u32[]{:S(2)}, u32[]{:S(2)}) collective-permute-start(bf16[512,2048]{1,0:T(8,128)(2,1)} %acts_ref.3), channel_id=1, source_target_pairs={{0,8},{2,10},{4,12},{6,14},{1,9},{3,11},{5,13},{7,15},{16,24},{18,... | collective-permute-start | bytes 6291464 | tf_op jit(solution)/shard_map/ppermute | solution.py:47
  4.4 1.8 %collective-permute-start.1 = (bf16[384,512]{1,0:T(8,128)(2,1)S(1)}, bf16[384,512]{1,0:T(8,128)(2,1)S(1)}, u32[]{:S(2)}, u32[]{:S(2)}) collective-permute-start(bf16[384,512]{1,0:T(8,128)(2,1)S(1)} %get-tuple-element.52), channel_id=1, source_target_pairs={{0,8},{2,10},{4,12},{6,14},{1,9},{3,11},{5,13},{7,15},{16,24},{18,... | collective-permute-start | bytes 1179656 | tf_op jit(solution)/shard_map/ppermute | solution.py:47
  8.7 12.8 %collective-permute-start.2 = (bf16[8,192,256]{2,1,0:T(8,128)(2,1)S(1)}, bf16[8,192,256]{2,1,0:T(8,128)(2,1)S(1)}, u32[]{:S(2)}, u32[]{:S(2)}) collective-permute-start(bf16[8,192,256]{2,1,0:T(8,128)(2,1)S(1)} %get-tuple-element.55), channel_id=1, source_target_pairs={{0,16},{2,18},{4,20},{6,22},{1,17},{3,19},{5,21},{7,23},{16,0},{18... | collective-permute-start | bytes 2359304 | tf_op jit(solution)/shard_map/ppermute | solution.py:47
  11.5 9.2 %collective-permute-start.3 = (bf16[192,256]{1,0:T(8,128)(2,1)S(1)}, bf16[192,256]{1,0:T(8,128)(2,1)S(1)}, u32[]{:S(2)}, u32[]{:S(2)}) collective-permute-start(bf16[192,256]{1,0:T(8,128)(2,1)S(1)} %get-tuple-element.48.refs_0_), channel_id=1, source_target_pairs={{0,4},{2,6},{4,0},{6,2},{1,5},{3,7},{5,1},{7,3},{16,20},{18,22},{2... | collective-permute-start | bytes 294920 | tf_op jit(solution)/shard_map/ppermute | solution.py:47
  14.1 8.0 %collective-permute-start.4 = (bf16[192,256]{1,0:T(8,128)(2,1)S(1)}, bf16[192,256]{1,0:T(8,128)(2,1)S(1)}, u32[]{:S(2)}, u32[]{:S(2)}) collective-permute-start(bf16[192,256]{1,0:T(8,128)(2,1)S(1)} %get-tuple-element.48.refs_0_), channel_id=1, source_target_pairs={{0,2},{2,0},{4,6},{6,4},{1,3},{3,1},{5,7},{7,5},{16,18},{18,16},{2... | collective-permute-start | bytes 294920 | tf_op jit(solution)/shard_map/ppermute | solution.py:47
  15.7 6.9 %collective-permute-start.5 = (bf16[192,256]{1,0:T(8,128)(2,1)S(1)}, bf16[192,256]{1,0:T(8,128)(2,1)S(1)}, u32[]{:S(2)}, u32[]{:S(2)}) collective-permute-start(bf16[192,256]{1,0:T(8,128)(2,1)S(1)} %get-tuple-element.48.refs_0_), channel_id=1, source_target_pairs={{0,6},{2,4},{4,2},{6,0},{1,7},{3,5},{5,3},{7,1},{16,22},{18,20},{2... | collective-permute-start | bytes 294920 | tf_op jit(solution)/shard_map/ppermute | solution.py:47
  18.5 13.6 %copy-start = (f32[2048]{0:T(1024)S(1)}, f32[2048]{0:T(1024)}, u32[]{:S(2)}) copy-start(f32[2048]{0:T(1024)} %param.5) | copy-start | bytes 24580
  22.6 2.2 %collective-permute-start.12 = (bf16[4,192,256]{2,1,0:T(8,128)(2,1)S(1)}, bf16[4,192,256]{2,1,0:T(8,128)(2,1)S(1)}, u32[]{:S(2)}, u32[]{:S(2)}) collective-permute-start(bf16[4,192,256]{2,1,0:T(8,128)(2,1)S(1)} %pack.1.own), channel_id=1, source_target_pairs={{0,8},{2,10},{4,12},{6,14},{1,9},{3,11},{5,13},{7,15},{16,24},{18,... | collective-permute-start | bytes 1179656 | tf_op jit(solution)/shard_map/ppermute | solution.py:47
  22.7 7.8 %collective-permute-start.8 = (bf16[4,192,256]{2,1,0:T(8,128)(2,1)S(1)}, bf16[4,192,256]{2,1,0:T(8,128)(2,1)S(1)}, u32[]{:S(2)}, u32[]{:S(2)}) collective-permute-start(bf16[4,192,256]{2,1,0:T(8,128)(2,1)S(1)} %half.1), channel_id=1, source_target_pairs={{0,1},{2,3},{4,5},{6,7},{1,0},{3,2},{5,4},{7,6},{16,17},{18,19},{2... | collective-permute-start | bytes 1179656 | tf_op jit(solution)/shard_map/ppermute | solution.py:47
  24.3 12.8 %collective-permute-start.6 = (bf16[4,192,256]{2,1,0:T(8,128)(2,1)S(1)}, bf16[4,192,256]{2,1,0:T(8,128)(2,1)S(1)}, u32[]{:S(2)}, u32[]{:S(2)}) collective-permute-start(bf16[4,192,256]{2,1,0:T(8,128)(2,1)S(1)} %pack.1.own), channel_id=1, source_target_pairs={{0,1},{2,3},{4,5},{6,7},{1,0},{3,2},{5,4},{7,6},{16,17},{18,19},{2... | collective-permute-start | bytes 1179656 | tf_op jit(solution)/shard_map/ppermute | solution.py:47
  30.5 7.9 %collective-permute-start.13 = (bf16[4,192,256]{2,1,0:T(8,128)(2,1)S(1)}, bf16[4,192,256]{2,1,0:T(8,128)(2,1)S(1)}, u32[]{:S(2)}, u32[]{:S(2)}) collective-permute-start(bf16[4,192,256]{2,1,0:T(8,128)(2,1)S(1)} %pack.1.own), channel_id=1, source_target_pairs={{0,16},{2,18},{4,20},{6,22},{1,17},{3,19},{5,21},{7,23},{16,0},{18... | collective-permute-start | bytes 1179656 | tf_op jit(solution)/shard_map/ppermute | solution.py:47
  32.9 10.7 %collective-permute-start.10 = (bf16[208,256]{1,0:T(8,128)(2,1)S(1)}, bf16[208,256]{1,0:T(8,128)(2,1)S(1)}, u32[]{:S(2)}, u32[]{:S(2)}) collective-permute-start(bf16[208,256]{1,0:T(8,128)(2,1)S(1)} %get-tuple-element.70), channel_id=1, source_target_pairs={{0,4},{2,6},{4,0},{6,2},{1,5},{3,7},{5,1},{7,3},{16,20},{18,22},{2... | collective-permute-start | bytes 319496 | tf_op jit(solution)/shard_map/ppermute | solution.py:47
  36.3 7.3 %collective-permute-start.11 = (bf16[208,256]{1,0:T(8,128)(2,1)S(1)}, bf16[208,256]{1,0:T(8,128)(2,1)S(1)}, u32[]{:S(2)}, u32[]{:S(2)}) collective-permute-start(bf16[208,256]{1,0:T(8,128)(2,1)S(1)} %get-tuple-element.71), channel_id=1, source_target_pairs={{0,6},{2,4},{4,2},{6,0},{1,7},{3,5},{5,3},{7,1},{16,22},{18,20},{2... | collective-permute-start | bytes 319496 | tf_op jit(solution)/shard_map/ppermute | solution.py:47
  36.9 7.0 %collective-permute-start.9 = (bf16[208,256]{1,0:T(8,128)(2,1)S(1)}, bf16[208,256]{1,0:T(8,128)(2,1)S(1)}, u32[]{:S(2)}, u32[]{:S(2)}) collective-permute-start(bf16[208,256]{1,0:T(8,128)(2,1)S(1)} %get-tuple-element.69), channel_id=1, source_target_pairs={{0,2},{2,0},{4,6},{6,4},{1,3},{3,1},{5,7},{7,5},{16,18},{18,16},{2... | collective-permute-start | bytes 319496 | tf_op jit(solution)/shard_map/ppermute | solution.py:47
  37.2 8.9 %collective-permute-start.7 = (bf16[4,192,256]{2,1,0:T(8,128)(2,1)S(1)}, bf16[4,192,256]{2,1,0:T(8,128)(2,1)S(1)}, u32[]{:S(2)}, u32[]{:S(2)}) collective-permute-start(bf16[4,192,256]{2,1,0:T(8,128)(2,1)S(1)} %collective-permute-done.6.over), channel_id=1, source_target_pairs={{0,16},{2,18},{4,20},{6,22},{1,17},{3,19},{5,21},{7,23},{16,0},{18... | collective-permute-start | bytes 1179656 | tf_op jit(solution)/shard_map/ppermute | solution.py:47
  38.4 7.7 %collective-permute-start.15 = (bf16[3,192,256]{2,1,0:T(8,128)(2,1)S(1)}, bf16[3,192,256]{2,1,0:T(8,128)(2,1)S(1)}, u32[]{:S(2)}, u32[]{:S(2)}) collective-permute-start(bf16[3,192,256]{2,1,0:T(8,128)(2,1)S(1)} %slice.17), channel_id=1, source_target_pairs={{0,8},{2,10},{4,12},{6,14},{1,9},{3,11},{5,13},{7,15},{16,24},{18,... | collective-permute-start | bytes 884744 | tf_op jit(solution)/shard_map/ppermute | solution.py:47
  44.7 1.5 %collective-permute-start.14 = (bf16[2,192,256]{2,1,0:T(8,128)(2,1)S(1)}, bf16[2,192,256]{2,1,0:T(8,128)(2,1)S(1)}, u32[]{:S(2)}, u32[]{:S(2)}) collective-permute-start(bf16[2,192,256]{2,1,0:T(8,128)(2,1)S(1)} %get-tuple-element.80), channel_id=1, source_target_pairs={{0,8},{2,10},{4,12},{6,14},{1,9},{3,11},{5,13},{7,15},{16,24},{18,... | collective-permute-start | bytes 589832 | tf_op jit(solution)/shard_map/ppermute | solution.py:47
  44.7 1.4 %collective-permute-start.16 = (f32[1,256]{1,0:T(1,128)S(1)}, f32[1,256]{1,0:T(1,128)S(1)}, u32[]{:S(2)}, u32[]{:S(2)}) collective-permute-start(f32[1,256]{1,0:T(1,128)S(1)} %get-tuple-element.81), channel_id=1, source_target_pairs={{0,8},{2,10},{4,12},{6,14},{1,9},{3,11},{5,13},{7,15},{16,24},{18,... | collective-permute-start | bytes 3080 | tf_op jit(solution)/shard_map/ppermute | solution.py:47
  46.1 2.4 %collective-permute-start.20 = (bf16[4,192,256]{2,1,0:T(8,128)(2,1)S(1)}, bf16[4,192,256]{2,1,0:T(8,128)(2,1)S(1)}, u32[]{:S(2)}, u32[]{:S(2)}) collective-permute-start(bf16[4,192,256]{2,1,0:T(8,128)(2,1)S(1)} %collective-permute-done.7.over_got), channel_id=1, source_target_pairs={{0,8},{2,10},{4,12},{6,14},{1,9},{3,11},{5,13},{7,15},{16,24},{18,... | collective-permute-start | bytes 1179656 | tf_op jit(solution)/shard_map/ppermute | solution.py:47
  46.4 2.2 %collective-permute-start.18 = (bf16[2,192,256]{2,1,0:T(8,128)(2,1)S(1)}, bf16[2,192,256]{2,1,0:T(8,128)(2,1)S(1)}, u32[]{:S(2)}, u32[]{:S(2)}) collective-permute-start(bf16[2,192,256]{2,1,0:T(8,128)(2,1)S(1)} %get-tuple-element.93), channel_id=1, source_target_pairs={{0,8},{2,10},{4,12},{6,14},{1,9},{3,11},{5,13},{7,15},{16,24},{18,... | collective-permute-start | bytes 589832 | tf_op jit(solution)/shard_map/ppermute | solution.py:47
  46.7 1.9 %collective-permute-start.19 = (bf16[1,192,256]{2,1,0:T(8,128)(2,1)S(1)}, bf16[1,192,256]{2,1,0:T(8,128)(2,1)S(1)}, u32[]{:S(2)}, u32[]{:S(2)}) collective-permute-start(bf16[1,192,256]{2,1,0:T(8,128)(2,1)S(1)} %slice.19), channel_id=1, source_target_pairs={{0,8},{2,10},{4,12},{6,14},{1,9},{3,11},{5,13},{7,15},{16,24},{18,... | collective-permute-start | bytes 294920 | tf_op jit(solution)/shard_map/ppermute | solution.py:47
  47.0 5.7 %collective-permute-start.17 = (f32[1,256]{1,0:T(1,128)S(1)}, f32[1,256]{1,0:T(1,128)S(1)}, u32[]{:S(2)}, u32[]{:S(2)}) collective-permute-start(f32[1,256]{1,0:T(1,128)S(1)} %add.17), channel_id=1, source_target_pairs={{0,16},{2,18},{4,20},{6,22},{1,17},{3,19},{5,21},{7,23},{16,0},{18... | collective-permute-start | bytes 3080 | tf_op jit(solution)/shard_map/ppermute | solution.py:47

commit v8 on v7

--- a/solution.py
+++ b/solution.py
@@ -269,7 +269,7 @@
 
 def grad_kernel(
     plan, where, acts, gain_ref, grads, inverse, partial, late_grads,
-    own, over, own_got, over_got, peer_own, peer_first, peer_over, peer_own_first, peer_own_rest, peer_over_got,
+    own, over, own_got, over_got, peer_own, peer_first, peer_over, peer_own_first, peer_over_got,
     out_ref, weight, grad_scaled, mean_ref, out, ends,
 ):
     core = where[0]
@@ -279,7 +279,7 @@
     place_weight(plan, where, [own, over], core, False, weight)
     place_weight(plan, where, [peer_own, peer_first, peer_over], 1 - core, False, weight)
     place_weight(plan, where, [own_got, over_got], core, True, weight)
-    place_weight(plan, where, [peer_own_first, peer_own_rest, peer_over_got], 1 - core, True, weight)
+    place_weight(plan, where, [peer_own_first, peer_over_got], 1 - core, True, weight)
     blocks = [(flip, step) for flip in range(2) for step in range(depth)]
 
     def multiply(number):
@@ -512,18 +512,17 @@
     rest, gains = lax.optimization_barrier((over[2 * EARLY :], gains))
     peer_over = plan.send(rest, to_core)
     gains = gains + plan.send(gains, to_core)
-    peer_own_first = plan.send(own_got[: depth - 1], to_core)
+    peer_own_first = plan.send(own_got, to_core)
     over_got, peer_over, peer_own_first, gains = lax.optimization_barrier(
         (over_got, peer_over, peer_own_first, gains)
     )
     peer_over_got = plan.send(over_got, to_core)
-    peer_own_rest = plan.send(own_got[depth - 1 :], to_core)
     peer_gains = plan.send(gains, to_y)
 
     input_grads = pl.pallas_call(
         functools.partial(grad_kernel, plan),
         out_shape=shape((tokens, model), BF16),
-        in_specs=[SMEM] + [VMEM] * 16,
+        in_specs=[SMEM] + [VMEM] * 15,
         out_specs=HBM,
         scratch_shapes=[
             pltpu.VMEM((2 * depth, key_width, cols), BF16),
@@ -537,7 +536,7 @@
         name="grad",
     )(
         where, acts, gain, grads, inverse, partial, late_grads,
-        own, over, own_got, over_got, peer_own, peer_first, peer_over, peer_own_first, peer_own_rest, peer_over_got,
+        own, over, own_got, over_got, peer_own, peer_first, peer_over, peer_own_first, peer_over_got,
     )
     peer_gains, input_grads = lax.optimization_barrier((peer_gains, input_grads))
     return input_grads, weight_grads.T, (gains + peer_gains).reshape(cols) / plan.groups

time: 53.4 us -> 53.1 us (level)
    ppermute x21 -> x20, starting transfers between devices: 20.7 us -> 20.4 us  [send(): return lax.ppermute(array, AXES, self.pairs(move))]
    ppermute x21 -> x20, waiting for transfers between devices: 13.8 us -> 13.9 us  [send(): return lax.ppermute(array, AXES, self.pairs(move))]
  transfers between devices with their start and end apart: 21 -> 20, of which waited for: 10 -> 10; matrix products, arithmetic and copies ran while one was open for 0% -> 0% of each run, Pallas kernels for 28% -> 28%
where the time goes in v8:
time: 53.1 us; the launch traced here: 52.9 us
  starting transfers between devices  20.4 us (38%)
  Pallas kernels  17.2 us (32%)
  waiting for transfers between devices  13.9 us (26%)
  between operations  0.75 us (1%)
  other arithmetic  0.65 us (1%)
    ppermute x20, starting transfers between devices, send(): return lax.ppermute(array, AXES, self.pairs(move))  20.4 us
    ppermute x20, waiting for transfers between devices, send(): return lax.ppermute(array, AXES, self.pairs(move))  13.9 us
    pallas_call x1, Pallas kernels, by_permutes(): pl.pallas_call(functools.partial(grad_kernel, plan), out_shape=shape((tok...  4.05 us
    pallas_call x1, Pallas kernels, by_permutes(): pl.pallas_call(functools.partial(mine_kernel, plan), out_shape=(pltpu.VME...  3.19 us
    pallas_call x1, Pallas kernels, by_permutes(): pl.pallas_call(functools.partial(load_kernel, plan), out_shape=(pltpu.VME...  2.57 us
    pallas_call x1, Pallas kernels, by_permutes(): pl.pallas_call(functools.partial(term_kernel, plan), out_shape=(pltpu.VME...  2.5 us
    pallas_call x1, Pallas kernels, by_permutes(): pl.pallas_call(functools.partial(early_kernel, plan), out_shape=(pltpu.VM...  1.8 us
  transfers between devices with their start and end apart: 20, of which 10 were waited for; matrix products, arithmetic and copies ran while one was open for 0% of the time, Pallas kernels for 28%

profile of v8, /device:TPU:0, one launch (start us, length us, event | category | flops | bytes accessed | tf_op | source)
XLA Modules:
  0.0 52.9 jit_solution(12759780874428307443)
XLA Ops:
  0.6 0.5 collective-permute-start
  1.1 0.1 pad_add_fusion.where
  1.2 3.2 %mine.1 = (bf16[512,2048]{1,0:T(8,128)(2,1)S(1)}, bf16[384,512]{1,0:T(8,128)(2,1)S(1)}, bf16[384,512]{1,0:T(8,128)(2,1)S(1)}, bf16[192,256]{1,0:T(8,128)(2,1)S(1)}, f32[1,2048]{1,0:T(1,128)S(1)}) custom-call(s32[4]{0:T(128)S(1)} %pad_add_fusion.where, bf16[512,2048]{1,0:T(8,128)(2,1)} %acts_ref.3, f32[1,2048]{1,0:T(1,128)} %bitcast.7, ...), custom_call_target="tpu_custom_call" | custom-call | tf_op jit(solution)/shard_map/mine/pallas_call | solution.py:384
  4.4 0.2 collective-permute-start.1
  4.6 0.5 collective-permute-done.acts
  5.1 0.9 %peer.1.peer_scaled = bf16[512,2048]{1,0:T(8,128)(2,1)S(1)} custom-call(bf16[512,2048]{1,0:T(8,128)(2,1)S(1)} %collective-permute-done.acts, f32[1,2048]{1,0:T(1,128)S(1)} %get-tuple-element.50.gain), custom_call_target="tpu_custom_call" | custom-call | tf_op jit(solution)/shard_map/peer/pallas_call | solution.py:407
  6.0 0.2 collective-permute-done.1.theirs
  6.2 2.5 %term.1 = (bf16[8,192,256]{2,1,0:T(8,128)(2,1)S(1)}, f32[4,192,256]{2,1,0:T(8,128)S(1)}, f32[4,192,256]{2,1,0:T(8,128)S(1)}) custom-call(s32[4]{0:T(128)S(1)} %pad_add_fusion.where, bf16[512,2048]{1,0:T(8,128)(2,1)S(1)} %get-tuple-element.49.scaled, bf16[512,2048]{1,0:T(8,128)(2,1)S(1)} %peer.1.peer_scaled, bf16[384,512]{1,0:T(8,128)(2,1)S(1)} %get-tuple-element.51.mine, ...), custom_call_target="tpu_custom_call" | custom-call | tf_op jit(solution)/shard_map/term/pallas_call | solution.py:417
  8.7 2.8 %collective-permute-start.2 = (bf16[8,192,256]{2,1,0:T(8,128)(2,1)S(1)}, bf16[8,192,256]{2,1,0:T(8,128)(2,1)S(1)}, u32[]{:S(2)}, u32[]{:S(2)}) collective-permute-start(bf16[8,192,256]{2,1,0:T(8,128)(2,1)S(1)} %get-tuple-element.55), channel_id=1, source_target_pairs={{0,16},{2,18},{4,20},{6,22},{1,17},{3,19},{5,21},{7,23},{16,0},{18... | collective-permute-start | bytes 2359304 | tf_op jit(solution)/shard_map/ppermute | solution.py:47
  11.5 2.6 %collective-permute-start.3 = (bf16[192,256]{1,0:T(8,128)(2,1)S(1)}, bf16[192,256]{1,0:T(8,128)(2,1)S(1)}, u32[]{:S(2)}, u32[]{:S(2)}) collective-permute-start(bf16[192,256]{1,0:T(8,128)(2,1)S(1)} %get-tuple-element.48.refs_0_), channel_id=1, source_target_pairs={{0,4},{2,6},{4,0},{6,2},{1,5},{3,7},{5,1},{7,3},{16,20},{18,22},{2... | collective-permute-start | bytes 294920 | tf_op jit(solution)/shard_map/ppermute | solution.py:47
  14.1 1.6 %collective-permute-start.4 = (bf16[192,256]{1,0:T(8,128)(2,1)S(1)}, bf16[192,256]{1,0:T(8,128)(2,1)S(1)}, u32[]{:S(2)}, u32[]{:S(2)}) collective-permute-start(bf16[192,256]{1,0:T(8,128)(2,1)S(1)} %get-tuple-element.48.refs_0_), channel_id=1, source_target_pairs={{0,2},{2,0},{4,6},{6,4},{1,3},{3,1},{5,7},{7,5},{16,18},{18,16},{2... | collective-permute-start | bytes 294920 | tf_op jit(solution)/shard_map/ppermute | solution.py:47
  15.7 0.2 collective-permute-start.5
  15.9 2.6 %load.1 = (bf16[2,4,512,256]{3,2,1,0:T(8,128)(2,1)S(1)}, bf16[512,768]{1,0:T(8,128)(2,1)S(1)}, f32[512,128]{1,0:T(8,128)S(1)}) custom-call(s32[4]{0:T(128)S(1)} %pad_add_fusion.where, bf16[512,2048]{1,0:T(8,128)(2,1)} %acts_ref.3, bf16[512,768]{1,0:T(8,128)(2,1)} %grads_ref.3), custom_call_target="tpu_custom_call" | custom-call | tf_op jit(solution)/shard_map/load/pallas_call | solution.py:433
  18.5 0.0 copy-start
  18.5 2.2 %collective-permute-done.3.refs_2_ = bf16[192,256]{1,0:T(8,128)(2,1)S(1)} collective-permute-done((bf16[192,256]{1,0:T(8,128)(2,1)S(1)}, bf16[192,256]{1,0:T(8,128)(2,1)S(1)}, u32[]{:S(2)}, u32[]{:S(2)}) %collective-permute-start.3) | collective-permute-done | bytes 98336 | tf_op jit(solution)/shard_map/ppermute | solution.py:47
  20.7 0.8 %collective-permute-done.2.got_ref = bf16[8,192,256]{2,1,0:T(8,128)(2,1)S(1)} collective-permute-done((bf16[8,192,256]{2,1,0:T(8,128)(2,1)S(1)}, bf16[8,192,256]{2,1,0:T(8,128)(2,1)S(1)}, u32[]{:S(2)}, u32[]{:S(2)}) %collective-permute-start.2) | collective-permute-done | bytes 786464 | tf_op jit(solution)/shard_map/ppermute | solution.py:47
  21.5 0.6 %half.1 = bf16[4,192,256]{2,1,0:T(8,128)(2,1)S(1)} custom-call(s32[4]{0:T(128)S(1)} %pad_add_fusion.where, f32[4,192,256]{2,1,0:T(8,128)S(1)} %get-tuple-element.54.kept, bf16[8,192,256]{2,1,0:T(8,128)(2,1)S(1)} %collective-permute-done.2.got_ref), custom_call_target="tpu_custom_call" | custom-call | tf_op jit(solution)/shard_map/half/pallas_call | solution.py:453
  22.1 0.0 collective-permute-done.4.refs_1_
  22.1 0.4 collective-permute-done.5.refs_3_
  22.6 0.1 collective-permute-start.12
  22.7 1.7 %collective-permute-start.8 = (bf16[4,192,256]{2,1,0:T(8,128)(2,1)S(1)}, bf16[4,192,256]{2,1,0:T(8,128)(2,1)S(1)}, u32[]{:S(2)}, u32[]{:S(2)}) collective-permute-start(bf16[4,192,256]{2,1,0:T(8,128)(2,1)S(1)} %half.1), channel_id=1, source_target_pairs={{0,1},{2,3},{4,5},{6,7},{1,0},{3,2},{5,4},{7,6},{16,17},{18,19},{2... | collective-permute-start | bytes 1179656 | tf_op jit(solution)/shard_map/ppermute | solution.py:47
  24.3 0.4 collective-permute-start.6
  24.8 5.7 %collective-permute-done.8.again_ref = bf16[4,192,256]{2,1,0:T(8,128)(2,1)S(1)} collective-permute-done((bf16[4,192,256]{2,1,0:T(8,128)(2,1)S(1)}, bf16[4,192,256]{2,1,0:T(8,128)(2,1)S(1)}, u32[]{:S(2)}, u32[]{:S(2)}) %collective-permute-start.8) | collective-permute-done | bytes 393248 | tf_op jit(solution)/shard_map/ppermute | solution.py:47
  30.5 1.6 %collective-permute-start.13 = (bf16[4,192,256]{2,1,0:T(8,128)(2,1)S(1)}, bf16[4,192,256]{2,1,0:T(8,128)(2,1)S(1)}, u32[]{:S(2)}, u32[]{:S(2)}) collective-permute-start(bf16[4,192,256]{2,1,0:T(8,128)(2,1)S(1)} %pack.1.own), channel_id=1, source_target_pairs={{0,16},{2,18},{4,20},{6,22},{1,17},{3,19},{5,21},{7,23},{16,0},{18... | collective-permute-start | bytes 1179656 | tf_op jit(solution)/shard_map/ppermute | solution.py:47
  32.1 0.8 %plane.1 = (f32[192,256]{1,0:T(8,128)S(1)}, f32[1,256]{1,0:T(1,128)S(1)}, bf16[208,256]{1,0:T(8,128)(2,1)S(1)}, bf16[208,256]{1,0:T(8,128)(2,1)S(1)}, bf16[208,256]{1,0:T(8,128)(2,1)S(1)}) custom-call(s32[4]{0:T(128)S(1)} %pad_add_fusion.where, f32[4,192,256]{2,1,0:T(8,128)S(1)} %get-tuple-element.66.held, ...), custom_call_target="tpu_custom_call" | custom-call | tf_op jit(solution)/shard_map/plane/pallas_call | solution.py:476
  32.9 3.4 %collective-permute-start.10 = (bf16[208,256]{1,0:T(8,128)(2,1)S(1)}, bf16[208,256]{1,0:T(8,128)(2,1)S(1)}, u32[]{:S(2)}, u32[]{:S(2)}) collective-permute-start(bf16[208,256]{1,0:T(8,128)(2,1)S(1)} %get-tuple-element.70), channel_id=1, source_target_pairs={{0,4},{2,6},{4,0},{6,2},{1,5},{3,7},{5,1},{7,3},{16,20},{18,22},{2... | collective-permute-start | bytes 319496 | tf_op jit(solution)/shard_map/ppermute | solution.py:47
  36.3 0.6 %collective-permute-start.11 = (bf16[208,256]{1,0:T(8,128)(2,1)S(1)}, bf16[208,256]{1,0:T(8,128)(2,1)S(1)}, u32[]{:S(2)}, u32[]{:S(2)}) collective-permute-start(bf16[208,256]{1,0:T(8,128)(2,1)S(1)} %get-tuple-element.71), channel_id=1, source_target_pairs={{0,6},{2,4},{4,2},{6,0},{1,7},{3,5},{5,3},{7,1},{16,22},{18,20},{2... | collective-permute-start | bytes 319496 | tf_op jit(solution)/shard_map/ppermute | solution.py:47
  36.9 0.2 collective-permute-start.9
  37.2 0.0 collective-permute-done.6.over
  37.2 1.2 %collective-permute-start.7 = (bf16[4,192,256]{2,1,0:T(8,128)(2,1)S(1)}, bf16[4,192,256]{2,1,0:T(8,128)(2,1)S(1)}, u32[]{:S(2)}, u32[]{:S(2)}) collective-permute-start(bf16[4,192,256]{2,1,0:T(8,128)(2,1)S(1)} %collective-permute-done.6.over), channel_id=1, source_target_pairs={{0,16},{2,18},{4,20},{6,22},{1,17},{3,19},{5,21},{7,23},{16,0},{18... | collective-permute-start | bytes 1179656 | tf_op jit(solution)/shard_map/ppermute | solution.py:47
  38.3 0.1 collective-permute-done.13.own_got
  38.4 0.7 %collective-permute-start.15 = (bf16[4,192,256]{2,1,0:T(8,128)(2,1)S(1)}, bf16[4,192,256]{2,1,0:T(8,128)(2,1)S(1)}, u32[]{:S(2)}, u32[]{:S(2)}) collective-permute-start(bf16[4,192,256]{2,1,0:T(8,128)(2,1)S(1)} %collective-permute-done.13.own_got), channel_id=1, source_target_pairs={{0,8},{2,10},{4,12},{6,14},{1,9},{3,11},{5,13},{7,15},{16,24},{18,... | collective-permute-start | bytes 1179656 | tf_op jit(solution)/shard_map/ppermute | solution.py:47
  39.1 1.8 %early.1 = (f32[4,512,256]{2,1,0:T(8,128)S(1)}, bf16[512,192]{1,0:T(8,128)(2,1)S(1)}) custom-call(s32[4]{0:T(128)S(1)} %pad_add_fusion.where, bf16[512,768]{1,0:T(8,128)(2,1)S(1)} %get-tuple-element.72.grads, bf16[4,192,256]{2,1,0:T(8,128)(2,1)S(1)} %pack.1.own, bf16[4,192,256]{2,1,0:T(8,128)(2,1)S(1)} %collective-permute-done.6.over, ...), custom_call_target="tpu_custom_call" | custom-call | tf_op jit(solution)/shard_map/early/pallas_call | solution.py:491
  40.9 2.7 %collective-permute-done.10.refs_1_ = bf16[208,256]{1,0:T(8,128)(2,1)S(1)} collective-permute-done((bf16[208,256]{1,0:T(8,128)(2,1)S(1)}, bf16[208,256]{1,0:T(8,128)(2,1)S(1)}, u32[]{:S(2)}, u32[]{:S(2)}) %collective-permute-start.10) | collective-permute-done | bytes 106528 | tf_op jit(solution)/shard_map/ppermute | solution.py:47
  43.6 0.0 collective-permute-done.11.refs_2_
  43.6 0.3 collective-permute-done.9.refs_0_
  43.9 0.7 %last.1 = (f32[192,256]{1,0:T(8,128)}, f32[1,256]{1,0:T(1,128)S(1)}) custom-call(f32[192,256]{1,0:T(8,128)S(1)} %get-tuple-element.67.sums_ref, f32[1,256]{1,0:T(1,128)S(1)} %get-tuple-element.68.gains_ref, bf16[208,256]{1,0:T(8,128)(2,1)S(1)} %collective-permute-done.9.refs_0_, bf16[208,256]{1,0:T(8,128)(2,1)S(1)} %collective-permute-done.10.refs_1_, ...), custom_call_target="tpu_custom_call" | custom-call | tf_op jit(solution)/shard_map/last/pallas_call | solution.py:502
  44.7 0.0 collective-permute-start.14
  44.7 0.5 collective-permute-start.16
  45.2 0.9 %collective-permute-done.16 = f32[1,256]{1,0:T(1,128)S(1)} collective-permute-done((f32[1,256]{1,0:T(1,128)S(1)}, f32[1,256]{1,0:T(1,128)S(1)}, u32[]{:S(2)}, u32[]{:S(2)}) %collective-permute-start.16) | collective-permute-done | bytes 1056 | tf_op jit(solution)/shard_map/ppermute | solution.py:47
  46.1 0.0 collective-permute-done.7.over_got
  46.1 0.0 collective-permute-done.14.peer_over
  46.1 0.3 collective-permute-start.19
  46.4 0.3 collective-permute-start.18
  46.7 1.6 %collective-permute-start.17 = (f32[1,256]{1,0:T(1,128)S(1)}, f32[1,256]{1,0:T(1,128)S(1)}, u32[]{:S(2)}, u32[]{:S(2)}) collective-permute-start(f32[1,256]{1,0:T(1,128)S(1)} %add.17), channel_id=1, source_target_pairs={{0,16},{2,18},{4,20},{6,22},{1,17},{3,19},{5,21},{7,23},{16,0},{18... | collective-permute-start | bytes 3080 | tf_op jit(solution)/shard_map/ppermute | solution.py:47
  48.3 0.0 collective-permute-done.19.peer_over_got
  48.3 4.0 %grad.1 = bf16[512,2048]{1,0:T(8,128)(2,1)} custom-call(s32[4]{0:T(128)S(1)} %pad_add_fusion.where, bf16[2,4,512,256]{3,2,1,0:T(8,128)(2,1)S(1)} %get-tuple-element.83.acts, f32[1,2048]{1,0:T(1,128)S(1)} %bitcast.9, bf16[512,768]{1,0:T(8,128)(2,1)S(1)} %get-tuple-element.72.grads, f32[512,128]{1,0:T(8,128)S(1)} %get-tuple-element.84.inverse, ...), custom_call_target="tpu_custom_call" | custom-call | tf_op jit(solution)/shard_map/grad/pallas_call | solution.py:522
  52.3 0.6 %add_multiply_fusion = f32[1,256]{1,0:T(1,128)} fusion(f32[1,256]{1,0:T(1,128)S(1)} %add.17, f32[1,256]{1,0:T(1,128)S(1)} %collective-permute-done.17), kind=kLoop, calls=%fused_computation | loop fusion | flops 512 | bytes 3072 | tf_op jit(solution)/shard_map/div | solution.py:542
  (8 shorter events, 0.1 us)
Async XLA Ops:
  0.6 4.5 %collective-permute-start = (bf16[512,2048]{1,0:T(8,128)(2,1)}, bf16[512,2048]{1,0:T(8,128)(2,1)S(1)}, u32[]{:S(2)}, u32[]{:S(2)}) collective-permute-start(bf16[512,2048]{1,0:T(8,128)(2,1)} %acts_ref.3), channel_id=1, source_target_pairs={{0,8},{2,10},{4,12},{6,14},{1,9},{3,11},{5,13},{7,15},{16,24},{18,... | collective-permute-start | bytes 6291464 | tf_op jit(solution)/shard_map/ppermute | solution.py:47
  4.4 1.8 %collective-permute-start.1 = (bf16[384,512]{1,0:T(8,128)(2,1)S(1)}, bf16[384,512]{1,0:T(8,128)(2,1)S(1)}, u32[]{:S(2)}, u32[]{:S(2)}) collective-permute-start(bf16[384,512]{1,0:T(8,128)(2,1)S(1)} %get-tuple-element.52), channel_id=1, source_target_pairs={{0,8},{2,10},{4,12},{6,14},{1,9},{3,11},{5,13},{7,15},{16,24},{18,... | collective-permute-start | bytes 1179656 | tf_op jit(solution)/shard_map/ppermute | solution.py:47
  8.7 12.8 %collective-permute-start.2 = (bf16[8,192,256]{2,1,0:T(8,128)(2,1)S(1)}, bf16[8,192,256]{2,1,0:T(8,128)(2,1)S(1)}, u32[]{:S(2)}, u32[]{:S(2)}) collective-permute-start(bf16[8,192,256]{2,1,0:T(8,128)(2,1)S(1)} %get-tuple-element.55), channel_id=1, source_target_pairs={{0,16},{2,18},{4,20},{6,22},{1,17},{3,19},{5,21},{7,23},{16,0},{18... | collective-permute-start | bytes 2359304 | tf_op jit(solution)/shard_map/ppermute | solution.py:47
  11.5 9.2 %collective-permute-start.3 = (bf16[192,256]{1,0:T(8,128)(2,1)S(1)}, bf16[192,256]{1,0:T(8,128)(2,1)S(1)}, u32[]{:S(2)}, u32[]{:S(2)}) collective-permute-start(bf16[192,256]{1,0:T(8,128)(2,1)S(1)} %get-tuple-element.48.refs_0_), channel_id=1, source_target_pairs={{0,4},{2,6},{4,0},{6,2},{1,5},{3,7},{5,1},{7,3},{16,20},{18,22},{2... | collective-permute-start | bytes 294920 | tf_op jit(solution)/shard_map/ppermute | solution.py:47
  14.1 8.0 %collective-permute-start.4 = (bf16[192,256]{1,0:T(8,128)(2,1)S(1)}, bf16[192,256]{1,0:T(8,128)(2,1)S(1)}, u32[]{:S(2)}, u32[]{:S(2)}) collective-permute-start(bf16[192,256]{1,0:T(8,128)(2,1)S(1)} %get-tuple-element.48.refs_0_), channel_id=1, source_target_pairs={{0,2},{2,0},{4,6},{6,4},{1,3},{3,1},{5,7},{7,5},{16,18},{18,16},{2... | collective-permute-start | bytes 294920 | tf_op jit(solution)/shard_map/ppermute | solution.py:47
  15.7 6.9 %collective-permute-start.5 = (bf16[192,256]{1,0:T(8,128)(2,1)S(1)}, bf16[192,256]{1,0:T(8,128)(2,1)S(1)}, u32[]{:S(2)}, u32[]{:S(2)}) collective-permute-start(bf16[192,256]{1,0:T(8,128)(2,1)S(1)} %get-tuple-element.48.refs_0_), channel_id=1, source_target_pairs={{0,6},{2,4},{4,2},{6,0},{1,7},{3,5},{5,3},{7,1},{16,22},{18,20},{2... | collective-permute-start | bytes 294920 | tf_op jit(solution)/shard_map/ppermute | solution.py:47
  18.5 13.6 %copy-start = (f32[2048]{0:T(1024)S(1)}, f32[2048]{0:T(1024)}, u32[]{:S(2)}) copy-start(f32[2048]{0:T(1024)} %param.5) | copy-start | bytes 24580
  22.6 2.2 %collective-permute-start.12 = (bf16[4,192,256]{2,1,0:T(8,128)(2,1)S(1)}, bf16[4,192,256]{2,1,0:T(8,128)(2,1)S(1)}, u32[]{:S(2)}, u32[]{:S(2)}) collective-permute-start(bf16[4,192,256]{2,1,0:T(8,128)(2,1)S(1)} %pack.1.own), channel_id=1, source_target_pairs={{0,8},{2,10},{4,12},{6,14},{1,9},{3,11},{5,13},{7,15},{16,24},{18,... | collective-permute-start | bytes 1179656 | tf_op jit(solution)/shard_map/ppermute | solution.py:47
  22.7 7.8 %collective-permute-start.8 = (bf16[4,192,256]{2,1,0:T(8,128)(2,1)S(1)}, bf16[4,192,256]{2,1,0:T(8,128)(2,1)S(1)}, u32[]{:S(2)}, u32[]{:S(2)}) collective-permute-start(bf16[4,192,256]{2,1,0:T(8,128)(2,1)S(1)} %half.1), channel_id=1, source_target_pairs={{0,1},{2,3},{4,5},{6,7},{1,0},{3,2},{5,4},{7,6},{16,17},{18,19},{2... | collective-permute-start | bytes 1179656 | tf_op jit(solution)/shard_map/ppermute | solution.py:47
  24.3 12.8 %collective-permute-start.6 = (bf16[4,192,256]{2,1,0:T(8,128)(2,1)S(1)}, bf16[4,192,256]{2,1,0:T(8,128)(2,1)S(1)}, u32[]{:S(2)}, u32[]{:S(2)}) collective-permute-start(bf16[4,192,256]{2,1,0:T(8,128)(2,1)S(1)} %pack.1.own), channel_id=1, source_target_pairs={{0,1},{2,3},{4,5},{6,7},{1,0},{3,2},{5,4},{7,6},{16,17},{18,19},{2... | collective-permute-start | bytes 1179656 | tf_op jit(solution)/shard_map/ppermute | solution.py:47
  30.5 7.9 %collective-permute-start.13 = (bf16[4,192,256]{2,1,0:T(8,128)(2,1)S(1)}, bf16[4,192,256]{2,1,0:T(8,128)(2,1)S(1)}, u32[]{:S(2)}, u32[]{:S(2)}) collective-permute-start(bf16[4,192,256]{2,1,0:T(8,128)(2,1)S(1)} %pack.1.own), channel_id=1, source_target_pairs={{0,16},{2,18},{4,20},{6,22},{1,17},{3,19},{5,21},{7,23},{16,0},{18... | collective-permute-start | bytes 1179656 | tf_op jit(solution)/shard_map/ppermute | solution.py:47
  32.9 10.7 %collective-permute-start.10 = (bf16[208,256]{1,0:T(8,128)(2,1)S(1)}, bf16[208,256]{1,0:T(8,128)(2,1)S(1)}, u32[]{:S(2)}, u32[]{:S(2)}) collective-permute-start(bf16[208,256]{1,0:T(8,128)(2,1)S(1)} %get-tuple-element.70), channel_id=1, source_target_pairs={{0,4},{2,6},{4,0},{6,2},{1,5},{3,7},{5,1},{7,3},{16,20},{18,22},{2... | collective-permute-start | bytes 319496 | tf_op jit(solution)/shard_map/ppermute | solution.py:47
  36.3 7.3 %collective-permute-start.11 = (bf16[208,256]{1,0:T(8,128)(2,1)S(1)}, bf16[208,256]{1,0:T(8,128)(2,1)S(1)}, u32[]{:S(2)}, u32[]{:S(2)}) collective-permute-start(bf16[208,256]{1,0:T(8,128)(2,1)S(1)} %get-tuple-element.71), channel_id=1, source_target_pairs={{0,6},{2,4},{4,2},{6,0},{1,7},{3,5},{5,3},{7,1},{16,22},{18,20},{2... | collective-permute-start | bytes 319496 | tf_op jit(solution)/shard_map/ppermute | solution.py:47
  36.9 7.0 %collective-permute-start.9 = (bf16[208,256]{1,0:T(8,128)(2,1)S(1)}, bf16[208,256]{1,0:T(8,128)(2,1)S(1)}, u32[]{:S(2)}, u32[]{:S(2)}) collective-permute-start(bf16[208,256]{1,0:T(8,128)(2,1)S(1)} %get-tuple-element.69), channel_id=1, source_target_pairs={{0,2},{2,0},{4,6},{6,4},{1,3},{3,1},{5,7},{7,5},{16,18},{18,16},{2... | collective-permute-start | bytes 319496 | tf_op jit(solution)/shard_map/ppermute | solution.py:47
  37.2 8.9 %collective-permute-start.7 = (bf16[4,192,256]{2,1,0:T(8,128)(2,1)S(1)}, bf16[4,192,256]{2,1,0:T(8,128)(2,1)S(1)}, u32[]{:S(2)}, u32[]{:S(2)}) collective-permute-start(bf16[4,192,256]{2,1,0:T(8,128)(2,1)S(1)} %collective-permute-done.6.over), channel_id=1, source_target_pairs={{0,16},{2,18},{4,20},{6,22},{1,17},{3,19},{5,21},{7,23},{16,0},{18... | collective-permute-start | bytes 1179656 | tf_op jit(solution)/shard_map/ppermute | solution.py:47
  38.4 7.7 %collective-permute-start.15 = (bf16[4,192,256]{2,1,0:T(8,128)(2,1)S(1)}, bf16[4,192,256]{2,1,0:T(8,128)(2,1)S(1)}, u32[]{:S(2)}, u32[]{:S(2)}) collective-permute-start(bf16[4,192,256]{2,1,0:T(8,128)(2,1)S(1)} %collective-permute-done.13.own_got), channel_id=1, source_target_pairs={{0,8},{2,10},{4,12},{6,14},{1,9},{3,11},{5,13},{7,15},{16,24},{18,... | collective-permute-start | bytes 1179656 | tf_op jit(solution)/shard_map/ppermute | solution.py:47
  44.7 1.5 %collective-permute-start.14 = (bf16[2,192,256]{2,1,0:T(8,128)(2,1)S(1)}, bf16[2,192,256]{2,1,0:T(8,128)(2,1)S(1)}, u32[]{:S(2)}, u32[]{:S(2)}) collective-permute-start(bf16[2,192,256]{2,1,0:T(8,128)(2,1)S(1)} %get-tuple-element.80), channel_id=1, source_target_pairs={{0,8},{2,10},{4,12},{6,14},{1,9},{3,11},{5,13},{7,15},{16,24},{18,... | collective-permute-start | bytes 589832 | tf_op jit(solution)/shard_map/ppermute | solution.py:47
  44.7 1.4 %collective-permute-start.16 = (f32[1,256]{1,0:T(1,128)S(1)}, f32[1,256]{1,0:T(1,128)S(1)}, u32[]{:S(2)}, u32[]{:S(2)}) collective-permute-start(f32[1,256]{1,0:T(1,128)S(1)} %get-tuple-element.81), channel_id=1, source_target_pairs={{0,8},{2,10},{4,12},{6,14},{1,9},{3,11},{5,13},{7,15},{16,24},{18,... | collective-permute-start | bytes 3080 | tf_op jit(solution)/shard_map/ppermute | solution.py:47
  46.1 2.2 %collective-permute-start.19 = (bf16[4,192,256]{2,1,0:T(8,128)(2,1)S(1)}, bf16[4,192,256]{2,1,0:T(8,128)(2,1)S(1)}, u32[]{:S(2)}, u32[]{:S(2)}) collective-permute-start(bf16[4,192,256]{2,1,0:T(8,128)(2,1)S(1)} %collective-permute-done.7.over_got), channel_id=1, source_target_pairs={{0,8},{2,10},{4,12},{6,14},{1,9},{3,11},{5,13},{7,15},{16,24},{18,... | collective-permute-start | bytes 1179656 | tf_op jit(solution)/shard_map/ppermute | solution.py:47
  46.4 1.9 %collective-permute-start.18 = (bf16[2,192,256]{2,1,0:T(8,128)(2,1)S(1)}, bf16[2,192,256]{2,1,0:T(8,128)(2,1)S(1)}, u32[]{:S(2)}, u32[]{:S(2)}) collective-permute-start(bf16[2,192,256]{2,1,0:T(8,128)(2,1)S(1)} %get-tuple-element.93), channel_id=1, source_target_pairs={{0,8},{2,10},{4,12},{6,14},{1,9},{3,11},{5,13},{7,15},{16,24},{18,... | collective-permute-start | bytes 589832 | tf_op jit(solution)/shard_map/ppermute | solution.py:47
  46.7 5.6 %collective-permute-start.17 = (f32[1,256]{1,0:T(1,128)S(1)}, f32[1,256]{1,0:T(1,128)S(1)}, u32[]{:S(2)}, u32[]{:S(2)}) collective-permute-start(f32[1,256]{1,0:T(1,128)S(1)} %add.17), channel_id=1, source_target_pairs={{0,16},{2,18},{4,20},{6,22},{1,17},{3,19},{5,21},{7,23},{16,0},{18... | collective-permute-start | bytes 3080 | tf_op jit(solution)/shard_map/ppermute | solution.py:47
